TPU v7x, 32 devices: a whole 2x2x4 slice. The times are simulated.
32 devices in a mesh: orb: 4 (over y, x), gx: 4 (over z), gy: 2 (over core).
Axes of the slice: x: 2, y: 2, z: 4, core: 2. Of those that a mesh axis runs over, the one named last changes fastest.
Arguments:
- orbitals: float32 [16, 512, 256], P('orb', 'gx', 'gy'), may hold values from -6 to 6
- potentials: float32 [64, 512, 256], P('orb', 'gx', 'gy'), may hold values from -6 to 6
- coefficients: float32 [5, 512, 256], P(None, 'gx', 'gy'), may hold values from 0.25 to 1
- metric: float32 [512, 256], P('gx', 'gy'), may hold values from 0.5 to 4.5, as said below
- sweep_counts: int32 [64], P('orb'), may hold values from 4 to 8, as said below
Outputs:
- new_orbitals: float32 [16, 512, 256], P('orb', 'gx', 'gy')
- new_potentials: float32 [64, 512, 256], P('orb', 'gx', 'gy')
Inputs may be any that keep to these rules, and one draw needn't show every extreme that they name: `sweep_counts`: each pair gets between 4 and 8 sweeps; both ends occur. `metric`: positive volume elements.
All inputs are finite; a program needn't handle non-finite values.
Results may differ from a plain program's by a relative error of at most 0.0003.
Values sent between devices are 32-bit elements; how exact they have to be, the bound alone decides.
No kernel may reach another device: no remote copies, remote signals or barrier semaphores. Data moves between devices by JAX's collectives and lax.ppermute only.
A program may use at most 64 MiB of HBM per device.

v0:
```python
import jax
import jax.numpy as jnp
from jax import lax
from jax.sharding import PartitionSpec as P

SWEEPS = 8


relaxation = 0.8
screening = 0.02
step_size = 0.1


def shifted(value, axis, by):
    size = lax.axis_size(axis)
    return lax.ppermute(value, axis, [(i, (i + by) % size) for i in range(size)])


def with_halo(block, sides, width):
    for axis, dim in sides:
        count = lax.axis_size(axis)
        forward = [(i, i + 1) for i in range(count - 1)]
        backward = [(target, source) for source, target in forward]
        low = lax.ppermute(
            lax.slice_in_dim(block, block.shape[dim] - width, None, axis=dim), axis, forward
        )
        high = lax.ppermute(lax.slice_in_dim(block, 0, width, axis=dim), axis, backward)
        block = jnp.concatenate([low, block, high], axis=dim)
    return block


def relaxed_sweep(padded, source, coef_ext, active, inside):
    coefs = coef_ext[:, 1:-1, 1:-1]
    center = padded[:, 1:-1, 1:-1]
    neighbours = coefs[0] * padded[:, :-2, 1:-1] + coefs[1] * padded[:, 2:, 1:-1]
    neighbours = neighbours + coefs[2] * padded[:, 1:-1, 2:] + coefs[3] * padded[:, 1:-1, :-2]
    neighbours = neighbours + coefs[4] * (
        padded[:, :-2, 2:] + padded[:, 2:, :-2] - padded[:, :-2, :-2] - padded[:, 2:, 2:]
    )
    diagonal = (1.0 + screening) * (coefs[0] + coefs[1] + coefs[2] + coefs[3] + 4.0 * coefs[4])
    diagonal = jnp.where(inside, diagonal, 1.0)
    result = center + relaxation * active * ((neighbours + source) / diagonal - center)
    result = jnp.where(inside[None], result, 0.0)
    return result


def deep_sweeps(fields, source_ext, coef_ext, sweep_counts, halo_depth, row_count, col_count):
    row_pos = (
        lax.axis_index("gx") * row_count
        - halo_depth
        + jnp.arange(row_count + 2 * halo_depth, dtype=jnp.int32)
    )
    col_pos = (
        lax.axis_index("gy") * col_count
        - halo_depth
        + jnp.arange(col_count + 2 * halo_depth, dtype=jnp.int32)
    )
    row_inside = (row_pos >= 0) & (row_pos < row_count * lax.axis_size("gx"))
    col_inside = (col_pos >= 0) & (col_pos < col_count * lax.axis_size("gy"))
    inside_all = row_inside[:, None] & col_inside[None, :]
    for sweep in range(halo_depth):
        margin = halo_depth - sweep
        active = (sweep_counts > sweep).astype(jnp.float32)[:, None, None]
        coef_now = coef_ext[
            :, sweep : sweep + row_count + 2 * margin, sweep : sweep + col_count + 2 * margin
        ]
        lower = sweep + 1
        source_now = source_ext[
            :,
            lower : lower + row_count + 2 * (margin - 1),
            lower : lower + col_count + 2 * (margin - 1),
        ]
        inside_now = inside_all[
            lower : lower + row_count + 2 * (margin - 1),
            lower : lower + col_count + 2 * (margin - 1),
        ]
        fields = relaxed_sweep(fields, source_now, coef_now, active, inside_now)
    return fields


def local(orbitals, potentials, coefficients, metric, sweep_counts):
    own_count, row_count, col_count = orbitals.shape
    pair_count = potentials.shape[0]
    partner = shifted(orbitals, "orb", 1)
    halo_depth = SWEEPS
    joined = jnp.concatenate([potentials, orbitals, partner, metric[None], coefficients], 0)
    stacked = with_halo(joined, (("gx", 1), ("gy", 2)), halo_depth)
    orb_ext = stacked[pair_count : pair_count + own_count]
    partner_ext = stacked[pair_count + own_count : pair_count + 2 * own_count]
    metric_ext = stacked[pair_count + 2 * own_count]
    coef_ext = stacked[pair_count + 2 * own_count + 1 :]
    ext_rows = row_count + 2 * halo_depth
    ext_cols = col_count + 2 * halo_depth
    source_ext = metric_ext[None] * (orb_ext[:, None] * partner_ext[None]).reshape(
        pair_count, ext_rows, ext_cols
    )
    fields = deep_sweeps(
        stacked[:pair_count], source_ext, coef_ext, sweep_counts, halo_depth, row_count, col_count
    )
    grouped = fields.reshape(own_count, own_count, row_count, col_count)
    own_terms = jnp.sum(grouped * partner[None], axis=1)
    back_terms = jnp.sum(grouped * orbitals[:, None], axis=0)
    received = shifted(back_terms, "orb", -1)
    updated = orbitals - step_size * (own_terms + received)
    local_norms = jnp.sum(metric[None] * updated * updated, axis=(1, 2))
    norm_sums = lax.psum(local_norms, ("gx", "gy"))
    cell_total = row_count * col_count * lax.axis_size("gx") * lax.axis_size("gy")
    rescale = jnp.sqrt(cell_total / norm_sums)
    return (updated * rescale[:, None, None], fields)


def solution(mesh):
    return jax.shard_map(
        local,
        mesh=mesh,
        in_specs=(
            P("orb", "gx", "gy"),
            P("orb", "gx", "gy"),
            P(None, "gx", "gy"),
            P("gx", "gy"),
            P("orb"),
        ),
        out_specs=(P("orb", "gx", "gy"), P("orb", "gx", "gy")),
        check_vma=False,
    )
```

profile of v0, /device:TPU:0, one launch (start us, length us, event | category | flops | bytes accessed | tf_op | source)
XLA Modules:
  0.0 107.8 jit_solution(2451091034591852940)
XLA Ops:
  0.6 3.0 %collective-permute-start = (f32[4,128,128]{2,1,0:T(8,128)}, f32[4,128,128]{2,1,0:T(8,128)S(1)}, u32[]{:S(2)}, u32[]{:S(2)}) collective-permute-start(f32[4,128,128]{2,1,0:T(8,128)} %param.5), channel_id=1, source_target_pairs={{0,8},{8,16},{16,24},{24,0},{1,9},{9,17},{17,25},{25,1},{2,10},{10... | collective-permute-start | bytes 786440 | tf_op jit(solution)/shard_map/ppermute | solution.py:16
  3.6 1.3 %constant_dynamic-update-slice_fusion.3 = f32[30,128,128]{2,1,0:T(8,128)S(1)} fusion(f32[16,128,128]{2,1,0:T(8,128)} %param.6), kind=kLoop, calls=%fused_computation.208 | loop fusion | bytes 2097152
  5.1 0.7 slice.673
  5.9 0.7 slice.672
  6.6 0.7 slice.671
  7.3 0.7 slice.670
  8.7 0.7 slice.668
  9.4 0.7 slice.667
  11.2 3.7 %collective-permute-start.1 = (f32[30,8,128]{2,1,0:T(8,128)S(1)}, f32[30,8,128]{2,1,0:T(8,128)S(1)}, u32[]{:S(2)}, u32[]{:S(2)}) collective-permute-start(f32[30,8,128]{2,1,0:T(8,128)S(1)} %get-tuple-element.47), channel_id=1, source_target_pairs={{0,2},{2,4},{4,6},{1,3},{3,5},{5,7},{8,10},{10,12},{12,14},{9,11},... | collective-permute-start | bytes 368648 | tf_op jit(solution)/shard_map/ppermute | solution.py:24
  14.9 1.3 %collective-permute-start.2 = (f32[30,8,128]{2,1,0:T(8,128)S(1)}, f32[30,8,128]{2,1,0:T(8,128)S(1)}, u32[]{:S(2)}, u32[]{:S(2)}) collective-permute-start(f32[30,8,128]{2,1,0:T(8,128)S(1)} %get-tuple-element.48), channel_id=1, source_target_pairs={{2,0},{4,2},{6,4},{3,1},{5,3},{7,5},{10,8},{12,10},{14,12},{11,9},... | collective-permute-start | bytes 368648 | tf_op jit(solution)/shard_map/ppermute | solution.py:27
  16.2 0.7 multiply_select_fusion.7
  17.3 4.4 %collective-permute-done.2 = f32[30,8,128]{2,1,0:T(8,128)S(1)} collective-permute-done((f32[30,8,128]{2,1,0:T(8,128)S(1)}, f32[30,8,128]{2,1,0:T(8,128)S(1)}, u32[]{:S(2)}, u32[]{:S(2)}) %collective-permute-start.2) | collective-permute-done | bytes 122912 | tf_op jit(solution)/shard_map/ppermute | solution.py:27
  21.8 2.7 %fusion.82 = (f32[30,144,8]{2,1,0:T(8,128)}, f32[30,144,8]{2,1,0:T(8,128)}) fusion(f32[30,144,128]{2,1,0:T(8,128)S(1)} %pad_maximum_fusion.1), kind=kLoop, calls=%fused_computation.221 | loop fusion | bytes 552960 | tf_op jit(solution)/shard_map/slice | solution.py:25
  24.6 2.7 %copy.19 = f32[30,144,8]{1,2,0:T(8,128)S(1)} copy(f32[30,144,8]{2,1,0:T(8,128)} %get-tuple-element.45) | data formatting | bytes 276480 | tf_op jit(solution)/shard_map/slice | solution.py:25
  27.3 2.0 %collective-permute-start.3 = (f32[30,144,8]{1,2,0:T(8,128)S(1)}, f32[30,144,8]{1,2,0:T(8,128)}, u32[]{:S(2)}, u32[]{:S(2)}) collective-permute-start(f32[30,144,8]{1,2,0:T(8,128)S(1)} %copy.19), channel_id=1, source_target_pairs={{0,1},{2,3},{4,5},{6,7},{8,9},{10,11},{12,13},{14,15},{16,17},{18,... | collective-permute-start | bytes 414728 | tf_op jit(solution)/shard_map/ppermute | solution.py:24
  29.3 3.4 %copy.20 = f32[30,144,8]{1,2,0:T(8,128)} copy(f32[30,144,8]{2,1,0:T(8,128)} %get-tuple-element.46) | data formatting | bytes 276480 | tf_op jit(solution)/shard_map/slice | solution.py:27
  32.6 1.3 %collective-permute-start.4 = (f32[30,144,8]{1,2,0:T(8,128)}, f32[30,144,8]{1,2,0:T(8,128)}, u32[]{:S(2)}, u32[]{:S(2)}) collective-permute-start(f32[30,144,8]{1,2,0:T(8,128)} %copy.20), channel_id=1, source_target_pairs={{1,0},{3,2},{5,4},{7,6},{9,8},{11,10},{13,12},{15,14},{17,16},{19,... | collective-permute-start | bytes 414728 | tf_op jit(solution)/shard_map/ppermute | solution.py:27
  34.1 3.0 %copy.21 = f32[30,144,8]{2,1,0:T(8,128)} copy(f32[30,144,8]{1,2,0:T(8,128)} %collective-permute-done.3) | data formatting | bytes 276480 | tf_op jit(solution)/shard_map/ppermute | solution.py:24
  37.1 3.0 %copy.22 = f32[30,144,8]{2,1,0:T(8,128)} copy(f32[30,144,8]{1,2,0:T(8,128)} %collective-permute-done.4) | data formatting | bytes 276480 | tf_op jit(solution)/shard_map/ppermute | solution.py:27
  40.1 4.1 %pad_maximum_fusion = f32[30,144,144]{2,1,0:T(8,128)S(1)} fusion(f32[30,144,8]{2,1,0:T(8,128)} %copy.22, f32[30,8,128]{2,1,0:T(8,128)S(1)} %collective-permute-done.2, f32[30,128,128]{2,1,0:T(8,128)S(1)} %constant_dynamic-update-slice_fusion, f32[30,8,128]{2,1,0:T(8,128)S(1)} %collective-permute-done.1, f32[30,144,8]{2,1,0:T(8,128)} %copy.21), kind=kLoop, calls=%fused_computation | loop fusion | flops 2488320 | bytes 4976640 | tf_op jit(solution)/shard_map/concatenate | solution.py:28
  49.3 4.5 %fusion.24 = f32[16,142,142]{2,1,0:T(8,128)S(1)} fusion(f32[16,144,144]{2,1,0:T(8,128)S(1)} %bitcast_multiply_fusion, f32[30,144,144]{2,1,0:T(8,128)S(1)} %pad_maximum_fusion, f32[142,142]{1,0:T(8,128)S(1)} %multiply_select_fusion.2, f32[142,142]{1,0:T(8,128)S(1)} %get-tuple-element.39, f32[142,142]{1,0:T(8,128)S(1)} %get-tuple-element.40, ...), kind=kLoop, calls=%fused_computation.42 | loop fusion | flops 5807232 | bytes 14699620 | tf_op jit(solution)/shard_map/jit(_where)/select_n | solution.py:43
  53.8 4.5 %fusion.14 = f32[16,140,140]{2,1,0:T(8,128)S(1)} fusion(f32[16,144,144]{2,1,0:T(8,128)S(1)} %bitcast_multiply_fusion, f32[16,142,142]{2,1,0:T(8,128)S(1)} %fusion.24, f32[140,140]{1,0:T(8,128)S(1)} %multiply_select_fusion.1, f32[140,140]{1,0:T(8,128)S(1)} %get-tuple-element.34, f32[140,140]{1,0:T(8,128)S(1)} %get-tuple-element.35, ...), kind=kLoop, calls=%fused_computation.24 | loop fusion | flops 5644800 | bytes 14288464 | tf_op jit(solution)/shard_map/jit(_where)/select_n | solution.py:43
  58.3 4.5 %fusion.4 = f32[16,138,138]{2,1,0:T(8,128)S(1)} fusion(f32[16,144,144]{2,1,0:T(8,128)S(1)} %bitcast_multiply_fusion, f32[16,140,140]{2,1,0:T(8,128)S(1)} %fusion.14, f32[138,138]{1,0:T(8,128)S(1)} %multiply_select_fusion, f32[138,138]{1,0:T(8,128)S(1)} %get-tuple-element.29, f32[138,138]{1,0:T(8,128)S(1)} %get-tuple-element.30, ...), kind=kLoop, calls=%fused_computation.6 | loop fusion | flops 5484672 | bytes 13883140 | tf_op jit(solution)/shard_map/jit(_where)/select_n | solution.py:43
  62.8 4.3 %fusion.64 = f32[16,136,136]{2,1,0:T(8,128)S(1)} fusion(f32[16,144,144]{2,1,0:T(8,128)S(1)} %bitcast_multiply_fusion, f32[16,138,138]{2,1,0:T(8,128)S(1)} %fusion.4, f32[136,136]{1,0:T(8,128)S(1)} %multiply_select_fusion.6, f32[136,136]{1,0:T(8,128)S(1)} %get-tuple-element.24, f32[136,136]{1,0:T(8,128)S(1)} %get-tuple-element.25, ...), kind=kLoop, calls=%fused_computation.115 | loop fusion | flops 5326848 | bytes 13483648 | tf_op jit(solution)/shard_map/jit(_where)/select_n | solution.py:43
  67.1 4.3 %fusion.54 = f32[16,134,134]{2,1,0:T(8,128)S(1)} fusion(f32[16,144,144]{2,1,0:T(8,128)S(1)} %bitcast_multiply_fusion, f32[16,136,136]{2,1,0:T(8,128)S(1)} %fusion.64, f32[134,134]{1,0:T(8,128)S(1)} %multiply_select_fusion.5, f32[134,134]{1,0:T(8,128)S(1)} %get-tuple-element.19, f32[134,134]{1,0:T(8,128)S(1)} %get-tuple-element.20, ...), kind=kLoop, calls=%fused_computation.97 | loop fusion | flops 5171328 | bytes 13089988 | tf_op jit(solution)/shard_map/jit(_where)/select_n | solution.py:43
  71.5 4.5 %fusion.44 = f32[16,132,132]{2,1,0:T(8,128)S(1)} fusion(f32[16,144,144]{2,1,0:T(8,128)S(1)} %bitcast_multiply_fusion, f32[16,134,134]{2,1,0:T(8,128)S(1)} %fusion.54, f32[132,132]{1,0:T(8,128)S(1)} %multiply_select_fusion.4, f32[132,132]{1,0:T(8,128)S(1)} %get-tuple-element.15, f32[132,132]{1,0:T(8,128)S(1)} %get-tuple-element.16, ...), kind=kLoop, calls=%fused_computation.79 | loop fusion | flops 5018112 | bytes 12702160 | tf_op jit(solution)/shard_map/jit(_where)/select_n | solution.py:43
  76.0 4.3 %fusion.34 = f32[16,130,130]{2,1,0:T(8,128)S(1)} fusion(f32[16,144,144]{2,1,0:T(8,128)S(1)} %bitcast_multiply_fusion, f32[16,132,132]{2,1,0:T(8,128)S(1)} %fusion.44, f32[130,130]{1,0:T(8,128)S(1)} %multiply_select_fusion.3, f32[130,130]{1,0:T(8,128)S(1)} %get-tuple-element.9, f32[130,130]{1,0:T(8,128)S(1)} %get-tuple-element.10, ...), kind=kLoop, calls=%fused_computation.61 | loop fusion | flops 4867200 | bytes 12320164 | tf_op jit(solution)/shard_map/jit(_where)/select_n | solution.py:43
  80.3 2.0 %fusion.74 = f32[16,128,128]{2,1,0:T(8,128)S(1)} fusion(f32[16,144,144]{2,1,0:T(8,128)S(1)} %bitcast_multiply_fusion, f32[16,130,130]{2,1,0:T(8,128)S(1)} %fusion.34, f32[128,128]{1,0:T(8,128)S(1)} %copy-done.5, f32[128,128]{1,0:T(8,128)S(1)} %copy-done.3, f32[128,128]{1,0:T(8,128)S(1)} %copy-done.4, f32[128,128]{1,0:T(8,128)S(1)} %get-tuple-element.50, ...), kind=kLoop, calls=%fused_computation.135 | loop fusion | flops 4718592 | bytes 11944000 | tf_op jit(solution)/shard_map/jit(_where)/select_n | solution.py:43
  82.9 1.6 %collective-permute-start.5 = (f32[4,128,128]{1,2,0:T(8,128)S(1)}, f32[4,128,128]{1,2,0:T(8,128)S(1)}, u32[]{:S(2)}, u32[]{:S(2)}) collective-permute-start(f32[4,128,128]{1,2,0:T(8,128)S(1)} %get-tuple-element.6), channel_id=1, source_target_pairs={{0,24},{8,0},{16,8},{24,16},{1,25},{9,1},{17,9},{25,17},{2,26},{10... | collective-permute-start | bytes 786440 | tf_op jit(solution)/shard_map/ppermute | solution.py:16
  84.6 6.7 %collective-permute-done.5 = f32[4,128,128]{1,2,0:T(8,128)S(1)} collective-permute-done((f32[4,128,128]{1,2,0:T(8,128)S(1)}, f32[4,128,128]{1,2,0:T(8,128)S(1)}, u32[]{:S(2)}, u32[]{:S(2)}) %collective-permute-start.5) | collective-permute-done | bytes 262176 | tf_op jit(solution)/shard_map/ppermute | solution.py:16
  91.5 15.4 %psum.7 = f32[4]{0:T(128)S(1)} all-reduce(f32[4]{0:T(128)S(1)} %fusion.80), channel_id=1, replica_groups=mesh['orb'=4,'gx'=4,'gy'=2] {'gx','gy'}, use_global_device_ids=true, to_apply=%region_3.4 | all-reduce | flops 4 | bytes 32 | tf_op jit(solution)/shard_map/psum | solution.py:106
  107.0 0.8 copy.29
  (74 shorter events, 8.4 us)
Async XLA Ops:
  0.6 4.5 %copy-start.2 = (f32[4,128,128]{2,1,0:T(8,128)S(1)}, f32[4,128,128]{2,1,0:T(8,128)}, u32[]{:S(2)}) copy-start(f32[4,128,128]{2,1,0:T(8,128)} %param.5) | copy-start | bytes 786436
  0.6 9.7 %copy-start.1 = (f32[5,128,128]{2,1,0:T(8,128)S(1)}, f32[5,128,128]{2,1,0:T(8,128)}, u32[]{:S(2)}) copy-start(f32[5,128,128]{2,1,0:T(8,128)} %param.7) | copy-start | bytes 983044
  0.6 10.5 %collective-permute-start = (f32[4,128,128]{2,1,0:T(8,128)}, f32[4,128,128]{2,1,0:T(8,128)S(1)}, u32[]{:S(2)}, u32[]{:S(2)}) collective-permute-start(f32[4,128,128]{2,1,0:T(8,128)} %param.5), channel_id=1, source_target_pairs={{0,8},{8,16},{16,24},{24,0},{1,9},{9,17},{17,25},{25,1},{2,10},{10... | collective-permute-start | bytes 786440 | tf_op jit(solution)/shard_map/ppermute | solution.py:16
  3.6 7.5 %copy-start.6 = (f32[128,128]{1,0:T(8,128)S(1)}, f32[128,128]{1,0:T(8,128)}, u32[]{:S(2)}) copy-start(f32[128,128]{1,0:T(8,128)} %param.8) | copy-start | bytes 196612
  11.2 6.1 %collective-permute-start.1 = (f32[30,8,128]{2,1,0:T(8,128)S(1)}, f32[30,8,128]{2,1,0:T(8,128)S(1)}, u32[]{:S(2)}, u32[]{:S(2)}) collective-permute-start(f32[30,8,128]{2,1,0:T(8,128)S(1)} %get-tuple-element.47), channel_id=1, source_target_pairs={{0,2},{2,4},{4,6},{1,3},{3,5},{5,7},{8,10},{10,12},{12,14},{9,11},... | collective-permute-start | bytes 368648 | tf_op jit(solution)/shard_map/ppermute | solution.py:24
  14.9 6.8 %collective-permute-start.2 = (f32[30,8,128]{2,1,0:T(8,128)S(1)}, f32[30,8,128]{2,1,0:T(8,128)S(1)}, u32[]{:S(2)}, u32[]{:S(2)}) collective-permute-start(f32[30,8,128]{2,1,0:T(8,128)S(1)} %get-tuple-element.48), channel_id=1, source_target_pairs={{2,0},{4,2},{6,4},{3,1},{5,3},{7,5},{10,8},{12,10},{14,12},{11,9},... | collective-permute-start | bytes 368648 | tf_op jit(solution)/shard_map/ppermute | solution.py:27
  24.6 9.3 %copy-start.15 = (s32[16]{0:T(128)S(1)}, s32[16]{0:T(128)}, u32[]{:S(2)}) copy-start(s32[16]{0:T(128)} %param.9) | copy-start | bytes 196
  27.3 6.8 %collective-permute-start.3 = (f32[30,144,8]{1,2,0:T(8,128)S(1)}, f32[30,144,8]{1,2,0:T(8,128)}, u32[]{:S(2)}, u32[]{:S(2)}) collective-permute-start(f32[30,144,8]{1,2,0:T(8,128)S(1)} %copy.19), channel_id=1, source_target_pairs={{0,1},{2,3},{4,5},{6,7},{8,9},{10,11},{12,13},{14,15},{16,17},{18,... | collective-permute-start | bytes 414728 | tf_op jit(solution)/shard_map/ppermute | solution.py:24
  32.6 4.5 %collective-permute-start.4 = (f32[30,144,8]{1,2,0:T(8,128)}, f32[30,144,8]{1,2,0:T(8,128)}, u32[]{:S(2)}, u32[]{:S(2)}) collective-permute-start(f32[30,144,8]{1,2,0:T(8,128)} %copy.20), channel_id=1, source_target_pairs={{1,0},{3,2},{5,4},{7,6},{9,8},{11,10},{13,12},{15,14},{17,16},{19,... | collective-permute-start | bytes 414728 | tf_op jit(solution)/shard_map/ppermute | solution.py:27
  48.5 0.8 copy-start.10
  49.3 4.5 %copy-start.9 = (pred[140,140]{1,0:T(8,128)(4,1)S(1)}, pred[140,140]{1,0:T(8,128)(4,1)}, u32[]{:S(2)}) copy-start(pred[140,140]{1,0:T(8,128)(4,1)} %slice.672) | copy-start | bytes 58804
  53.7 4.5 %copy-start.8 = (pred[138,138]{1,0:T(8,128)(4,1)S(1)}, pred[138,138]{1,0:T(8,128)(4,1)}, u32[]{:S(2)}) copy-start(pred[138,138]{1,0:T(8,128)(4,1)} %slice.671) | copy-start | bytes 57136
  58.3 4.5 %copy-start.14 = (pred[136,136]{1,0:T(8,128)(4,1)S(1)}, pred[136,136]{1,0:T(8,128)(4,1)}, u32[]{:S(2)}) copy-start(pred[136,136]{1,0:T(8,128)(4,1)} %slice.670) | copy-start | bytes 55492
  62.8 4.3 %copy-start.13 = (pred[134,134]{1,0:T(8,128)(4,1)S(1)}, pred[134,134]{1,0:T(8,128)(4,1)}, u32[]{:S(2)}) copy-start(pred[134,134]{1,0:T(8,128)(4,1)} %slice.669) | copy-start | bytes 53872
  67.1 4.4 %copy-start.12 = (pred[132,132]{1,0:T(8,128)(4,1)S(1)}, pred[132,132]{1,0:T(8,128)(4,1)}, u32[]{:S(2)}) copy-start(pred[132,132]{1,0:T(8,128)(4,1)} %slice.668) | copy-start | bytes 52276
  71.5 4.5 %copy-start.11 = (pred[130,130]{1,0:T(8,128)(4,1)S(1)}, pred[130,130]{1,0:T(8,128)(4,1)}, u32[]{:S(2)}) copy-start(pred[130,130]{1,0:T(8,128)(4,1)} %slice.667) | copy-start | bytes 50704
  76.0 4.3 %copy-start.3 = (f32[128,128]{1,0:T(8,128)S(1)}, f32[128,128]{1,0:T(8,128)}, u32[]{:S(2)}) copy-start(f32[128,128]{1,0:T(8,128)} %get-tuple-element.52) | copy-start | bytes 196612
  76.0 4.3 %copy-start.4 = (f32[128,128]{1,0:T(8,128)S(1)}, f32[128,128]{1,0:T(8,128)}, u32[]{:S(2)}) copy-start(f32[128,128]{1,0:T(8,128)} %get-tuple-element.53) | copy-start | bytes 196612
  76.0 4.3 %copy-start.5 = (f32[128,128]{1,0:T(8,128)S(1)}, f32[128,128]{1,0:T(8,128)}, u32[]{:S(2)}) copy-start(f32[128,128]{1,0:T(8,128)} %multiply_select_fusion.7) | copy-start | bytes 196612
  82.3 9.1 %copy-start = (f32[16,128,128]{2,1,0:T(8,128)}, f32[16,128,128]{2,1,0:T(8,128)S(1)}, u32[]{:S(2)}) copy-start(f32[16,128,128]{2,1,0:T(8,128)S(1)} %fusion.74) | copy-start | bytes 3145732
  82.4 2.1 %copy-start.7 = (f32[128,128]{1,0:T(8,128)S(1)}, f32[128,128]{1,0:T(8,128)}, u32[]{:S(2)}) copy-start(f32[128,128]{1,0:T(8,128)} %param.8) | copy-start | bytes 196612
  82.9 8.4 %collective-permute-start.5 = (f32[4,128,128]{1,2,0:T(8,128)S(1)}, f32[4,128,128]{1,2,0:T(8,128)S(1)}, u32[]{:S(2)}, u32[]{:S(2)}) collective-permute-start(f32[4,128,128]{1,2,0:T(8,128)S(1)} %get-tuple-element.6), channel_id=1, source_target_pairs={{0,24},{8,0},{16,8},{24,16},{1,25},{9,1},{17,9},{25,17},{2,26},{10... | collective-permute-start | bytes 786440 | tf_op jit(solution)/shard_map/ppermute | solution.py:16
where the time goes:
time: 108 us
  other arithmetic  40.9 us (38%)
  local copies, waits for them, and re-layouts  26 us (24%)
  blocking collectives  15.4 us (14%)
  starting transfers between devices  12.8 us (12%)
  waiting for transfers between devices  11.5 us (11%)
  between operations  1.19 us (1%)
    select_n x8, other arithmetic, relaxed_sweep(): result = jnp.where(inside[None], result, 0.0)  32.8 us
    psum x1, blocking collectives, local(): norm_sums = lax.psum(local_norms, ('gx', 'gy'))  15.4 us
    ppermute x2, waiting for transfers between devices, shifted(): lax.ppermute(value, axis, [(i, (i + by) % size) for i in range(size)])  6.76 us
    ppermute x2, starting transfers between devices, with_halo(): lax.ppermute(lax.slice_in_dim(block, block.shape[dim] - width, None, axis...  5.68 us
    slice x3, local copies, waits for them, and re-layouts, with_halo(): lax.slice_in_dim(block, block.shape[dim] - width, None, axis=dim)  5.43 us
    slice x8, local copies, waits for them, and re-layouts, deep_sweeps(): inside_all[lower:lower + row_count + 2 * (margin - 1), lower:lower + col_...  5.09 us
    ppermute x2, starting transfers between devices, shifted(): lax.ppermute(value, axis, [(i, (i + by) % size) for i in range(size)])  4.59 us
    ppermute x2, waiting for transfers between devices, with_halo(): lax.ppermute(lax.slice_in_dim(block, 0, width, axis=dim), axis, backward)  4.36 us
  transfers between devices with their start and end apart: 6, of which 4 were waited for; matrix products, arithmetic and copies ran while one was open for 14% of the time, Pallas kernels for 0%

commit v1 on v0

v1 whole, which is shorter than its diff:
```python
import functools

import jax
import jax.numpy as jnp
from jax import lax
from jax.experimental import pallas as pl
from jax.experimental.pallas import tpu as pltpu
from jax.sharding import PartitionSpec as P

SWEEPS = 8

relaxation = 0.8
screening = 0.02
step_size = 0.1

LANES = 128
SUB = 8
HALO = 8
STRIP = 32
BLOCKS = LANES // STRIP
VMEM_LIMIT = 40 * 1024 * 1024

VMEM = pl.BlockSpec(memory_space=pltpu.VMEM)
SMEM = pl.BlockSpec(memory_space=pltpu.SMEM)
ANY = pl.BlockSpec(memory_space=pl.ANY)


def f32(*shape):
    return jax.ShapeDtypeStruct(shape, jnp.float32)


def params(limit=VMEM_LIMIT):
    return pltpu.CompilerParams(vmem_limit_bytes=limit)


def lane_of(rows=SUB):
    return lax.broadcasted_iota(jnp.int32, (rows, LANES), 1)


def packed(fields):
    rows = fields[0].shape[0]
    block = lane_of(rows) // STRIP
    out = jnp.zeros((rows, LANES), jnp.float32)
    for at, value in enumerate(fields):
        turned = pltpu.roll(value, (STRIP * at + STRIP // 2) % LANES, 1)
        out = jnp.where(block == at, turned, out)
    return out


def replicated(value, at):
    one = jnp.where(lane_of(value.shape[0]) // STRIP == at, value, 0.0)
    one = one + pltpu.roll(one, STRIP, 1)
    return one + pltpu.roll(one, 2 * STRIP, 1)


def pack_kernel(v_ref, o_ref, m_ref, c_ref, e_ref):
    own = o_ref.shape[0]
    e_ref[0] = packed([o_ref[k] for k in range(own)])
    for first in range(own):
        e_ref[1 + first] = packed([v_ref[first * own + k] for k in range(own)])
    e_ref[1 + own] = packed([m_ref[...], c_ref[0], c_ref[1], c_ref[2]])
    e_ref[2 + own] = packed([c_ref[3], c_ref[4]])


def pack_edges(potentials, orbitals, metric, coefficients):
    own, rows, lanes = orbitals.shape
    return pl.pallas_call(
        pack_kernel,
        out_shape=f32(own + 3, rows, lanes),
        in_specs=[VMEM] * 4,
        out_specs=VMEM,
        compiler_params=params(),
        name="pack_edges",
    )(potentials, orbitals, metric, coefficients)


def rows_kernel(sides, par_ref, v_ref, o_ref, m_ref, c_ref, *refs):
    e_refs, (pay_a, pay_b), sems = refs[:sides], refs[sides : sides + 2], refs[sides + 2]
    own, rows, _ = o_ref.shape
    pairs = v_ref.shape[0]
    groups = e_refs[0].shape[0]
    odd = par_ref[0]
    copies = []

    def send(source, pay, start, at, count):
        copy = pltpu.make_async_copy(
            source.at[:, pl.ds(start, HALO), :], pay.at[pl.ds(at, count)], sems.at[len(copies)]
        )
        copy.start()
        copies.append(copy)

    for pay, start in ((pay_a, (1 - odd) * (rows - HALO)), (pay_b, odd * (rows - HALO))):
        start = pl.multiple_of(start, HALO)
        send(o_ref, pay, start, 0, own)
        at = own + sides
        send(v_ref, pay, start, at, pairs)
        at += pairs
        send(m_ref, pay, start, at, 1)
        send(c_ref, pay, start, at + 1, 5)
        at += 6
        for side, e_ref in enumerate(e_refs):
            send(e_ref.at[pl.ds(0, 1)], pay, start, own + side, 1)
            send(e_ref.at[pl.ds(1, groups - 1)], pay, start, at, groups - 1)
            at += groups - 1
    for copy in copies:
        copy.wait()


def row_payloads(odd, potentials, orbitals, metric, coefficients, received):
    own, rows, lanes = orbitals.shape
    sides = len(received)
    fields = own + potentials.shape[0] + 6 + sides * received[0].shape[0]
    return pl.pallas_call(
        functools.partial(rows_kernel, sides),
        out_shape=(f32(fields, HALO, lanes),) * 2,
        in_specs=[SMEM] + [ANY] * (4 + sides),
        out_specs=(ANY, ANY),
        scratch_shapes=[pltpu.SemaphoreType.DMA((2 * (4 + 2 * sides),))],
        compiler_params=params(),
        name="row_payloads",
    )(odd, potentials, orbitals, metric[None], coefficients, *received)


def spread(ref, count, *index):
    return [ref[(*index, pl.ds(t, SUB, stride=count), slice(None))] for t in range(count)]


def spread_store(ref, values, *index):
    count = len(values)
    for t, value in enumerate(values):
        ref[(*index, pl.ds(t, SUB, stride=count), slice(None))] = value


def scaled_coefs(coefs):
    total = coefs[0] + coefs[1] + coefs[2] + coefs[3] + 4.0 * coefs[4]
    diagonal = (1.0 + screening) * total
    return relaxation / jnp.where(diagonal == 0.0, 1.0, diagonal)


def swept(field, source, coefs, mask_west=None, mask_east=None):
    count = len(field)
    east = [pltpu.roll(v, LANES - 1, 1) for v in field]
    west = [pltpu.roll(v, 1, 1) for v in field]
    if mask_west is not None:
        west = [jnp.where(mask_west, 0.0, w) for w in west]
        east = [jnp.where(mask_east, 0.0, e) for e in east]
    slope = [e - w for e, w in zip(east, west)]

    def above(values, t):
        return values[t - 1] if t else pltpu.roll(values[count - 1], 1, 0)

    def below(values, t):
        return values[t + 1] if t < count - 1 else pltpu.roll(values[0], SUB - 1, 0)

    out = []
    for t in range(count):
        value = (1.0 - relaxation) * field[t] + source(t)
        value = value + coefs(0, t) * above(field, t) + coefs(1, t) * below(field, t)
        value = value + coefs(2, t) * east[t] + coefs(3, t) * west[t]
        out.append(value + coefs(4, t) * (above(slope, t) - below(slope, t)))
    return out


def relaxed(count, field, source, coefs, masks):
    west, east, dead = masks
    field = swept(field, source, coefs, west, east)
    field = [jnp.where(dead, 0.0, v) for v in field]

    def body(_, values):
        return tuple(swept(list(values), source, coefs))

    return list(lax.fori_loop(1, count, body, tuple(field)))


def lane_masks(odd):
    lane = lane_of()
    west = (lane == 0) & (odd == 0)
    east = (lane == LANES - 1) & (odd == 1)
    dead = lane == (1 - odd) * (LANES - 1)
    return west, east, dead


def interior_kernel(odd_ref, n_ref, v_ref, o_ref, p_ref, m_ref, c_ref, out_ref, cf, ms, sr):
    own, rows, _ = o_ref.shape
    count = rows // SUB
    masks = lane_masks(odd_ref[1])
    dead = masks[2]
    metric = spread(m_ref, count)
    raw = [spread(c_ref, count, n) for n in range(5)]
    for t in range(count):
        scale = scaled_coefs([raw[n][t] for n in range(5)])
        scale = jnp.where(dead, 0.0, scale)
        ms[t] = scale * metric[t]
        for n in range(5):
            cf[n, t] = scale * raw[n][t]

    def pair(p, carry):
        first, second = p // own, p % own
        o, q = spread(o_ref, count, first), spread(p_ref, count, second)
        for t in range(count):
            sr[t] = ms[t] * (o[t] * q[t])
        field = spread(v_ref, count, p)
        field = relaxed(n_ref[p], field, lambda t: sr[t], lambda n, t: cf[n, t], masks)
        spread_store(out_ref, field, p)
        return carry

    lax.fori_loop(0, v_ref.shape[0], pair, 0)


def interior(odd, counts, potentials, orbitals, partner, metric, coefficients):
    own, rows, lanes = orbitals.shape
    count = rows // SUB
    return pl.pallas_call(
        interior_kernel,
        out_shape=f32(*potentials.shape),
        in_specs=[SMEM, SMEM] + [VMEM] * 5,
        out_specs=VMEM,
        scratch_shapes=[
            pltpu.VMEM((5, count, SUB, lanes), jnp.float32),
            pltpu.VMEM((count, SUB, lanes), jnp.float32),
            pltpu.VMEM((count, SUB, lanes), jnp.float32),
        ],
        compiler_params=params(),
        name="interior",
    )(odd, counts, potentials, orbitals, partner, metric, coefficients)


def boundary_kernel(
    sides, odd_ref, n_ref, v_ref, o_ref, p_ref, m_ref, c_ref, inner_ref, e_ref, *refs
):
    recv = refs[:sides]
    ra_ref, rb_ref, p2_ref, pe_ref = refs[sides : sides + 4]
    out_ref, home_ref, back_ref = refs[sides + 4 : sides + 7]
    rb, rcf, rms, rsr, st, scf, sms, ssr, sv = refs[sides + 7 :]
    own, rows, _ = o_ref.shape
    pairs = v_ref.shape[0]
    groups = e_ref.shape[0]
    row_odd, col_odd = odd_ref[0], odd_ref[1]
    lane = lane_of()
    low_is_a = row_odd == 1

    def beyond(at):
        a, b = ra_ref[at], rb_ref[at]
        return jnp.where(low_is_a, a, b), jnp.where(low_is_a, b, a)

    def beyond_partner(at):
        a, b = p2_ref[at], p2_ref[own + sides + at]
        return jnp.where(low_is_a, a, b), jnp.where(low_is_a, b, a)

    v_at, m_at = own + sides, own + sides + pairs
    e_at = m_at + 6
    band = 3 * SUB

    def fill(at, low, high, top, bottom):
        rb[at, 0:SUB] = low
        rb[at, SUB:band] = top
        rb[at, band : band + 2 * SUB] = bottom
        rb[at, band + 2 * SUB : 2 * band] = high

    def fill_from(at, ends, ref, index):
        fill(
            at, *ends, ref[(*index, slice(0, 2 * SUB))], ref[(*index, slice(rows - 2 * SUB, rows))]
        )

    ends_o = [beyond(k) for k in range(own)]
    ends_p = [beyond_partner(k) for k in range(own)]
    ends_v = [beyond(v_at + k) for k in range(pairs)]
    ends_m = beyond(m_at)
    ends_c = [beyond(m_at + 1 + n) for n in range(5)]
    for k in range(pairs):
        fill_from(k, ends_v[k], v_ref, (k,))
    for k in range(own):
        fill_from(pairs + k, ends_o[k], o_ref, (k,))
        fill_from(pairs + own + k, ends_p[k], p_ref, (k,))
    fill_from(pairs + 2 * own, ends_m, m_ref, ())
    for n in range(5):
        fill_from(pairs + 2 * own + 1 + n, ends_c[n], c_ref, (n,))

    count = 2 * band // SUB
    masks = lane_masks(col_odd)
    metric = spread(rb, count, pairs + 2 * own)
    raw = [spread(rb, count, pairs + 2 * own + 1 + n) for n in range(5)]
    for t in range(count):
        scale = jnp.where(masks[2], 0.0, scaled_coefs([raw[n][t] for n in range(5)]))
        rms[t] = scale * metric[t]
        for n in range(5):
            rcf[n, t] = scale * raw[n][t]

    def row_pair(p, carry):
        first, second = p // own, p % own
        o, q = spread(rb, count, pairs + first), spread(rb, count, pairs + own + second)
        for t in range(count):
            rsr[t] = rms[t] * (o[t] * q[t])
        field = spread(rb, count, p)
        field = relaxed(n_ref[p], field, lambda t: rsr[t], lambda n, t: rcf[n, t], masks)
        spread_store(rb, field, p)
        inner_ref[p, 0:SUB] = rb[p, SUB : 2 * SUB]
        inner_ref[p, rows - SUB : rows] = rb[p, band + SUB : band + 2 * SUB]
        return carry

    lax.fori_loop(0, pairs, row_pair, 0)

    tall = rows + 2 * SUB
    high = tall // SUB
    corner_own = {}
    for end in range(2):
        corner_own[end] = [packed([ends_o[k][end] for k in range(own)])]
        for first in range(own):
            corner_own[end].append(
                packed([ends_v[first * own + k][end] for k in range(own)])
            )
        corner_own[end].append(packed([ends_m[end]] + [ends_c[n][end] for n in range(3)]))
        corner_own[end].append(packed([ends_c[n][end] for n in range(3, 5)]))
        corner_own[end].append(packed([ends_p[k][end] for k in range(own)]))
    own_partner = packed([p_ref[k] for k in range(own)])

    for side in range(sides):
        left_own = (col_odd == 0) if side == 0 else (col_odd == 1)
        from_own = jnp.where(left_own, lane % STRIP, STRIP - 1 - lane % STRIP) < STRIP // 2
        from_own_tall = (
            jnp.where(left_own, lane_of(rows) % STRIP, STRIP - 1 - lane_of(rows) % STRIP)
            < STRIP // 2
        )
        for g in range(groups + 1):
            if g == groups:
                mine, theirs = own_partner, pe_ref[side]
                ends = beyond_partner(own + side)
            else:
                mine, theirs = e_ref[g], recv[side][g]
                ends = (
                    beyond(own + side)
                    if g == 0
                    else beyond(e_at + side * (groups - 1) + g - 1)
                )
            st[g, SUB : SUB + rows] = jnp.where(from_own_tall, mine, theirs)
            st[g, 0:SUB] = jnp.where(from_own, corner_own[0][g], ends[0])
            st[g, SUB + rows : tall] = jnp.where(from_own, corner_own[1][g], ends[1])

        mg, cg = spread(st, high, own + 1), spread(st, high, own + 2)
        for t in range(high):
            cs = [replicated(mg[t], 1 + n) for n in range(3)]
            cs += [replicated(cg[t], n) for n in range(2)]
            scale = scaled_coefs(cs)
            sms[t] = scale * replicated(mg[t], 0)
            for n in range(5):
                scf[n, t] = scale * cs[n]

        def strip_group(g, carry):
            o, q = spread(st, high, 0), spread(st, high, groups)
            for t in range(high):
                ssr[t] = sms[t] * (replicated(o[t], g) * q[t])
            steps = jnp.zeros((SUB, LANES), jnp.int32)
            for k in range(own):
                steps = jnp.where(lane // STRIP == k, n_ref[g * own + k], steps)

            def body(s, values):
                new = swept(list(values), lambda t: ssr[t], lambda n, t: scf[n, t])
                return tuple(jnp.where(steps > s, n, v) for n, v in zip(new, values))

            field = tuple(spread(st, high, 1 + g))
            field = lax.fori_loop(0, SWEEPS, body, field)
            spread_store(sv, list(field), g)
            return carry

        lax.fori_loop(0, own, strip_group, 0)

        right = left_own
        edge = jnp.where(right, LANES - 1 - lane, lane) < HALO

        def merge(r, carry):
            at = pl.multiple_of(r * SUB, SUB)
            for first in range(own):
                strip = sv[first, pl.ds(at + SUB, SUB)]
                for second in range(own):
                    p = first * own + second
                    turned = pltpu.roll(strip, (-(STRIP * second + STRIP // 2)) % LANES, 1)
                    old = inner_ref[p, pl.ds(at, SUB)]
                    inner_ref[p, pl.ds(at, SUB)] = jnp.where(edge, turned, old)
            return carry

        lax.fori_loop(0, rows // SUB, merge, 0)

    def sums(r, carry):
        at = pl.multiple_of(r * SUB, SUB)
        o = [o_ref[k, pl.ds(at, SUB)] for k in range(own)]
        q = [p_ref[k, pl.ds(at, SUB)] for k in range(own)]
        home, back = [0.0] * own, [0.0] * own
        for first in range(own):
            for second in range(own):
                p = first * own + second
                v = inner_ref[p, pl.ds(at, SUB)]
                out_ref[p, pl.ds(at, SUB)] = v
                home[first] = home[first] + v * q[second]
                back[second] = back[second] + v * o[first]
        for k in range(own):
            home_ref[k, pl.ds(at, SUB)] = o[k] - step_size * home[k]
            back_ref[k, pl.ds(at, SUB)] = back[k]
        return carry

    lax.fori_loop(0, rows // SUB, sums, 0)


def boundary(
    odd, counts, potentials, orbitals, partner, metric, coefficients, inner, edges, received,
    rows_a, rows_b, partner_rows, partner_edges,
):
    own, rows, lanes = orbitals.shape
    sides = len(received)
    groups = edges.shape[0]
    pairs = potentials.shape[0]
    count, high = 6, rows // SUB + 2
    fields = pairs + 2 * own + 6
    return pl.pallas_call(
        functools.partial(boundary_kernel, sides),
        out_shape=(f32(*potentials.shape), f32(*orbitals.shape), f32(*orbitals.shape)),
        in_specs=[SMEM, SMEM] + [VMEM] * (7 + sides + 4),
        out_specs=(VMEM, VMEM, VMEM),
        scratch_shapes=[
            pltpu.VMEM((fields, count * SUB, lanes), jnp.float32),
            pltpu.VMEM((5, count, SUB, lanes), jnp.float32),
            pltpu.VMEM((count, SUB, lanes), jnp.float32),
            pltpu.VMEM((count, SUB, lanes), jnp.float32),
            pltpu.VMEM((groups + 1, high * SUB, lanes), jnp.float32),
            pltpu.VMEM((5, high, SUB, lanes), jnp.float32),
            pltpu.VMEM((high, SUB, lanes), jnp.float32),
            pltpu.VMEM((high, SUB, lanes), jnp.float32),
            pltpu.VMEM((own, high * SUB, lanes), jnp.float32),
        ],
        compiler_params=params(),
        name="boundary",
    )(
        odd, counts, potentials, orbitals, partner, metric, coefficients, inner, edges, *received,
        rows_a, rows_b, partner_rows, partner_edges,
    )


def norm_kernel(home_ref, recv_ref, m_ref, upd_ref, norm_ref):
    own = home_ref.shape[0]
    norm_ref[...] = jnp.zeros_like(norm_ref)
    for k in range(own):
        updated = home_ref[k] - step_size * recv_ref[k]
        upd_ref[k] = updated
        weighted = m_ref[...] * updated * updated
        norm_ref[k : k + 1] = jnp.sum(weighted, axis=0, keepdims=True)


def partial_norms(home, received, metric):
    own, _, lanes = home.shape
    return pl.pallas_call(
        norm_kernel,
        out_shape=(f32(*home.shape), f32(-(-own // SUB) * SUB, lanes)),
        in_specs=[VMEM] * 3,
        out_specs=(VMEM, VMEM),
        compiler_params=params(),
        name="partial_norms",
    )(home, received, metric)


def scale_kernel(cells, upd_ref, norm_ref, other_ref, out_ref):
    for k in range(upd_ref.shape[0]):
        total = norm_ref[k : k + 1] + other_ref[k : k + 1]
        norm = jnp.sum(total, axis=1, keepdims=True)
        out_ref[k] = upd_ref[k] * jnp.sqrt(cells / norm)


def rescaled(updated, norms, others, cells):
    return pl.pallas_call(
        functools.partial(scale_kernel, float(cells)),
        out_shape=f32(*updated.shape),
        in_specs=[VMEM] * 3,
        out_specs=VMEM,
        compiler_params=params(),
        name="rescaled",
    )(updated, norms, others)


def shifted(value, axis, by):
    size = lax.axis_size(axis)
    return lax.ppermute(value, axis, [(i, (i + by) % size) for i in range(size)])


def pair_swaps(size):
    even = [(i, i + 1) for i in range(0, size - 1, 2)]
    odd = [(i, i + 1) for i in range(1, size - 1, 2)]
    return [p + [(b, a) for a, b in p] for p in (even, odd)]


def local(orbitals, potentials, coefficients, metric, sweep_counts):
    own, rows, lanes = orbitals.shape
    gx, gy = lax.axis_size("gx"), lax.axis_size("gy")
    odd = jnp.stack([lax.axis_index("gx") % 2, lax.axis_index("gy") % 2]).astype(jnp.int32)
    col_swaps = [p for p in pair_swaps(gy) if p]
    row_swaps = pair_swaps(gx)

    partner = shifted(orbitals, "orb", 1)
    edges = pack_edges(potentials, orbitals, metric, coefficients)
    received = [lax.ppermute(edges, "gy", swap) for swap in col_swaps]
    pay_a, pay_b = row_payloads(odd, potentials, orbitals, metric, coefficients, received)
    rows_a = lax.ppermute(pay_a, "gx", row_swaps[0])
    rows_b = lax.ppermute(pay_b, "gx", row_swaps[1])
    sides = len(received)
    lead = own + sides
    beside = [rows_a[:lead], rows_b[:lead]]
    beside += [r[0].reshape(rows // SUB, SUB, lanes) for r in received]
    second = shifted(jnp.concatenate(beside, 0), "orb", 1)
    partner_rows = second[: 2 * lead]
    partner_edges = second[2 * lead :].reshape(sides, rows, lanes)

    inner = interior(odd, sweep_counts, potentials, orbitals, partner, metric, coefficients)
    fields, home, back = boundary(
        odd, sweep_counts, potentials, orbitals, partner, metric, coefficients, inner, edges,
        received, rows_a, rows_b, partner_rows, partner_edges,
    )
    updated, norms = partial_norms(home, shifted(back, "orb", -1), metric)
    hops = [("gy", 1 << k) for k in range(gy.bit_length() - 1)]
    hops += [("gx", 1 << k) for k in range(gx.bit_length() - 1)]
    for at, (axis, by) in enumerate(hops):
        size = lax.axis_size(axis)
        other = lax.ppermute(norms, axis, [(i, i ^ by) for i in range(size)])
        if at < len(hops) - 1:
            norms = norms + other
    return (rescaled(updated, norms, other, rows * lanes * gx * gy), fields)


def solution(mesh):
    return jax.shard_map(
        local,
        mesh=mesh,
        in_specs=(
            P("orb", "gx", "gy"),
            P("orb", "gx", "gy"),
            P(None, "gx", "gy"),
            P("gx", "gy"),
            P("orb"),
        ),
        out_specs=(P("orb", "gx", "gy"), P("orb", "gx", "gy")),
        check_vma=False,
    )
```

time: 108 us -> 66.5 us (0.62)
  other arithmetic: 40.9 us -> 0.09 us
  Pallas kernels: 0 us -> 31.4 us
  local copies, waits for them, and re-layouts: 26 us -> 3.07 us
  blocking collectives: 15.4 us -> 0 us
  starting transfers between devices: 12.8 us -> 17.6 us
  waiting for transfers between devices: 11.5 us -> 13.8 us
    select_n x16 -> x0, other arithmetic: 35.6 us -> none  [the longest x8 32.8 us: relaxed_sweep(): result = jnp.where(inside[None], result, 0.0)]
    pallas_call x0 -> x6, Pallas kernels: none -> 31.4 us  [the longest x1 16.4 us: boundary(): pl.pallas_call(functools.partial(boundary_kernel, sides), out_shape=(f32(...]
    psum x1 -> x0, blocking collectives: 15.4 us -> none  [local(): norm_sums = lax.psum(local_norms, ('gx', 'gy'))]
    slice x13 -> x3, local copies, waits for them, and re-layouts: 14 us -> 0.01 us  [the longest x2 0.01 us: local(): beside = [rows_a[:lead], rows_b[:lead]]]
    ppermute x3 -> x0, local copies, waits for them, and re-layouts: 6.14 us -> none  [the longest x1 3.02 us: with_halo(): lax.ppermute(lax.slice_in_dim(block, block.shape[dim] - width, None, axis...]
    concatenate x2 -> x1, other arithmetic: 4.22 us -> 0.01 us  [local(): second = shifted(jnp.concatenate(beside, 0), 'orb', 1)]
    ppermute x4 -> x6, waiting for transfers between devices: 4.76 us -> 7.6 us  [the longest x3 4.37 us: local(): other = lax.ppermute(norms, axis, [(i, i ^ by) for i in range(size)])]
    ppermute x2 -> x3, starting transfers between devices: 4.59 us -> 7.09 us  [shifted(): lax.ppermute(value, axis, [(i, (i + by) % size) for i in range(size)])]
  transfers between devices with their start and end apart: 6 -> 9, of which waited for: 4 -> 5; matrix products, arithmetic and copies ran while one was open for 14% -> 0% of each run, Pallas kernels for 0% -> 19%
where the time goes in v1:
time: 66.5 us; the launch traced here: 66.7 us
  Pallas kernels  31.4 us (47%)
  starting transfers between devices  17.6 us (26%)
  waiting for transfers between devices  13.8 us (21%)
  local copies, waits for them, and re-layouts  3.07 us (5%)
  between operations  0.76 us (1%)
    pallas_call x1, Pallas kernels, boundary(): pl.pallas_call(functools.partial(boundary_kernel, sides), out_shape=(f32(...  16.4 us
    pallas_call x1, Pallas kernels, interior(): pl.pallas_call(interior_kernel, out_shape=f32(*potentials.shape), in_spec...  11.2 us
    ppermute x3, starting transfers between devices, local(): other = lax.ppermute(norms, axis, [(i, i ^ by) for i in range(size)])  7.51 us
    ppermute x3, starting transfers between devices, shifted(): lax.ppermute(value, axis, [(i, (i + by) % size) for i in range(size)])  7.09 us
    ppermute x3, waiting for transfers between devices, shifted(): lax.ppermute(value, axis, [(i, (i + by) % size) for i in range(size)])  6.22 us
    ppermute x3, waiting for transfers between devices, local(): other = lax.ppermute(norms, axis, [(i, i ^ by) for i in range(size)])  4.37 us
    ppermute x1, waiting for transfers between devices, local(): rows_a = lax.ppermute(pay_a, 'gx', row_swaps[0])  3.22 us
    unnamed x14, local copies, waits for them, and re-layouts  3.05 us
  transfers between devices with their start and end apart: 9, of which 5 were waited for; matrix products, arithmetic and copies ran while one was open for 0% of the time, Pallas kernels for 19%

profile of v1, /device:TPU:0, one launch (start us, length us, event | category | flops | bytes accessed | tf_op | source)
XLA Modules:
  0.0 66.7 jit_solution(11163240949734474589)
XLA Ops:
  0.6 0.0 copy-start
  0.6 1.2 %copy-done = f32[16,128,128]{2,1,0:T(8,128)S(1)} copy-done((f32[16,128,128]{2,1,0:T(8,128)S(1)}, f32[16,128,128]{2,1,0:T(8,128)}, u32[]{:S(2)}) %copy-start) | copy-done | bytes 1048600
  1.9 1.0 %copy-done.2 = f32[5,128,128]{2,1,0:T(8,128)S(1)} copy-done((f32[5,128,128]{2,1,0:T(8,128)S(1)}, f32[5,128,128]{2,1,0:T(8,128)}, u32[]{:S(2)}) %copy-start.2) | copy-done | bytes 327704
  2.8 0.8 %copy-done.4 = f32[128,128]{1,0:T(8,128)S(1)} copy-done((f32[128,128]{1,0:T(8,128)S(1)}, f32[128,128]{1,0:T(8,128)}, u32[]{:S(2)}) %copy-start.4) | copy-done | bytes 65560
  3.7 1.6 %pack_edges.1.e_ref = f32[7,128,128]{2,1,0:T(8,128)S(1)} custom-call(f32[16,128,128]{2,1,0:T(8,128)S(1)} %copy-done, f32[4,128,128]{2,1,0:T(8,128)} %o_ref.7, f32[128,128]{1,0:T(8,128)S(1)} %copy-done.4, f32[5,128,128]{2,1,0:T(8,128)S(1)} %copy-done.2), custom_call_target="tpu_custom_call" | custom-call | tf_op jit(solution)/shard_map/pack_edges/pallas_call | solution.py:67
  5.2 0.5 collective-permute-start.1
  5.8 2.6 %collective-permute-start = (f32[4,128,128]{2,1,0:T(8,128)}, f32[4,128,128]{2,1,0:T(8,128)S(1)}, u32[]{:S(2)}, u32[]{:S(2)}) collective-permute-start(f32[4,128,128]{2,1,0:T(8,128)} %o_ref.7), channel_id=1, source_target_pairs={{0,8},{8,16},{16,24},{24,0},{1,9},{9,17},{17,25},{25,1},{2,10},{10... | collective-permute-start | bytes 786440 | tf_op jit(solution)/shard_map/ppermute | solution.py:479
  8.3 0.1 pad_add_fusion.odd_ref.par_ref
  8.4 0.0 collective-permute-done.1.refs_0_
  8.4 0.0 copy-done.1
  8.4 0.0 copy-done.3
  8.4 1.4 %row_payloads.1 = (f32[33,8,128]{2,1,0:T(8,128)S(1)}, f32[33,8,128]{2,1,0:T(8,128)S(1)}) custom-call(s32[2]{0:T(128)S(1)} %pad_add_fusion.odd_ref.par_ref, f32[16,128,128]{2,1,0:T(8,128)S(1)} %copy-done.1, f32[4,128,128]{2,1,0:T(8,128)} %o_ref.7, f32[1,128,128]{2,1,0:T(8,128)S(1)} %bitcast.7, f32[5,128,128]{2,1,0:T(8,128)S(1)} %copy-done.3, ...), custom_call_target="tpu_custom_call" | custom-call | tf_op jit(solution)/shard_map/row_payloads/pallas_call | solution.py:113
  9.8 1.8 %collective-permute-start.2 = (f32[33,8,128]{2,1,0:T(8,128)S(1)}, f32[33,8,128]{2,1,0:T(8,128)S(1)}, u32[]{:S(2)}, u32[]{:S(2)}) collective-permute-start(f32[33,8,128]{2,1,0:T(8,128)S(1)} %get-tuple-element.9), channel_id=1, source_target_pairs={{0,2},{4,6},{2,0},{6,4},{1,3},{5,7},{3,1},{7,5},{8,10},{12,14},{10... | collective-permute-start | bytes 405512 | tf_op jit(solution)/shard_map/ppermute | solution.py:499
  11.6 0.7 collective-permute-start.3
  12.3 3.2 %collective-permute-done.2.refs_1_ = f32[33,8,128]{2,1,0:T(8,128)S(1)} collective-permute-done((f32[33,8,128]{2,1,0:T(8,128)S(1)}, f32[33,8,128]{2,1,0:T(8,128)S(1)}, u32[]{:S(2)}, u32[]{:S(2)}) %collective-permute-start.2) | collective-permute-done | bytes 135200 | tf_op jit(solution)/shard_map/ppermute | solution.py:499
  15.6 0.0 collective-permute-done.3.refs_2_
  15.6 0.0 copy-start.6
  15.6 1.7 %collective-permute-start.4 = (f32[26,8,128]{2,1,0:T(8,128)S(1)}, f32[26,8,128]{2,1,0:T(8,128)S(1)}, u32[]{:S(2)}, u32[]{:S(2)}) collective-permute-start(f32[26,8,128]{2,1,0:T(8,128)S(1)} %pad_maximum_fusion), channel_id=1, source_target_pairs={{0,8},{8,16},{16,24},{24,0},{1,9},{9,17},{17,25},{25,1},{2,10},{10... | collective-permute-start | bytes 319496 | tf_op jit(solution)/shard_map/ppermute | solution.py:479
  17.3 0.0 collective-permute-done.p_ref
  17.3 11.2 %interior.1.inner_ref = f32[16,128,128]{2,1,0:T(8,128)S(1)} custom-call(s32[2]{0:T(128)S(1)} %pad_add_fusion.odd_ref.par_ref, s32[16]{0:T(128)S(1)} %copy-done.6, f32[16,128,128]{2,1,0:T(8,128)S(1)} %copy-done.1, f32[4,128,128]{2,1,0:T(8,128)} %o_ref.7, f32[4,128,128]{2,1,0:T(8,128)S(1)} %collective-permute-done.p_ref, f32[128,128]{1,0:T(8,128)S(1)} %copy-done.5, ...), custom_call_target="tpu_custom_call" | custom-call | tf_op jit(solution)/shard_map/interior/pallas_call | solution.py:213
  28.5 0.0 collective-permute-done.4
  28.5 16.4 %boundary.1 = (f32[16,128,128]{2,1,0:T(8,128)}, f32[4,128,128]{2,1,0:T(8,128)S(1)}, f32[4,128,128]{2,1,0:T(8,128)S(1)}) custom-call(s32[2]{0:T(128)S(1)} %pad_add_fusion.odd_ref.par_ref, s32[16]{0:T(128)S(1)} %copy-done.6, f32[16,128,128]{2,1,0:T(8,128)S(1)} %copy-done.1, f32[4,128,128]{2,1,0:T(8,128)} %o_ref.7, ...), custom_call_target="tpu_custom_call" | custom-call | tf_op jit(solution)/shard_map/boundary/pallas_call | solution.py:413
  44.9 2.9 %collective-permute-start.5 = (f32[4,128,128]{2,1,0:T(8,128)S(1)}, f32[4,128,128]{2,1,0:T(8,128)S(1)}, u32[]{:S(2)}, u32[]{:S(2)}) collective-permute-start(f32[4,128,128]{2,1,0:T(8,128)S(1)} %get-tuple-element.12), channel_id=1, source_target_pairs={{0,24},{8,0},{16,8},{24,16},{1,25},{9,1},{17,9},{25,17},{2,26},{10... | collective-permute-start | bytes 786440 | tf_op jit(solution)/shard_map/ppermute | solution.py:479
  47.7 6.2 %collective-permute-done.5.recv_ref = f32[4,128,128]{2,1,0:T(8,128)S(1)} collective-permute-done((f32[4,128,128]{2,1,0:T(8,128)S(1)}, f32[4,128,128]{2,1,0:T(8,128)S(1)}, u32[]{:S(2)}, u32[]{:S(2)}) %collective-permute-start.5) | collective-permute-done | bytes 262176 | tf_op jit(solution)/shard_map/ppermute | solution.py:479
  53.9 0.1 partial_norms.1
  54.0 0.1 collective-permute-start.6
  54.1 1.2 %collective-permute-done.6 = f32[8,128]{1,0:T(8,128)S(1)} collective-permute-done((f32[8,128]{1,0:T(8,128)S(1)}, f32[8,128]{1,0:T(8,128)S(1)}, u32[]{:S(2)}, u32[]{:S(2)}) %collective-permute-start.6) | collective-permute-done | bytes 4128 | tf_op jit(solution)/shard_map/ppermute | solution.py:519
  55.2 4.6 %collective-permute-start.7 = (f32[8,128]{1,0:T(8,128)S(1)}, f32[8,128]{1,0:T(8,128)S(1)}, u32[]{:S(2)}, u32[]{:S(2)}) collective-permute-start(f32[8,128]{1,0:T(8,128)S(1)} %add.15), channel_id=1, source_target_pairs={{0,2},{2,0},{4,6},{6,4},{1,3},{3,1},{5,7},{7,5},{8,10},{10,8},{12,... | collective-permute-start | bytes 12296 | tf_op jit(solution)/shard_map/ppermute | solution.py:519
  59.8 1.6 %collective-permute-done.7 = f32[8,128]{1,0:T(8,128)S(1)} collective-permute-done((f32[8,128]{1,0:T(8,128)S(1)}, f32[8,128]{1,0:T(8,128)S(1)}, u32[]{:S(2)}, u32[]{:S(2)}) %collective-permute-start.7) | collective-permute-done | bytes 4128 | tf_op jit(solution)/shard_map/ppermute | solution.py:519
  61.4 2.9 %collective-permute-start.8 = (f32[8,128]{1,0:T(8,128)S(1)}, f32[8,128]{1,0:T(8,128)S(1)}, u32[]{:S(2)}, u32[]{:S(2)}) collective-permute-start(f32[8,128]{1,0:T(8,128)S(1)} %add.16.norm_ref), channel_id=1, source_target_pairs={{0,4},{2,6},{4,0},{6,2},{1,5},{3,7},{5,1},{7,3},{8,12},{10,14},{12... | collective-permute-start | bytes 12296 | tf_op jit(solution)/shard_map/ppermute | solution.py:519
  64.3 1.6 %collective-permute-done.8.other_ref = f32[8,128]{1,0:T(8,128)S(1)} collective-permute-done((f32[8,128]{1,0:T(8,128)S(1)}, f32[8,128]{1,0:T(8,128)S(1)}, u32[]{:S(2)}, u32[]{:S(2)}) %collective-permute-start.8) | collective-permute-done | bytes 4128 | tf_op jit(solution)/shard_map/ppermute | solution.py:519
  65.9 0.8 %rescaled.1 = f32[4,128,128]{2,1,0:T(8,128)} custom-call(f32[4,128,128]{2,1,0:T(8,128)S(1)} %get-tuple-element.13.upd_ref, f32[8,128]{1,0:T(8,128)S(1)} %add.16.norm_ref, f32[8,128]{1,0:T(8,128)S(1)} %collective-permute-done.8.other_ref), custom_call_target="tpu_custom_call" | custom-call | tf_op jit(solution)/shard_map/rescaled/pallas_call | solution.py:467
  (15 shorter events, 0.1 us)
Async XLA Ops:
  0.6 1.2 %copy-start = (f32[16,128,128]{2,1,0:T(8,128)S(1)}, f32[16,128,128]{2,1,0:T(8,128)}, u32[]{:S(2)}) copy-start(f32[16,128,128]{2,1,0:T(8,128)} %v_ref.7) | copy-start | bytes 3145732
  1.9 1.0 %copy-start.2 = (f32[5,128,128]{2,1,0:T(8,128)S(1)}, f32[5,128,128]{2,1,0:T(8,128)}, u32[]{:S(2)}) copy-start(f32[5,128,128]{2,1,0:T(8,128)} %c_ref.7) | copy-start | bytes 983044
  2.8 0.8 %copy-start.4 = (f32[128,128]{1,0:T(8,128)S(1)}, f32[128,128]{1,0:T(8,128)}, u32[]{:S(2)}) copy-start(f32[128,128]{1,0:T(8,128)} %m_ref.7) | copy-start | bytes 196612
  3.7 4.7 %copy-start.1 = (f32[16,128,128]{2,1,0:T(8,128)S(1)}, f32[16,128,128]{2,1,0:T(8,128)}, u32[]{:S(2)}) copy-start(f32[16,128,128]{2,1,0:T(8,128)} %v_ref.7) | copy-start | bytes 3145732
  3.7 4.7 %copy-start.3 = (f32[5,128,128]{2,1,0:T(8,128)S(1)}, f32[5,128,128]{2,1,0:T(8,128)}, u32[]{:S(2)}) copy-start(f32[5,128,128]{2,1,0:T(8,128)} %c_ref.7) | copy-start | bytes 983044
  3.7 4.7 %copy-start.5 = (f32[128,128]{1,0:T(8,128)S(1)}, f32[128,128]{1,0:T(8,128)}, u32[]{:S(2)}) copy-start(f32[128,128]{1,0:T(8,128)} %m_ref.7) | copy-start | bytes 196612
  5.2 3.1 %collective-permute-start.1 = (f32[7,128,128]{2,1,0:T(8,128)S(1)}, f32[7,128,128]{2,1,0:T(8,128)S(1)}, u32[]{:S(2)}, u32[]{:S(2)}) collective-permute-start(f32[7,128,128]{2,1,0:T(8,128)S(1)} %pack_edges.1.e_ref), channel_id=1, source_target_pairs={{0,1},{1,0},{2,3},{3,2},{4,5},{5,4},{6,7},{7,6},{8,9},{9,8},{10,11... | collective-permute-start | bytes 1376264 | tf_op jit(solution)/shard_map/ppermute | solution.py:497
  5.8 11.5 %collective-permute-start = (f32[4,128,128]{2,1,0:T(8,128)}, f32[4,128,128]{2,1,0:T(8,128)S(1)}, u32[]{:S(2)}, u32[]{:S(2)}) collective-permute-start(f32[4,128,128]{2,1,0:T(8,128)} %o_ref.7), channel_id=1, source_target_pairs={{0,8},{8,16},{16,24},{24,0},{1,9},{9,17},{17,25},{25,1},{2,10},{10... | collective-permute-start | bytes 786440 | tf_op jit(solution)/shard_map/ppermute | solution.py:479
  9.8 5.7 %collective-permute-start.2 = (f32[33,8,128]{2,1,0:T(8,128)S(1)}, f32[33,8,128]{2,1,0:T(8,128)S(1)}, u32[]{:S(2)}, u32[]{:S(2)}) collective-permute-start(f32[33,8,128]{2,1,0:T(8,128)S(1)} %get-tuple-element.9), channel_id=1, source_target_pairs={{0,2},{4,6},{2,0},{6,4},{1,3},{5,7},{3,1},{7,5},{8,10},{12,14},{10... | collective-permute-start | bytes 405512 | tf_op jit(solution)/shard_map/ppermute | solution.py:499
  11.6 3.9 %collective-permute-start.3 = (f32[33,8,128]{2,1,0:T(8,128)S(1)}, f32[33,8,128]{2,1,0:T(8,128)S(1)}, u32[]{:S(2)}, u32[]{:S(2)}) collective-permute-start(f32[33,8,128]{2,1,0:T(8,128)S(1)} %get-tuple-element.10), channel_id=1, source_target_pairs={{2,4},{4,2},{3,5},{5,3},{10,12},{12,10},{11,13},{13,11},{18,20},{2... | collective-permute-start | bytes 405512 | tf_op jit(solution)/shard_map/ppermute | solution.py:500
  15.6 1.7 %copy-start.6 = (s32[16]{0:T(128)S(1)}, s32[16]{0:T(128)}, u32[]{:S(2)}) copy-start(s32[16]{0:T(128)} %n_ref.3) | copy-start | bytes 196
  15.6 12.9 %collective-permute-start.4 = (f32[26,8,128]{2,1,0:T(8,128)S(1)}, f32[26,8,128]{2,1,0:T(8,128)S(1)}, u32[]{:S(2)}, u32[]{:S(2)}) collective-permute-start(f32[26,8,128]{2,1,0:T(8,128)S(1)} %pad_maximum_fusion), channel_id=1, source_target_pairs={{0,8},{8,16},{16,24},{24,0},{1,9},{9,17},{17,25},{25,1},{2,10},{10... | collective-permute-start | bytes 319496 | tf_op jit(solution)/shard_map/ppermute | solution.py:479
  44.9 9.1 %collective-permute-start.5 = (f32[4,128,128]{2,1,0:T(8,128)S(1)}, f32[4,128,128]{2,1,0:T(8,128)S(1)}, u32[]{:S(2)}, u32[]{:S(2)}) collective-permute-start(f32[4,128,128]{2,1,0:T(8,128)S(1)} %get-tuple-element.12), channel_id=1, source_target_pairs={{0,24},{8,0},{16,8},{24,16},{1,25},{9,1},{17,9},{25,17},{2,26},{10... | collective-permute-start | bytes 786440 | tf_op jit(solution)/shard_map/ppermute | solution.py:479
  54.0 1.2 %collective-permute-start.6 = (f32[8,128]{1,0:T(8,128)S(1)}, f32[8,128]{1,0:T(8,128)S(1)}, u32[]{:S(2)}, u32[]{:S(2)}) collective-permute-start(f32[8,128]{1,0:T(8,128)S(1)} %get-tuple-element.14), channel_id=1, source_target_pairs={{0,1},{1,0},{2,3},{3,2},{4,5},{5,4},{6,7},{7,6},{8,9},{9,8},{10,11... | collective-permute-start | bytes 12296 | tf_op jit(solution)/shard_map/ppermute | solution.py:519
  55.2 6.2 %collective-permute-start.7 = (f32[8,128]{1,0:T(8,128)S(1)}, f32[8,128]{1,0:T(8,128)S(1)}, u32[]{:S(2)}, u32[]{:S(2)}) collective-permute-start(f32[8,128]{1,0:T(8,128)S(1)} %add.15), channel_id=1, source_target_pairs={{0,2},{2,0},{4,6},{6,4},{1,3},{3,1},{5,7},{7,5},{8,10},{10,8},{12,... | collective-permute-start | bytes 12296 | tf_op jit(solution)/shard_map/ppermute | solution.py:519
  61.4 4.5 %collective-permute-start.8 = (f32[8,128]{1,0:T(8,128)S(1)}, f32[8,128]{1,0:T(8,128)S(1)}, u32[]{:S(2)}, u32[]{:S(2)}) collective-permute-start(f32[8,128]{1,0:T(8,128)S(1)} %add.16.norm_ref), channel_id=1, source_target_pairs={{0,4},{2,6},{4,0},{6,2},{1,5},{3,7},{5,1},{7,3},{8,12},{10,14},{12... | collective-permute-start | bytes 12296 | tf_op jit(solution)/shard_map/ppermute | solution.py:519

commit v2 on v0

v2 whole, which is shorter than its diff:
```python
import functools

import jax
import jax.numpy as jnp
from jax import lax
from jax.experimental import pallas as pl
from jax.experimental.pallas import tpu as pltpu
from jax.sharding import PartitionSpec as P

SWEEPS = 8

relaxation = 0.8
screening = 0.02
step_size = 0.1

LANES = 128
SUB = 8
HALO = 8
STRIP = 32
LEAST = 4
GROUP = 4
BANDS = 8
AHEAD = 16
VMEM_LIMIT = 40 * 1024 * 1024

VMEM = pl.BlockSpec(memory_space=pltpu.VMEM)
SMEM = pl.BlockSpec(memory_space=pltpu.SMEM)
ANY = pl.BlockSpec(memory_space=pl.ANY)


def f32(*shape):
    return jax.ShapeDtypeStruct(shape, jnp.float32)


def params(limit=VMEM_LIMIT):
    return pltpu.CompilerParams(vmem_limit_bytes=limit)


def lane_of(rows=SUB):
    return lax.broadcasted_iota(jnp.int32, (rows, LANES), 1)


def packed(fields):
    rows = fields[0].shape[0]
    block = lane_of(rows) // STRIP
    out = jnp.zeros((rows, LANES), jnp.float32)
    for at, value in enumerate(fields):
        turned = pltpu.roll(value, (STRIP * at + STRIP // 2) % LANES, 1)
        out = jnp.where(block == at, turned, out)
    return out


def replicated(value, at):
    one = jnp.where(lane_of(value.shape[0]) // STRIP == at, value, 0.0)
    one = one + pltpu.roll(one, STRIP, 1)
    return one + pltpu.roll(one, 2 * STRIP, 1)


def spread(ref, count, *index):
    return [ref[(*index, pl.ds(t, SUB, stride=count), slice(None))] for t in range(count)]


def spread_store(ref, values, *index):
    count = len(values)
    for t, value in enumerate(values):
        ref[(*index, pl.ds(t, SUB, stride=count), slice(None))] = value


def scaled_coefs(coefs):
    total = coefs[0] + coefs[1] + coefs[2] + coefs[3] + 4.0 * coefs[4]
    diagonal = (1.0 + screening) * total
    return relaxation / jnp.where(diagonal == 0.0, 1.0, diagonal)


def sweep(fields, count, old, new, source, coefs, west=None, east=None, dead=None, keep=None):
    held, to_east, to_west, slopes = {}, {}, {}, {}

    def issue(k, t):
        value = old[k, t]
        held[k, t] = value
        e, w = pltpu.roll(value, LANES - 1, 1), pltpu.roll(value, 1, 1)
        if west is not None:
            w, e = jnp.where(west, 0.0, w), jnp.where(east, 0.0, e)
        to_east[k, t], to_west[k, t] = e, w

    def field(k, t):
        return held[k, t]

    def slope(k, t):
        if (k, t) not in slopes:
            slopes[k, t] = to_east[k, t] - to_west[k, t]
        return slopes[k, t]

    def above(get, k, t):
        return get(k, t - 1) if t else pltpu.roll(get(k, count - 1), 1, 0)

    def below(get, k, t):
        return get(k, t + 1) if t < count - 1 else pltpu.roll(get(k, 0), SUB - 1, 0)

    order = []
    for k in range(fields):
        order += [(k, count - 1)] + [(k, t) for t in range(count - 1)]
    done = 0
    for at in range(fields * count):
        k, t = divmod(at, count)
        until = min(len(order), max(at + AHEAD, k * count + min(t + 3, count)))
        while done < until:
            issue(*order[done])
            done += 1
        value = (1.0 - relaxation) * field(k, t) + source[k, t]
        value = value + coefs[0, t] * above(field, k, t) + coefs[1, t] * below(field, k, t)
        value = value + coefs[2, t] * to_east[k, t] + coefs[3, t] * to_west[k, t]
        value = value + coefs[4, t] * (above(slope, k, t) - below(slope, k, t))
        if dead is not None:
            value = jnp.where(dead, 0.0, value)
        if keep is not None:
            value = jnp.where(keep[k], value, field(k, t))
        new[k, t] = value


def relax(steps, count, here, there, source, coefs, masks):
    fields = len(steps)
    west, east, dead = masks
    pair = (here, there)
    sweep(fields, count, here, there, source, coefs, west, east, dead)
    for s in range(1, LEAST):
        sweep(fields, count, pair[s % 2], pair[1 - s % 2], source, coefs)
    top = functools.reduce(jnp.maximum, steps)

    def body(turn, carry):
        for s in range(2):
            at = LEAST + 2 * turn + s
            keep = [jnp.full((SUB, LANES), n, jnp.int32) > at for n in steps]
            sweep(fields, count, pair[s], pair[1 - s], source, coefs, keep=keep)
        return carry

    lax.fori_loop(0, (top - LEAST + 1) // 2, body, 0)


def lane_masks(odd):
    lane = lane_of()
    west = (lane == 0) & (odd == 0)
    east = (lane == LANES - 1) & (odd == 1)
    dead = lane == (1 - odd) * (LANES - 1)
    return west, east, dead


def prepare_kernel(odd_ref, v_ref, o_ref, m_ref, c_ref, vs_ref, om_ref, cf_ref, e_ref):
    own, rows, _ = o_ref.shape
    count = rows // SUB
    e_ref[0] = packed([o_ref[k] for k in range(own)])
    for first in range(own):
        e_ref[1 + first] = packed([v_ref[first * own + k] for k in range(own)])
    e_ref[1 + own] = packed([m_ref[...], c_ref[0], c_ref[1], c_ref[2]])
    e_ref[2 + own] = packed([c_ref[3], c_ref[4]])
    dead = lane_masks(odd_ref[1])[2]
    metric = spread(m_ref, count)
    raw = [spread(c_ref, count, n) for n in range(5)]
    weights = []
    for t in range(count):
        scale = jnp.where(dead, 0.0, scaled_coefs([raw[n][t] for n in range(5)]))
        weights.append(scale * metric[t])
        for n in range(5):
            cf_ref[n, t] = scale * raw[n][t]
    for k in range(own):
        for t, value in enumerate(spread(o_ref, count, k)):
            om_ref[k, t] = weights[t] * value

    def one(p, carry):
        for t, value in enumerate(spread(v_ref, count, p)):
            vs_ref[p, t] = value
        return carry

    lax.fori_loop(0, v_ref.shape[0], one, 0)


def prepare(odd, potentials, orbitals, metric, coefficients):
    own, rows, lanes = orbitals.shape
    count = rows // SUB
    return pl.pallas_call(
        prepare_kernel,
        out_shape=(
            f32(potentials.shape[0], count, SUB, lanes),
            f32(own, count, SUB, lanes),
            f32(5, count, SUB, lanes),
            f32(own + 3, rows, lanes),
        ),
        in_specs=[SMEM] + [VMEM] * 4,
        out_specs=(VMEM,) * 4,
        compiler_params=params(),
        name="prepare",
    )(odd, potentials, orbitals, metric, coefficients)


def rows_kernel(par_ref, o_ref, v_ref, m_ref, c_ref, pay_a, pay_b, sems):
    rows = o_ref.shape[1]
    odd = par_ref[0]
    copies = []
    for pay, start in ((pay_a, (1 - odd) * (rows - HALO)), (pay_b, odd * (rows - HALO))):
        start = pl.multiple_of(start, HALO)
        at = 0
        for ref in (o_ref, v_ref, m_ref, c_ref):
            count = ref.shape[0]
            copy = pltpu.make_async_copy(
                ref.at[:, pl.ds(start, HALO), :], pay.at[pl.ds(at, count)], sems.at[len(copies)]
            )
            copy.start()
            copies.append(copy)
            at += count
    for copy in copies:
        copy.wait()


def row_payloads(odd, orbitals, potentials, metric, coefficients):
    own, _, lanes = orbitals.shape
    fields = own + potentials.shape[0] + 1 + coefficients.shape[0]
    return pl.pallas_call(
        rows_kernel,
        out_shape=(f32(fields, HALO, lanes),) * 2,
        in_specs=[SMEM] + [ANY] * 4,
        out_specs=(ANY, ANY),
        scratch_shapes=[pltpu.SemaphoreType.DMA((8,))],
        compiler_params=params(),
        name="row_payloads",
    )(odd, orbitals, potentials, metric[None], coefficients)


def interior_kernel(groups, before, odd_ref, n_ref, by_ref, vs_ref, om_ref, cf_ref, p_ref, *refs):
    out_ref, qs, sr, va, vb = refs[-5:]
    own, count = om_ref.shape[:2]
    masks = lane_masks(odd_ref[1])
    if before:
        earlier = refs[0]

        def keep(k, carry):
            out_ref[by_ref[k]] = earlier[by_ref[k]]
            return carry

        lax.fori_loop(0, before * GROUP, keep, 0)
    for k in range(own):
        for t, value in enumerate(spread(p_ref, count, k)):
            qs[k, t] = value

    def group(g, carry):
        pairs = [by_ref[g * GROUP + k] for k in range(GROUP)]
        for k, p in enumerate(pairs):
            first, second = p // own, p % own
            for t in range(count):
                sr[k, t] = om_ref[first, t] * qs[second, t]
                va[k, t] = vs_ref[p, t]
        relax([n_ref[p] for p in pairs], count, va, vb, sr, cf_ref, masks)
        for k, p in enumerate(pairs):
            spread_store(out_ref, [va[k, t] for t in range(count)], p)
        return carry

    lax.fori_loop(before, before + groups, group, 0)


def interior(groups, before, odd, counts, order, ready, partner, *earlier):
    spread_v, weighted, coefs, _ = ready
    pairs, count, _, lanes = spread_v.shape
    own, rows, _ = partner.shape
    four = pltpu.VMEM((GROUP, count, SUB, lanes), jnp.float32)
    return pl.pallas_call(
        functools.partial(interior_kernel, groups, before),
        out_shape=f32(pairs, rows, lanes),
        in_specs=[SMEM] * 3 + [VMEM] * (4 + len(earlier)),
        out_specs=VMEM,
        scratch_shapes=[pltpu.VMEM((own, count, SUB, lanes), jnp.float32), four, four, four],
        compiler_params=params(),
        name=f"interior{before}",
    )(odd, counts, order, spread_v, weighted, coefs, partner, *earlier)


def beyond(odd, a, b):
    low_is_a = odd == 1
    return jnp.where(low_is_a, a, b), jnp.where(low_is_a, b, a)


def edges_kernel(odd_ref, e_ref, ra_ref, rb_ref, p2_ref, p_ref, out_ref):
    own, rows, _ = p_ref.shape
    odd = odd_ref[0]
    groups = e_ref.shape[0]
    for g in range(groups):
        out_ref[g, SUB : SUB + rows] = e_ref[g]
    out_ref[groups, SUB : SUB + rows] = packed([p_ref[k] for k in range(own)])
    pairs = own * own
    ends = [beyond(odd, ra_ref[f], rb_ref[f]) for f in range(own + pairs + 6)]
    ends += [beyond(odd, p2_ref[k], p2_ref[own + k]) for k in range(own)]
    lists = [range(own)] + [range(own * (1 + k), own * (2 + k)) for k in range(own)]
    at = own + pairs
    lists += [range(at, at + 4), range(at + 4, at + 6), range(at + 6, at + 6 + own)]
    for g, fields in enumerate(lists):
        out_ref[g, 0:SUB] = packed([ends[f][0] for f in fields])
        out_ref[g, SUB + rows :] = packed([ends[f][1] for f in fields])


def tall_edges(odd, edges, rows_a, rows_b, partner_rows, partner):
    groups, rows, lanes = edges.shape
    return pl.pallas_call(
        edges_kernel,
        out_shape=f32(groups + 1, rows + 2 * SUB, lanes),
        in_specs=[SMEM] + [VMEM] * 5,
        out_specs=VMEM,
        compiler_params=params(),
        name="tall_edges",
    )(odd, edges, rows_a, rows_b, partner_rows, partner)


def bands_kernel(
    odd_ref, n_ref, by_ref, v_ref, o_ref, p_ref, m_ref, c_ref, ra_ref, rb_ref, p2_ref,
    out_ref, band, cf, ms, sr, va, vb,
):
    own, rows, _ = o_ref.shape
    pairs = v_ref.shape[0]
    odd = odd_ref[0]
    tall = 3 * SUB
    count = 2 * tall // SUB

    def fill(at, ends, ref, *index):
        band[at, 0:SUB] = ends[0]
        band[at, SUB:tall] = ref[(*index, slice(0, 2 * SUB))]
        band[at, tall : tall + 2 * SUB] = ref[(*index, slice(rows - 2 * SUB, rows))]
        band[at, tall + 2 * SUB : 2 * tall] = ends[1]

    def received(f):
        return beyond(odd, ra_ref[f], rb_ref[f])

    def fill_pair(p, carry):
        fill(p, received(own + p), v_ref, p)
        return carry

    lax.fori_loop(0, pairs, fill_pair, 0, unroll=4)
    o_at, p_at = pairs, pairs + own
    m_at = p_at + own
    for k in range(own):
        fill(o_at + k, received(k), o_ref, k)
        fill(p_at + k, beyond(odd, p2_ref[k], p2_ref[own + k]), p_ref, k)
    fill(m_at, received(own + pairs), m_ref)
    for n in range(5):
        fill(m_at + 1 + n, received(own + pairs + 1 + n), c_ref, n)

    masks = lane_masks(odd_ref[1])
    metric = spread(band, count, m_at)
    raw = [spread(band, count, m_at + 1 + n) for n in range(5)]
    for t in range(count):
        scale = jnp.where(masks[2], 0.0, scaled_coefs([raw[n][t] for n in range(5)]))
        ms[t] = scale * metric[t]
        for n in range(5):
            cf[n, t] = scale * raw[n][t]

    def group(g, carry):
        chosen = [by_ref[g * BANDS + k] for k in range(BANDS)]
        for k, p in enumerate(chosen):
            o, q = spread(band, count, o_at + p // own), spread(band, count, p_at + p % own)
            v = spread(band, count, p)
            for t in range(count):
                sr[k, t] = ms[t] * (o[t] * q[t])
                va[k, t] = v[t]
        relax([n_ref[p] for p in chosen], count, va, vb, sr, cf, masks)
        for k, p in enumerate(chosen):
            spread_store(band, [va[k, t] for t in range(count)], p)
            out_ref[p, 0] = band[p, SUB : 2 * SUB]
            out_ref[p, 1] = band[p, tall + SUB : tall + 2 * SUB]
        return carry

    lax.fori_loop(0, pairs // BANDS, group, 0)


def bands(odd, counts, order, potentials, orbitals, partner, metric, coefficients, *received):
    own, rows, lanes = orbitals.shape
    pairs = potentials.shape[0]
    count = 6
    some = pltpu.VMEM((BANDS, count, SUB, lanes), jnp.float32)
    return pl.pallas_call(
        bands_kernel,
        out_shape=f32(pairs, 2, SUB, lanes),
        in_specs=[SMEM] * 3 + [VMEM] * 8,
        out_specs=VMEM,
        scratch_shapes=[
            pltpu.VMEM((pairs + 2 * own + 6, count * SUB, lanes), jnp.float32),
            pltpu.VMEM((5, count, SUB, lanes), jnp.float32),
            pltpu.VMEM((count, SUB, lanes), jnp.float32),
            some,
            some,
            some,
        ],
        compiler_params=params(),
        name="bands",
    )(odd, counts, order, potentials, orbitals, partner, metric, coefficients, *received)


def finish_kernel(sides, odd_ref, n_ref, inner_ref, ends_ref, o_ref, p_ref, e_ref, *refs):
    recv = refs[:sides]
    v_ref, home_ref, back_ref = refs[sides : sides + 3]
    st, cf, ms, sr, va, vb, sv, full, sems = refs[sides + 3 :]
    own, rows, _ = o_ref.shape
    groups, tall, _ = e_ref.shape
    count = tall // SUB
    lane = lane_of()
    block = lane // STRIP

    for side in range(sides):
        left_own = odd_ref[1] == side
        within = lane_of(tall) % STRIP
        from_own = jnp.where(left_own, within, STRIP - 1 - within) < STRIP // 2
        for g in range(groups):
            st[g] = jnp.where(from_own, e_ref[g], recv[side][g])
        first_group, second_group = spread(st, count, own + 1), spread(st, count, own + 2)
        for t in range(count):
            cs = [replicated(first_group[t], 1 + n) for n in range(3)]
            cs += [replicated(second_group[t], n) for n in range(2)]
            scale = scaled_coefs(cs)
            ms[t] = scale * replicated(first_group[t], 0)
            for n in range(5):
                cf[n, t] = scale * cs[n]
        o, q = spread(st, count, 0), spread(st, count, groups - 1)
        for t in range(count):
            weighted = ms[t] * q[t]
            for g in range(own):
                sr[g, t] = replicated(o[t], g) * weighted
        steps = []
        for g in range(own):
            for t, value in enumerate(spread(st, count, 1 + g)):
                va[g, t] = value
            n = jnp.zeros((SUB, LANES), jnp.int32)
            for k in range(own):
                n = jnp.where(block == k, n_ref[g * own + k], n)
            steps.append(n)

        def body(turn, carry):
            for s in range(2):
                keep = [n > 2 * turn + s for n in steps]
                sweep(own, count, (va, vb)[s], (vb, va)[s], sr, cf, keep=keep)
            return carry

        lax.fori_loop(0, SWEEPS // 2, body, 0)
        for g in range(own):
            spread_store(sv, [va[g, t] for t in range(count)], side * own + g)

    def merge(r, carry):
        at = pl.multiple_of(r * SUB, SUB)
        o = [o_ref[k, pl.ds(at, SUB)] for k in range(own)]
        q = [p_ref[k, pl.ds(at, SUB)] for k in range(own)]
        home, back = [0.0] * own, [0.0] * own
        for first in range(own):
            strips = [sv[side * own + first, pl.ds(at + SUB, SUB)] for side in range(sides)]
            for second in range(own):
                p = first * own + second
                value = inner_ref[p, pl.ds(at, SUB)]
                value = jnp.where(r == 0, ends_ref[p, 0], value)
                value = jnp.where(r == rows // SUB - 1, ends_ref[p, 1], value)
                for side in range(sides):
                    right = odd_ref[1] == side
                    edge = jnp.where(right, LANES - 1 - lane, lane) < HALO
                    turned = pltpu.roll(
                        strips[side], (-(STRIP * second + STRIP // 2)) % LANES, 1
                    )
                    value = jnp.where(edge, turned, value)
                full[p, pl.ds(at, SUB)] = value
                home[first] = home[first] + value * q[second]
                back[second] = back[second] + value * o[first]
        for k in range(own):
            home_ref[k, pl.ds(at, SUB)] = o[k] - step_size * home[k]
            back_ref[k, pl.ds(at, SUB)] = back[k]
        copy_out(r).start()
        return carry

    def copy_out(r):
        at = pl.multiple_of(r * SUB, SUB)
        return pltpu.make_async_copy(
            full.at[:, pl.ds(at, SUB), :], v_ref.at[:, pl.ds(at, SUB), :], sems.at[r]
        )

    lax.fori_loop(0, rows // SUB, merge, 0)

    def finished(r, carry):
        copy_out(r).wait()
        return carry

    lax.fori_loop(0, rows // SUB, finished, 0)


def finish(odd, counts, inner, ends, orbitals, partner, edges, received):
    own, rows, lanes = orbitals.shape
    sides = len(received)
    groups, tall, _ = edges.shape
    count = tall // SUB
    strips = pltpu.VMEM((own, count, SUB, lanes), jnp.float32)
    return pl.pallas_call(
        functools.partial(finish_kernel, sides),
        out_shape=(f32(*inner.shape), f32(*orbitals.shape), f32(*orbitals.shape)),
        in_specs=[SMEM] * 2 + [VMEM] * (5 + sides),
        out_specs=(ANY, VMEM, VMEM),
        scratch_shapes=[
            pltpu.VMEM((groups, tall, lanes), jnp.float32),
            pltpu.VMEM((5, count, SUB, lanes), jnp.float32),
            pltpu.VMEM((count, SUB, lanes), jnp.float32),
            strips,
            strips,
            strips,
            pltpu.VMEM((sides * own, tall, lanes), jnp.float32),
            pltpu.VMEM(inner.shape, jnp.float32),
            pltpu.SemaphoreType.DMA((rows // SUB,)),
        ],
        compiler_params=params(),
        name="finish",
    )(odd, counts, inner, ends, orbitals, partner, edges, *received)


def norm_kernel(home_ref, recv_ref, m_ref, upd_ref, norm_ref):
    own = home_ref.shape[0]
    norm_ref[...] = jnp.zeros_like(norm_ref)
    for k in range(own):
        updated = home_ref[k] - step_size * recv_ref[k]
        upd_ref[k] = updated
        weighted = m_ref[...] * updated * updated
        norm_ref[k : k + 1] = jnp.sum(weighted, axis=0, keepdims=True)


def partial_norms(home, received, metric):
    own, _, lanes = home.shape
    return pl.pallas_call(
        norm_kernel,
        out_shape=(f32(*home.shape), f32(-(-own // SUB) * SUB, lanes)),
        in_specs=[VMEM] * 3,
        out_specs=(VMEM, VMEM),
        compiler_params=params(),
        name="partial_norms",
    )(home, received, metric)


def scale_kernel(cells, upd_ref, norm_ref, other_ref, out_ref):
    for k in range(upd_ref.shape[0]):
        total = norm_ref[k : k + 1] + other_ref[k : k + 1]
        norm = jnp.sum(total, axis=1, keepdims=True)
        out_ref[k] = upd_ref[k] * jnp.sqrt(cells / norm)


def rescaled(updated, norms, others, cells):
    return pl.pallas_call(
        functools.partial(scale_kernel, float(cells)),
        out_shape=f32(*updated.shape),
        in_specs=[VMEM] * 3,
        out_specs=VMEM,
        compiler_params=params(),
        name="rescaled",
    )(updated, norms, others)


def shifted(value, axis, by):
    size = lax.axis_size(axis)
    return lax.ppermute(value, axis, [(i, (i + by) % size) for i in range(size)])


def pair_swaps(size):
    even = [(i, i + 1) for i in range(0, size - 1, 2)]
    odd = [(i, i + 1) for i in range(1, size - 1, 2)]
    return [p + [(b, a) for a, b in p] for p in (even, odd)]


def by_count(counts):
    at = jnp.arange(counts.shape[0], dtype=jnp.int32)
    more = counts[None] > counts[:, None]
    tie = (counts[None] == counts[:, None]) & (at[None] < at[:, None])
    rank = jnp.sum((more | tie).astype(jnp.int32), axis=1)
    return jnp.sum(jnp.where(rank[None] == at[:, None], at[None], 0), axis=1)


def local(orbitals, potentials, coefficients, metric, sweep_counts):
    own, rows, lanes = orbitals.shape
    gx, gy = lax.axis_size("gx"), lax.axis_size("gy")
    odd = jnp.stack([lax.axis_index("gx") % 2, lax.axis_index("gy") % 2]).astype(jnp.int32)
    order = by_count(sweep_counts)
    col_swaps = [p for p in pair_swaps(gy) if p]
    row_swaps = pair_swaps(gx)
    half = potentials.shape[0] // GROUP // 2

    partner = shifted(orbitals, "orb", 1)
    pay_a, pay_b = row_payloads(odd, orbitals, potentials, metric, coefficients)
    rows_a = lax.ppermute(pay_a, "gx", row_swaps[0])
    ready = prepare(odd, potentials, orbitals, metric, coefficients)
    pay_b, ready = lax.optimization_barrier((pay_b, ready))
    rows_b = lax.ppermute(pay_b, "gx", row_swaps[1])
    inner = interior(half, 0, odd, sweep_counts, order, ready, partner)
    beside = jnp.concatenate([rows_a[:own], rows_b[:own]], 0)
    beside, inner = lax.optimization_barrier((beside, inner))
    partner_rows = shifted(beside, "orb", 1)
    inner = interior(half, half, odd, sweep_counts, order, ready, partner, inner)
    partner_rows, inner = lax.optimization_barrier((partner_rows, inner))
    edges = tall_edges(odd, ready[3], rows_a, rows_b, partner_rows, partner)
    received = [lax.ppermute(edges, "gy", swap) for swap in col_swaps]
    ends = bands(
        odd, sweep_counts, order, potentials, orbitals, partner, metric, coefficients,
        rows_a, rows_b, partner_rows,
    )
    fields, home, back = finish(
        odd, sweep_counts, inner, ends, orbitals, partner, edges, received
    )
    updated, norms = partial_norms(home, shifted(back, "orb", -1), metric)
    hops = [("gy", 1 << k) for k in range(gy.bit_length() - 1)]
    hops += [("gx", 1 << k) for k in range(gx.bit_length() - 1)]
    for at, (axis, by) in enumerate(hops):
        size = lax.axis_size(axis)
        other = lax.ppermute(norms, axis, [(i, i ^ by) for i in range(size)])
        if at < len(hops) - 1:
            norms = norms + other
    return (rescaled(updated, norms, other, rows * lanes * gx * gy), fields)


def solution(mesh):
    return jax.shard_map(
        local,
        mesh=mesh,
        in_specs=(
            P("orb", "gx", "gy"),
            P("orb", "gx", "gy"),
            P(None, "gx", "gy"),
            P("gx", "gy"),
            P("orb"),
        ),
        out_specs=(P("orb", "gx", "gy"), P("orb", "gx", "gy")),
        check_vma=False,
    )
```

time: 108 us -> 54.4 us (0.50)
  other arithmetic: 40.9 us -> 0.39 us
  local copies, waits for them, and re-layouts: 26 us -> 4.41 us
  Pallas kernels: 0 us -> 19.1 us
  blocking collectives: 15.4 us -> 0 us
  starting transfers between devices: 12.8 us -> 17.5 us
    select_n x16 -> x0, other arithmetic: 35.6 us -> none  [the longest x8 32.8 us: relaxed_sweep(): result = jnp.where(inside[None], result, 0.0)]
    pallas_call x0 -> x9, Pallas kernels: none -> 19.1 us  [the longest x2 7.38 us: interior(): pl.pallas_call(functools.partial(interior_kernel, groups, before), out_sh...]
    psum x1 -> x0, blocking collectives: 15.4 us -> none  [local(): norm_sums = lax.psum(local_norms, ('gx', 'gy'))]
    slice x13 -> x2, local copies, waits for them, and re-layouts: 14 us -> 0.01 us  [local(): beside = jnp.concatenate([rows_a[:own], rows_b[:own]], 0)]
    ppermute x3 -> x0, local copies, waits for them, and re-layouts: 6.14 us -> none  [the longest x1 3.02 us: with_halo(): lax.ppermute(lax.slice_in_dim(block, block.shape[dim] - width, None, axis...]
    concatenate x2 -> x1, other arithmetic: 4.22 us -> 0.01 us  [local(): beside = jnp.concatenate([rows_a[:own], rows_b[:own]], 0)]
    ppermute x4 -> x6, starting transfers between devices: 8.25 us -> 12.1 us  [the longest x3 9.76 us: local(): other = lax.ppermute(norms, axis, [(i, i ^ by) for i in range(size)])]
    mul x9 -> x0, local copies, waits for them, and re-layouts: 2.5 us -> none  [the longest x8 2.49 us: relaxed_sweep(): coefs[0] * padded[:, :-2, 1:-1] + coefs[1] * padded[:, 2:, 1:-1]]
  transfers between devices with their start and end apart: 6 -> 9, of which waited for: 4 -> 5; matrix products, arithmetic and copies ran while one was open for 14% -> 1% of each run, Pallas kernels for 0% -> 16%
where the time goes in v2:
time: 54.4 us; the launch traced here: 54.5 us
  Pallas kernels  19.1 us (35%)
  starting transfers between devices  17.5 us (32%)
  waiting for transfers between devices  12.4 us (23%)
  local copies, waits for them, and re-layouts  4.41 us (8%)
  between operations  0.78 us (1%)
    ppermute x3, starting transfers between devices, local(): other = lax.ppermute(norms, axis, [(i, i ^ by) for i in range(size)])  9.76 us
    ppermute x3, waiting for transfers between devices, shifted(): lax.ppermute(value, axis, [(i, (i + by) % size) for i in range(size)])  7.55 us
    pallas_call x2, Pallas kernels, interior(): pl.pallas_call(functools.partial(interior_kernel, groups, before), out_sh...  7.38 us
    ppermute x3, starting transfers between devices, shifted(): lax.ppermute(value, axis, [(i, (i + by) % size) for i in range(size)])  5.34 us
    pallas_call x1, Pallas kernels, finish(): pl.pallas_call(functools.partial(finish_kernel, sides), out_shape=(f32(*i...  4.98 us
    unnamed x16, local copies, waits for them, and re-layouts  4.41 us
    ppermute x3, waiting for transfers between devices, local(): other = lax.ppermute(norms, axis, [(i, i ^ by) for i in range(size)])  4.32 us
    pallas_call x1, Pallas kernels, bands(): pl.pallas_call(bands_kernel, out_shape=f32(pairs, 2, SUB, lanes), in_spec...  2.83 us
  transfers between devices with their start and end apart: 9, of which 5 were waited for; matrix products, arithmetic and copies ran while one was open for 1% of the time, Pallas kernels for 16%

profile of v2, /device:TPU:0, one launch (start us, length us, event | category | flops | bytes accessed | tf_op | source)
XLA Modules:
  0.0 54.5 jit_solution(2668280768463294365)
XLA Ops:
  0.6 3.0 %collective-permute-start.2 = (f32[4,128,128]{2,1,0:T(8,128)}, f32[4,128,128]{2,1,0:T(8,128)S(1)}, u32[]{:S(2)}, u32[]{:S(2)}) collective-permute-start(f32[4,128,128]{2,1,0:T(8,128)} %o_ref.7), channel_id=1, source_target_pairs={{0,8},{8,16},{16,24},{24,0},{1,9},{9,17},{17,25},{25,1},{2,10},{10... | collective-permute-start | bytes 786440 | tf_op jit(solution)/shard_map/ppermute | solution.py:553
  3.6 0.1 pad_add_fusion.par_ref.odd_ref
  3.7 1.2 %copy-done = f32[16,128,128]{2,1,0:T(8,128)S(1)} copy-done((f32[16,128,128]{2,1,0:T(8,128)S(1)}, f32[16,128,128]{2,1,0:T(8,128)}, u32[]{:S(2)}) %copy-start) | copy-done | bytes 1048600
  4.9 0.9 %copy-done.2 = f32[4,128,128]{2,1,0:T(8,128)S(1)} copy-done((f32[4,128,128]{2,1,0:T(8,128)S(1)}, f32[4,128,128]{2,1,0:T(8,128)}, u32[]{:S(2)}) %copy-start.2) | copy-done | bytes 262168
  5.9 1.0 %copy-done.4 = f32[5,128,128]{2,1,0:T(8,128)S(1)} copy-done((f32[5,128,128]{2,1,0:T(8,128)S(1)}, f32[5,128,128]{2,1,0:T(8,128)}, u32[]{:S(2)}) %copy-start.4) | copy-done | bytes 327704
  6.8 0.8 %copy-done.6 = f32[128,128]{1,0:T(8,128)S(1)} copy-done((f32[128,128]{1,0:T(8,128)S(1)}, f32[128,128]{1,0:T(8,128)}, u32[]{:S(2)}) %copy-start.6) | copy-done | bytes 65560
  7.7 0.7 %row_payloads.1 = (f32[26,8,128]{2,1,0:T(8,128)S(1)}, f32[26,8,128]{2,1,0:T(8,128)S(1)}) custom-call(s32[2]{0:T(128)S(1)} %pad_add_fusion.par_ref.odd_ref, f32[4,128,128]{2,1,0:T(8,128)S(1)} %copy-done.2, f32[16,128,128]{2,1,0:T(8,128)S(1)} %copy-done, f32[1,128,128]{2,1,0:T(8,128)S(1)} %bitcast.3, f32[5,128,128]{2,1,0:T(8,128)S(1)} %copy-done.4), custom_call_target="tpu_custom_call" | custom-call | tf_op jit(solution)/shard_map/row_payloads/pallas_call | solution.py:217
  8.4 1.6 %collective-permute-start = (f32[26,8,128]{2,1,0:T(8,128)S(1)}, f32[26,8,128]{2,1,0:T(8,128)S(1)}, u32[]{:S(2)}, u32[]{:S(2)}) collective-permute-start(f32[26,8,128]{2,1,0:T(8,128)S(1)} %get-tuple-element.22), channel_id=1, source_target_pairs={{0,2},{4,6},{2,0},{6,4},{1,3},{5,7},{3,1},{7,5},{8,10},{12,14},{10... | collective-permute-start | bytes 319496 | tf_op jit(solution)/shard_map/ppermute | solution.py:581
  10.0 1.6 %prepare.1 = (f32[16,16,8,128]{3,2,1,0:T(8,128)S(1)}, f32[4,16,8,128]{3,2,1,0:T(8,128)S(1)}, f32[5,16,8,128]{3,2,1,0:T(8,128)S(1)}, f32[7,128,128]{2,1,0:T(8,128)S(1)}) custom-call(s32[2]{0:T(128)S(1)} %pad_add_fusion.par_ref.odd_ref, f32[16,128,128]{2,1,0:T(8,128)S(1)} %copy-done, f32[4,128,128]{2,1,0:T(8,128)S(1)} %copy-done.2, f32[128,128]{1,0:T(8,128)S(1)} %copy-done.6, ...), custom_call_target="tpu_custom_call" | custom-call | tf_op jit(solution)/shard_map/prepare/pallas_call | solution.py:180
  11.6 0.7 %collective-permute-start.1 = (f32[26,8,128]{2,1,0:T(8,128)S(1)}, f32[26,8,128]{2,1,0:T(8,128)S(1)}, u32[]{:S(2)}, u32[]{:S(2)}) collective-permute-start(f32[26,8,128]{2,1,0:T(8,128)S(1)} %get-tuple-element.28), channel_id=1, source_target_pairs={{2,4},{4,2},{3,5},{5,3},{10,12},{12,10},{11,13},{13,11},{18,20},{2... | collective-permute-start | bytes 319496 | tf_op jit(solution)/shard_map/ppermute | solution.py:584
  12.3 0.2 convert_reduce_fusion
  12.5 0.1 select_reduce_fusion.by_ref
  12.6 0.5 collective-permute-done.ra_ref
  13.2 3.9 %interior0.1.refs_0_ = f32[16,128,128]{2,1,0:T(8,128)S(1)} custom-call(s32[2]{0:T(128)S(1)} %pad_add_fusion.par_ref.odd_ref, s32[16]{0:T(128)S(1)} %copy-done.7, s32[16]{0:T(128)S(1)} %select_reduce_fusion.by_ref, f32[16,16,8,128]{3,2,1,0:T(8,128)S(1)} %get-tuple-element.29.vs_ref, f32[4,16,8,128]{3,2,1,0:T(8,128)S(1)} %get-tuple-element.30.om_ref, ...), custom_call_target="tpu_custom_call" | custom-call | tf_op jit(solution)/shard_map/interior0/pallas_call | solution.py:264
  17.0 1.5 %collective-permute-start.3 = (f32[8,8,128]{2,1,0:T(8,128)S(1)}, f32[8,8,128]{2,1,0:T(8,128)S(1)}, u32[]{:S(2)}, u32[]{:S(2)}) collective-permute-start(f32[8,8,128]{2,1,0:T(8,128)S(1)} %pad_maximum_fusion), channel_id=1, source_target_pairs={{0,8},{8,16},{16,24},{24,0},{1,9},{9,17},{17,25},{25,1},{2,10},{10... | collective-permute-start | bytes 98312 | tf_op jit(solution)/shard_map/ppermute | solution.py:553
  18.6 3.5 %interior2.1.inner_ref = f32[16,128,128]{2,1,0:T(8,128)S(1)} custom-call(s32[2]{0:T(128)S(1)} %pad_add_fusion.par_ref.odd_ref, s32[16]{0:T(128)S(1)} %copy-done.7, s32[16]{0:T(128)S(1)} %select_reduce_fusion.by_ref, f32[16,16,8,128]{3,2,1,0:T(8,128)S(1)} %get-tuple-element.29.vs_ref, f32[4,16,8,128]{3,2,1,0:T(8,128)S(1)} %get-tuple-element.30.om_ref, ...), custom_call_target="tpu_custom_call" | custom-call | tf_op jit(solution)/shard_map/interior2/pallas_call | solution.py:264
  22.2 0.7 %tall_edges.1.e_ref = f32[8,144,128]{2,1,0:T(8,128)S(1)} custom-call(s32[2]{0:T(128)S(1)} %pad_add_fusion.par_ref.odd_ref, f32[7,128,128]{2,1,0:T(8,128)S(1)} %get-tuple-element.36.e_ref, f32[26,8,128]{2,1,0:T(8,128)S(1)} %collective-permute-done.ra_ref, f32[26,8,128]{2,1,0:T(8,128)S(1)} %collective-permute-done.1.rb_ref, ...), custom_call_target="tpu_custom_call" | custom-call | tf_op jit(solution)/shard_map/tall_edges/pallas_call | solution.py:300
  22.9 0.1 collective-permute-start.4
  23.0 0.4 copy-done.1
  23.4 0.0 copy-done.3
  23.4 2.8 %bands.1.ends_ref = f32[16,2,8,128]{3,2,1,0:T(8,128)S(1)} custom-call(s32[2]{0:T(128)S(1)} %pad_add_fusion.par_ref.odd_ref, s32[16]{0:T(128)S(1)} %copy-done.7, s32[16]{0:T(128)S(1)} %select_reduce_fusion.by_ref, f32[16,128,128]{2,1,0:T(8,128)S(1)} %copy-done.1, f32[4,128,128]{2,1,0:T(8,128)S(1)} %copy-done.3, ...), custom_call_target="tpu_custom_call" | custom-call | tf_op jit(solution)/shard_map/bands/pallas_call | solution.py:375
  26.2 5.0 %finish.1 = (f32[16,128,128]{2,1,0:T(8,128)}, f32[4,128,128]{2,1,0:T(8,128)S(1)}, f32[4,128,128]{2,1,0:T(8,128)S(1)}) custom-call(s32[2]{0:T(128)S(1)} %pad_add_fusion.par_ref.odd_ref, s32[16]{0:T(128)S(1)} %copy-done.7, f32[16,128,128]{2,1,0:T(8,128)S(1)} %interior2.1.inner_ref, f32[16,2,8,128]{3,2,1,0:T(8,128)S(1)} %bands.1.ends_ref, ...), custom_call_target="tpu_custom_call" | custom-call | tf_op jit(solution)/shard_map/finish/pallas_call | solution.py:490
  31.2 0.8 %collective-permute-start.5 = (f32[4,128,128]{2,1,0:T(8,128)S(1)}, f32[4,128,128]{2,1,0:T(8,128)S(1)}, u32[]{:S(2)}, u32[]{:S(2)}) collective-permute-start(f32[4,128,128]{2,1,0:T(8,128)S(1)} %get-tuple-element.38), channel_id=1, source_target_pairs={{0,24},{8,0},{16,8},{24,16},{1,25},{9,1},{17,9},{25,17},{2,26},{10... | collective-permute-start | bytes 786440 | tf_op jit(solution)/shard_map/ppermute | solution.py:553
  32.0 7.5 %collective-permute-done.5.recv_ref = f32[4,128,128]{2,1,0:T(8,128)S(1)} collective-permute-done((f32[4,128,128]{2,1,0:T(8,128)S(1)}, f32[4,128,128]{2,1,0:T(8,128)S(1)}, u32[]{:S(2)}, u32[]{:S(2)}) %collective-permute-start.5) | collective-permute-done | bytes 262176 | tf_op jit(solution)/shard_map/ppermute | solution.py:553
  39.6 0.1 partial_norms.1
  39.6 0.1 collective-permute-start.6
  39.7 1.2 %collective-permute-done.6 = f32[8,128]{1,0:T(8,128)S(1)} collective-permute-done((f32[8,128]{1,0:T(8,128)S(1)}, f32[8,128]{1,0:T(8,128)S(1)}, u32[]{:S(2)}, u32[]{:S(2)}) %collective-permute-start.6) | collective-permute-done | bytes 4128 | tf_op jit(solution)/shard_map/ppermute | solution.py:605
  40.9 6.2 %collective-permute-start.7 = (f32[8,128]{1,0:T(8,128)S(1)}, f32[8,128]{1,0:T(8,128)S(1)}, u32[]{:S(2)}, u32[]{:S(2)}) collective-permute-start(f32[8,128]{1,0:T(8,128)S(1)} %add.15), channel_id=1, source_target_pairs={{0,2},{2,0},{4,6},{6,4},{1,3},{3,1},{5,7},{7,5},{8,10},{10,8},{12,... | collective-permute-start | bytes 12296 | tf_op jit(solution)/shard_map/ppermute | solution.py:605
  47.1 1.6 %collective-permute-done.7 = f32[8,128]{1,0:T(8,128)S(1)} collective-permute-done((f32[8,128]{1,0:T(8,128)S(1)}, f32[8,128]{1,0:T(8,128)S(1)}, u32[]{:S(2)}, u32[]{:S(2)}) %collective-permute-start.7) | collective-permute-done | bytes 4128 | tf_op jit(solution)/shard_map/ppermute | solution.py:605
  48.7 3.5 %collective-permute-start.8 = (f32[8,128]{1,0:T(8,128)S(1)}, f32[8,128]{1,0:T(8,128)S(1)}, u32[]{:S(2)}, u32[]{:S(2)}) collective-permute-start(f32[8,128]{1,0:T(8,128)S(1)} %add.16.norm_ref), channel_id=1, source_target_pairs={{0,4},{2,6},{4,0},{6,2},{1,5},{3,7},{5,1},{7,3},{8,12},{10,14},{12... | collective-permute-start | bytes 12296 | tf_op jit(solution)/shard_map/ppermute | solution.py:605
  52.1 1.6 %collective-permute-done.8.other_ref = f32[8,128]{1,0:T(8,128)S(1)} collective-permute-done((f32[8,128]{1,0:T(8,128)S(1)}, f32[8,128]{1,0:T(8,128)S(1)}, u32[]{:S(2)}, u32[]{:S(2)}) %collective-permute-start.8) | collective-permute-done | bytes 4128 | tf_op jit(solution)/shard_map/ppermute | solution.py:605
  53.7 0.8 %rescaled.1 = f32[4,128,128]{2,1,0:T(8,128)} custom-call(f32[4,128,128]{2,1,0:T(8,128)S(1)} %get-tuple-element.39.upd_ref, f32[8,128]{1,0:T(8,128)S(1)} %add.16.norm_ref, f32[8,128]{1,0:T(8,128)S(1)} %collective-permute-done.8.other_ref), custom_call_target="tpu_custom_call" | custom-call | tf_op jit(solution)/shard_map/rescaled/pallas_call | solution.py:541
  (19 shorter events, 0.1 us)
Async XLA Ops:
  0.6 12.5 %collective-permute-start.2 = (f32[4,128,128]{2,1,0:T(8,128)}, f32[4,128,128]{2,1,0:T(8,128)S(1)}, u32[]{:S(2)}, u32[]{:S(2)}) collective-permute-start(f32[4,128,128]{2,1,0:T(8,128)} %o_ref.7), channel_id=1, source_target_pairs={{0,8},{8,16},{16,24},{24,0},{1,9},{9,17},{17,25},{25,1},{2,10},{10... | collective-permute-start | bytes 786440 | tf_op jit(solution)/shard_map/ppermute | solution.py:553
  3.7 1.2 %copy-start = (f32[16,128,128]{2,1,0:T(8,128)S(1)}, f32[16,128,128]{2,1,0:T(8,128)}, u32[]{:S(2)}) copy-start(f32[16,128,128]{2,1,0:T(8,128)} %v_ref.5) | copy-start | bytes 3145732
  4.9 0.9 %copy-start.2 = (f32[4,128,128]{2,1,0:T(8,128)S(1)}, f32[4,128,128]{2,1,0:T(8,128)}, u32[]{:S(2)}) copy-start(f32[4,128,128]{2,1,0:T(8,128)} %o_ref.7) | copy-start | bytes 786436
  5.9 1.0 %copy-start.4 = (f32[5,128,128]{2,1,0:T(8,128)S(1)}, f32[5,128,128]{2,1,0:T(8,128)}, u32[]{:S(2)}) copy-start(f32[5,128,128]{2,1,0:T(8,128)} %c_ref.5) | copy-start | bytes 983044
  6.8 0.8 %copy-start.6 = (f32[128,128]{1,0:T(8,128)S(1)}, f32[128,128]{1,0:T(8,128)}, u32[]{:S(2)}) copy-start(f32[128,128]{1,0:T(8,128)} %m_ref.5) | copy-start | bytes 196612
  8.4 4.8 %collective-permute-start = (f32[26,8,128]{2,1,0:T(8,128)S(1)}, f32[26,8,128]{2,1,0:T(8,128)S(1)}, u32[]{:S(2)}, u32[]{:S(2)}) collective-permute-start(f32[26,8,128]{2,1,0:T(8,128)S(1)} %get-tuple-element.22), channel_id=1, source_target_pairs={{0,2},{4,6},{2,0},{6,4},{1,3},{5,7},{3,1},{7,5},{8,10},{12,14},{10... | collective-permute-start | bytes 319496 | tf_op jit(solution)/shard_map/ppermute | solution.py:581
  11.6 0.7 %copy-start.7 = (s32[16]{0:T(128)S(1)}, s32[16]{0:T(128)}, u32[]{:S(2)}) copy-start(s32[16]{0:T(128)} %n_ref.7) | copy-start | bytes 196
  11.6 1.5 %collective-permute-start.1 = (f32[26,8,128]{2,1,0:T(8,128)S(1)}, f32[26,8,128]{2,1,0:T(8,128)S(1)}, u32[]{:S(2)}, u32[]{:S(2)}) collective-permute-start(f32[26,8,128]{2,1,0:T(8,128)S(1)} %get-tuple-element.28), channel_id=1, source_target_pairs={{2,4},{4,2},{3,5},{5,3},{10,12},{12,10},{11,13},{13,11},{18,20},{2... | collective-permute-start | bytes 319496 | tf_op jit(solution)/shard_map/ppermute | solution.py:584
  17.0 5.1 %collective-permute-start.3 = (f32[8,8,128]{2,1,0:T(8,128)S(1)}, f32[8,8,128]{2,1,0:T(8,128)S(1)}, u32[]{:S(2)}, u32[]{:S(2)}) collective-permute-start(f32[8,8,128]{2,1,0:T(8,128)S(1)} %pad_maximum_fusion), channel_id=1, source_target_pairs={{0,8},{8,16},{16,24},{24,0},{1,9},{9,17},{17,25},{25,1},{2,10},{10... | collective-permute-start | bytes 98312 | tf_op jit(solution)/shard_map/ppermute | solution.py:553
  18.6 4.4 %copy-start.5 = (f32[5,128,128]{2,1,0:T(8,128)S(1)}, f32[5,128,128]{2,1,0:T(8,128)}, u32[]{:S(2)}) copy-start(f32[5,128,128]{2,1,0:T(8,128)} %c_ref.5) | copy-start | bytes 983044
  22.1 1.2 %copy-start.1 = (f32[16,128,128]{2,1,0:T(8,128)S(1)}, f32[16,128,128]{2,1,0:T(8,128)}, u32[]{:S(2)}) copy-start(f32[16,128,128]{2,1,0:T(8,128)} %v_ref.5) | copy-start | bytes 3145732
  22.1 1.3 %copy-start.3 = (f32[4,128,128]{2,1,0:T(8,128)S(1)}, f32[4,128,128]{2,1,0:T(8,128)}, u32[]{:S(2)}) copy-start(f32[4,128,128]{2,1,0:T(8,128)} %o_ref.7) | copy-start | bytes 786436
  22.9 3.3 %collective-permute-start.4 = (f32[8,144,128]{2,1,0:T(8,128)S(1)}, f32[8,144,128]{2,1,0:T(8,128)S(1)}, u32[]{:S(2)}, u32[]{:S(2)}) collective-permute-start(f32[8,144,128]{2,1,0:T(8,128)S(1)} %tall_edges.1.e_ref), channel_id=1, source_target_pairs={{0,1},{1,0},{2,3},{3,2},{4,5},{5,4},{6,7},{7,6},{8,9},{9,8},{10,11... | collective-permute-start | bytes 1769480 | tf_op jit(solution)/shard_map/ppermute | solution.py:592
  31.2 8.4 %collective-permute-start.5 = (f32[4,128,128]{2,1,0:T(8,128)S(1)}, f32[4,128,128]{2,1,0:T(8,128)S(1)}, u32[]{:S(2)}, u32[]{:S(2)}) collective-permute-start(f32[4,128,128]{2,1,0:T(8,128)S(1)} %get-tuple-element.38), channel_id=1, source_target_pairs={{0,24},{8,0},{16,8},{24,16},{1,25},{9,1},{17,9},{25,17},{2,26},{10... | collective-permute-start | bytes 786440 | tf_op jit(solution)/shard_map/ppermute | solution.py:553
  39.6 1.2 %collective-permute-start.6 = (f32[8,128]{1,0:T(8,128)S(1)}, f32[8,128]{1,0:T(8,128)S(1)}, u32[]{:S(2)}, u32[]{:S(2)}) collective-permute-start(f32[8,128]{1,0:T(8,128)S(1)} %get-tuple-element.40), channel_id=1, source_target_pairs={{0,1},{1,0},{2,3},{3,2},{4,5},{5,4},{6,7},{7,6},{8,9},{9,8},{10,11... | collective-permute-start | bytes 12296 | tf_op jit(solution)/shard_map/ppermute | solution.py:605
  40.9 7.8 %collective-permute-start.7 = (f32[8,128]{1,0:T(8,128)S(1)}, f32[8,128]{1,0:T(8,128)S(1)}, u32[]{:S(2)}, u32[]{:S(2)}) collective-permute-start(f32[8,128]{1,0:T(8,128)S(1)} %add.15), channel_id=1, source_target_pairs={{0,2},{2,0},{4,6},{6,4},{1,3},{3,1},{5,7},{7,5},{8,10},{10,8},{12,... | collective-permute-start | bytes 12296 | tf_op jit(solution)/shard_map/ppermute | solution.py:605
  48.7 5.1 %collective-permute-start.8 = (f32[8,128]{1,0:T(8,128)S(1)}, f32[8,128]{1,0:T(8,128)S(1)}, u32[]{:S(2)}, u32[]{:S(2)}) collective-permute-start(f32[8,128]{1,0:T(8,128)S(1)} %add.16.norm_ref), channel_id=1, source_target_pairs={{0,4},{2,6},{4,0},{6,2},{1,5},{3,7},{5,1},{7,3},{8,12},{10,14},{12... | collective-permute-start | bytes 12296 | tf_op jit(solution)/shard_map/ppermute | solution.py:605

commit v3 on v2

--- a/solution.py
+++ b/solution.py
@@ -26,6 +26,7 @@
 VMEM = pl.BlockSpec(memory_space=pltpu.VMEM)
 SMEM = pl.BlockSpec(memory_space=pltpu.SMEM)
 ANY = pl.BlockSpec(memory_space=pl.ANY)
+HBM = pl.BlockSpec(memory_space=pltpu.HBM)
 
 
 def f32(*shape):
@@ -217,7 +218,7 @@
     return pl.pallas_call(
         rows_kernel,
         out_shape=(f32(fields, HALO, lanes),) * 2,
-        in_specs=[SMEM] + [ANY] * 4,
+        in_specs=[SMEM] + [HBM] * 4,
         out_specs=(ANY, ANY),
         scratch_shapes=[pltpu.SemaphoreType.DMA((8,))],
         compiler_params=params(),
@@ -272,21 +273,21 @@
     )(odd, counts, order, spread_v, weighted, coefs, partner, *earlier)
 
 
-def beyond(odd, a, b):
-    low_is_a = odd == 1
+def beyond(odd_ref, a, b):
+    low_is_a = odd_ref[0] == 1
+    b = jnp.where(odd_ref[2] == 1, b, 0.0)
     return jnp.where(low_is_a, a, b), jnp.where(low_is_a, b, a)
 
 
 def edges_kernel(odd_ref, e_ref, ra_ref, rb_ref, p2_ref, p_ref, out_ref):
     own, rows, _ = p_ref.shape
-    odd = odd_ref[0]
     groups = e_ref.shape[0]
     for g in range(groups):
         out_ref[g, SUB : SUB + rows] = e_ref[g]
     out_ref[groups, SUB : SUB + rows] = packed([p_ref[k] for k in range(own)])
     pairs = own * own
-    ends = [beyond(odd, ra_ref[f], rb_ref[f]) for f in range(own + pairs + 6)]
-    ends += [beyond(odd, p2_ref[k], p2_ref[own + k]) for k in range(own)]
+    ends = [beyond(odd_ref, ra_ref[f], rb_ref[f]) for f in range(own + pairs + 6)]
+    ends += [beyond(odd_ref, p2_ref[k], p2_ref[own + k]) for k in range(own)]
     lists = [range(own)] + [range(own * (1 + k), own * (2 + k)) for k in range(own)]
     at = own + pairs
     lists += [range(at, at + 4), range(at + 4, at + 6), range(at + 6, at + 6 + own)]
@@ -313,7 +314,6 @@
 ):
     own, rows, _ = o_ref.shape
     pairs = v_ref.shape[0]
-    odd = odd_ref[0]
     tall = 3 * SUB
     count = 2 * tall // SUB
 
@@ -324,7 +324,7 @@
         band[at, tall + 2 * SUB : 2 * tall] = ends[1]
 
     def received(f):
-        return beyond(odd, ra_ref[f], rb_ref[f])
+        return beyond(odd_ref, ra_ref[f], rb_ref[f])
 
     def fill_pair(p, carry):
         fill(p, received(own + p), v_ref, p)
@@ -335,7 +335,7 @@
     m_at = p_at + own
     for k in range(own):
         fill(o_at + k, received(k), o_ref, k)
-        fill(p_at + k, beyond(odd, p2_ref[k], p2_ref[own + k]), p_ref, k)
+        fill(p_at + k, beyond(odd_ref, p2_ref[k], p2_ref[own + k]), p_ref, k)
     fill(m_at, received(own + pairs), m_ref)
     for n in range(5):
         fill(m_at + 1 + n, received(own + pairs + 1 + n), c_ref, n)
@@ -472,7 +472,7 @@
             full.at[:, pl.ds(at, SUB), :], v_ref.at[:, pl.ds(at, SUB), :], sems.at[r]
         )
 
-    lax.fori_loop(0, rows // SUB, merge, 0)
+    lax.fori_loop(0, rows // SUB, merge, 0, unroll=4)
 
     def finished(r, carry):
         copy_out(r).wait()
@@ -559,6 +559,22 @@
     return [p + [(b, a) for a, b in p] for p in (even, odd)]
 
 
+def row_swap(swap, gx, gy):
+    to = dict(swap)
+    pairs = []
+    for i in range(gx):
+        for j in range(gy):
+            pairs.append((i * gy + j, to[i] * gy + j if i in to else i * gy + (j ^ 1)))
+    return pairs
+
+
+def norm_hops(gx, gy):
+    hops = [[(i, i ^ (1 << k)) for i in range(gx * gy)] for k in range(gy.bit_length() - 1)]
+    for k in range(gx.bit_length() - 1):
+        hops.append([(i, i ^ (gy << k) ^ 1) for i in range(gx * gy)])
+    return hops
+
+
 def by_count(counts):
     at = jnp.arange(counts.shape[0], dtype=jnp.int32)
     more = counts[None] > counts[:, None]
@@ -570,21 +586,23 @@
 def local(orbitals, potentials, coefficients, metric, sweep_counts):
     own, rows, lanes = orbitals.shape
     gx, gy = lax.axis_size("gx"), lax.axis_size("gy")
-    odd = jnp.stack([lax.axis_index("gx") % 2, lax.axis_index("gy") % 2]).astype(jnp.int32)
+    row_at = lax.axis_index("gx")
+    inside = (row_at > 0) & (row_at < gx - 1)
+    odd = jnp.stack([row_at % 2, lax.axis_index("gy") % 2, inside]).astype(jnp.int32)
     order = by_count(sweep_counts)
     col_swaps = [p for p in pair_swaps(gy) if p]
-    row_swaps = pair_swaps(gx)
+    row_swaps = [row_swap(p, gx, gy) for p in pair_swaps(gx)]
     half = potentials.shape[0] // GROUP // 2
 
     partner = shifted(orbitals, "orb", 1)
     pay_a, pay_b = row_payloads(odd, orbitals, potentials, metric, coefficients)
-    rows_a = lax.ppermute(pay_a, "gx", row_swaps[0])
+    rows_a = lax.ppermute(pay_a, ("gx", "gy"), row_swaps[0])
     ready = prepare(odd, potentials, orbitals, metric, coefficients)
     pay_b, ready = lax.optimization_barrier((pay_b, ready))
-    rows_b = lax.ppermute(pay_b, "gx", row_swaps[1])
+    rows_b = lax.ppermute(pay_b, ("gx", "gy"), row_swaps[1])
     inner = interior(half, 0, odd, sweep_counts, order, ready, partner)
+    rows_a, rows_b, inner = lax.optimization_barrier((rows_a, rows_b, inner))
     beside = jnp.concatenate([rows_a[:own], rows_b[:own]], 0)
-    beside, inner = lax.optimization_barrier((beside, inner))
     partner_rows = shifted(beside, "orb", 1)
     inner = interior(half, half, odd, sweep_counts, order, ready, partner, inner)
     partner_rows, inner = lax.optimization_barrier((partner_rows, inner))
@@ -598,11 +616,9 @@
         odd, sweep_counts, inner, ends, orbitals, partner, edges, received
     )
     updated, norms = partial_norms(home, shifted(back, "orb", -1), metric)
-    hops = [("gy", 1 << k) for k in range(gy.bit_length() - 1)]
-    hops += [("gx", 1 << k) for k in range(gx.bit_length() - 1)]
-    for at, (axis, by) in enumerate(hops):
-        size = lax.axis_size(axis)
-        other = lax.ppermute(norms, axis, [(i, i ^ by) for i in range(size)])
+    hops = norm_hops(gx, gy)
+    for at, hop in enumerate(hops):
+        other = lax.ppermute(norms, ("gx", "gy"), hop)
         if at < len(hops) - 1:
             norms = norms + other
     return (rescaled(updated, norms, other, rows * lanes * gx * gy), fields)

time: 54.4 us -> 46.8 us (0.86)
  starting transfers between devices: 17.5 us -> 12.2 us
  Pallas kernels: 19.1 us -> 17.1 us
  local copies, waits for them, and re-layouts: 4.41 us -> 3.75 us
    ppermute x5, starting transfers between devices: 12.1 us -> 5.85 us  [the longest x3 4.14 us: local(): other = lax.ppermute(norms, ('gx', 'gy'), hop)]
    ppermute x3, starting transfers between devices: 5.34 us -> 6.25 us  [shifted(): lax.ppermute(value, axis, [(i, (i + by) % size) for i in range(size)])]
    pallas_call x1, Pallas kernels: 4.98 us -> 4.11 us  [finish(): pl.pallas_call(functools.partial(finish_kernel, sides), out_shape=(f32(*i...]
    pallas_call x2, Pallas kernels: 7.38 us -> 6.58 us  [interior(): pl.pallas_call(functools.partial(interior_kernel, groups, before), out_sh...]
    unnamed x16, local copies, waits for them, and re-layouts: 4.41 us -> 3.74 us
  transfers between devices with their start and end apart: 9 -> 9, of which waited for: 5 -> 5; matrix products, arithmetic and copies ran while one was open for 1% -> 1% of each run, Pallas kernels for 16% -> 25%
where the time goes in v3:
time: 46.8 us; the launch traced here: 46.6 us
  Pallas kernels  17.1 us (37%)
  waiting for transfers between devices  12.3 us (26%)
  starting transfers between devices  12.2 us (26%)
  local copies, waits for them, and re-layouts  3.75 us (8%)
  between operations  0.81 us (2%)
    ppermute x3, waiting for transfers between devices, shifted(): lax.ppermute(value, axis, [(i, (i + by) % size) for i in range(size)])  7.59 us
    pallas_call x2, Pallas kernels, interior(): pl.pallas_call(functools.partial(interior_kernel, groups, before), out_sh...  6.58 us
    ppermute x3, starting transfers between devices, shifted(): lax.ppermute(value, axis, [(i, (i + by) % size) for i in range(size)])  6.25 us
    ppermute x3, waiting for transfers between devices, local(): other = lax.ppermute(norms, ('gx', 'gy'), hop)  4.69 us
    ppermute x3, starting transfers between devices, local(): other = lax.ppermute(norms, ('gx', 'gy'), hop)  4.14 us
    pallas_call x1, Pallas kernels, finish(): pl.pallas_call(functools.partial(finish_kernel, sides), out_shape=(f32(*i...  4.11 us
    unnamed x16, local copies, waits for them, and re-layouts  3.74 us
    pallas_call x1, Pallas kernels, bands(): pl.pallas_call(bands_kernel, out_shape=f32(pairs, 2, SUB, lanes), in_spec...  2.56 us
  transfers between devices with their start and end apart: 9, of which 5 were waited for; matrix products, arithmetic and copies ran while one was open for 1% of the time, Pallas kernels for 25%

profile of v3, /device:TPU:0, one launch (start us, length us, event | category | flops | bytes accessed | tf_op | source)
XLA Modules:
  0.0 46.6 jit_solution(10137058110468337564)
XLA Ops:
  0.6 3.0 %collective-permute-start.2 = (f32[4,128,128]{2,1,0:T(8,128)}, f32[4,128,128]{2,1,0:T(8,128)S(1)}, u32[]{:S(2)}, u32[]{:S(2)}) collective-permute-start(f32[4,128,128]{2,1,0:T(8,128)} %o_ref.7), channel_id=1, source_target_pairs={{0,8},{8,16},{16,24},{24,0},{1,9},{9,17},{17,25},{25,1},{2,10},{10... | collective-permute-start | bytes 786440 | tf_op jit(solution)/shard_map/ppermute | solution.py:553
  3.6 0.1 pad_add_fusion.par_ref.odd_ref
  3.7 1.2 %copy-done = f32[16,128,128]{2,1,0:T(8,128)S(1)} copy-done((f32[16,128,128]{2,1,0:T(8,128)S(1)}, f32[16,128,128]{2,1,0:T(8,128)}, u32[]{:S(2)}) %copy-start) | copy-done | bytes 1048600
  4.9 0.9 %copy-done.2 = f32[4,128,128]{2,1,0:T(8,128)S(1)} copy-done((f32[4,128,128]{2,1,0:T(8,128)S(1)}, f32[4,128,128]{2,1,0:T(8,128)}, u32[]{:S(2)}) %copy-start.2) | copy-done | bytes 262168
  5.9 1.0 %copy-done.4 = f32[5,128,128]{2,1,0:T(8,128)S(1)} copy-done((f32[5,128,128]{2,1,0:T(8,128)S(1)}, f32[5,128,128]{2,1,0:T(8,128)}, u32[]{:S(2)}) %copy-start.4) | copy-done | bytes 327704
  6.9 0.7 %row_payloads.1 = (f32[26,8,128]{2,1,0:T(8,128)S(1)}, f32[26,8,128]{2,1,0:T(8,128)S(1)}) custom-call(s32[3]{0:T(128)S(1)} %pad_add_fusion.par_ref.odd_ref, f32[4,128,128]{2,1,0:T(8,128)S(1)} %copy-done.2, f32[16,128,128]{2,1,0:T(8,128)S(1)} %copy-done, f32[1,128,128]{2,1,0:T(8,128)S(1)} %bitcast.4, f32[5,128,128]{2,1,0:T(8,128)S(1)} %copy-done.4), custom_call_target="tpu_custom_call" | custom-call | tf_op jit(solution)/shard_map/row_payloads/pallas_call | solution.py:218
  7.6 1.6 %collective-permute-start = (f32[26,8,128]{2,1,0:T(8,128)S(1)}, f32[26,8,128]{2,1,0:T(8,128)S(1)}, u32[]{:S(2)}, u32[]{:S(2)}) collective-permute-start(f32[26,8,128]{2,1,0:T(8,128)S(1)} %get-tuple-element.23), channel_id=1, source_target_pairs={{0,2},{1,3},{2,0},{3,1},{4,6},{5,7},{6,4},{7,5},{8,10},{9,11},{10,... | collective-permute-start | bytes 319496 | tf_op jit(solution)/shard_map/ppermute | solution.py:599
  9.2 1.6 %prepare.1 = (f32[16,16,8,128]{3,2,1,0:T(8,128)S(1)}, f32[4,16,8,128]{3,2,1,0:T(8,128)S(1)}, f32[5,16,8,128]{3,2,1,0:T(8,128)S(1)}, f32[7,128,128]{2,1,0:T(8,128)S(1)}) custom-call(s32[3]{0:T(128)S(1)} %pad_add_fusion.par_ref.odd_ref, f32[16,128,128]{2,1,0:T(8,128)S(1)} %copy-done, f32[4,128,128]{2,1,0:T(8,128)S(1)} %copy-done.2, f32[128,128]{1,0:T(8,128)S(1)} %copy-done.6, ...), custom_call_target="tpu_custom_call" | custom-call | tf_op jit(solution)/shard_map/prepare/pallas_call | solution.py:181
  10.8 0.0 copy-start.7
  10.8 0.1 collective-permute-start.1
  10.9 0.6 %copy-done.7 = s32[16]{0:T(128)S(1)} copy-done((s32[16]{0:T(128)S(1)}, s32[16]{0:T(128)}, u32[]{:S(2)}) %copy-start.7) | copy-done | bytes 88
  11.5 0.2 convert_reduce_fusion
  11.7 0.1 select_reduce_fusion.by_ref
  11.8 3.9 %interior0.1.refs_0_ = f32[16,128,128]{2,1,0:T(8,128)S(1)} custom-call(s32[3]{0:T(128)S(1)} %pad_add_fusion.par_ref.odd_ref, s32[16]{0:T(128)S(1)} %copy-done.7, s32[16]{0:T(128)S(1)} %select_reduce_fusion.by_ref, f32[16,16,8,128]{3,2,1,0:T(8,128)S(1)} %get-tuple-element.30.vs_ref, f32[4,16,8,128]{3,2,1,0:T(8,128)S(1)} %get-tuple-element.31.om_ref, ...), custom_call_target="tpu_custom_call" | custom-call | tf_op jit(solution)/shard_map/interior0/pallas_call | solution.py:265
  15.7 1.5 %collective-permute-start.3 = (f32[8,8,128]{2,1,0:T(8,128)S(1)}, f32[8,8,128]{2,1,0:T(8,128)S(1)}, u32[]{:S(2)}, u32[]{:S(2)}) collective-permute-start(f32[8,8,128]{2,1,0:T(8,128)S(1)} %pad_maximum_fusion), channel_id=1, source_target_pairs={{0,8},{8,16},{16,24},{24,0},{1,9},{9,17},{17,25},{25,1},{2,10},{10... | collective-permute-start | bytes 98312 | tf_op jit(solution)/shard_map/ppermute | solution.py:553
  17.2 2.7 %interior2.1.inner_ref = f32[16,128,128]{2,1,0:T(8,128)S(1)} custom-call(s32[3]{0:T(128)S(1)} %pad_add_fusion.par_ref.odd_ref, s32[16]{0:T(128)S(1)} %copy-done.7, s32[16]{0:T(128)S(1)} %select_reduce_fusion.by_ref, f32[16,16,8,128]{3,2,1,0:T(8,128)S(1)} %get-tuple-element.30.vs_ref, f32[4,16,8,128]{3,2,1,0:T(8,128)S(1)} %get-tuple-element.31.om_ref, ...), custom_call_target="tpu_custom_call" | custom-call | tf_op jit(solution)/shard_map/interior2/pallas_call | solution.py:265
  20.0 0.0 copy-start.1
  20.0 0.6 %collective-permute-done.3.p2_ref = f32[8,8,128]{2,1,0:T(8,128)S(1)} collective-permute-done((f32[8,8,128]{2,1,0:T(8,128)S(1)}, f32[8,8,128]{2,1,0:T(8,128)S(1)}, u32[]{:S(2)}, u32[]{:S(2)}) %collective-permute-start.3) | collective-permute-done | bytes 32800 | tf_op jit(solution)/shard_map/ppermute | solution.py:553
  20.6 0.7 %tall_edges.1.e_ref = f32[8,144,128]{2,1,0:T(8,128)S(1)} custom-call(s32[3]{0:T(128)S(1)} %pad_add_fusion.par_ref.odd_ref, f32[7,128,128]{2,1,0:T(8,128)S(1)} %get-tuple-element.38.e_ref, f32[26,8,128]{2,1,0:T(8,128)S(1)} %collective-permute-done.ra_ref, f32[26,8,128]{2,1,0:T(8,128)S(1)} %collective-permute-done.1.rb_ref, ...), custom_call_target="tpu_custom_call" | custom-call | tf_op jit(solution)/shard_map/tall_edges/pallas_call | solution.py:301
  21.3 0.1 collective-permute-start.4
  21.4 2.6 %bands.1.ends_ref = f32[16,2,8,128]{3,2,1,0:T(8,128)S(1)} custom-call(s32[3]{0:T(128)S(1)} %pad_add_fusion.par_ref.odd_ref, s32[16]{0:T(128)S(1)} %copy-done.7, s32[16]{0:T(128)S(1)} %select_reduce_fusion.by_ref, f32[16,128,128]{2,1,0:T(8,128)S(1)} %copy-done.1, f32[4,128,128]{2,1,0:T(8,128)S(1)} %copy-done.3, ...), custom_call_target="tpu_custom_call" | custom-call | tf_op jit(solution)/shard_map/bands/pallas_call | solution.py:375
  24.0 4.1 %finish.1 = (f32[16,128,128]{2,1,0:T(8,128)}, f32[4,128,128]{2,1,0:T(8,128)S(1)}, f32[4,128,128]{2,1,0:T(8,128)S(1)}) custom-call(s32[3]{0:T(128)S(1)} %pad_add_fusion.par_ref.odd_ref, s32[16]{0:T(128)S(1)} %copy-done.7, f32[16,128,128]{2,1,0:T(8,128)S(1)} %interior2.1.inner_ref, f32[16,2,8,128]{3,2,1,0:T(8,128)S(1)} %bands.1.ends_ref, ...), custom_call_target="tpu_custom_call" | custom-call | tf_op jit(solution)/shard_map/finish/pallas_call | solution.py:490
  28.1 1.7 %collective-permute-start.5 = (f32[4,128,128]{2,1,0:T(8,128)S(1)}, f32[4,128,128]{2,1,0:T(8,128)S(1)}, u32[]{:S(2)}, u32[]{:S(2)}) collective-permute-start(f32[4,128,128]{2,1,0:T(8,128)S(1)} %get-tuple-element.40), channel_id=1, source_target_pairs={{0,24},{8,0},{16,8},{24,16},{1,25},{9,1},{17,9},{25,17},{2,26},{10... | collective-permute-start | bytes 786440 | tf_op jit(solution)/shard_map/ppermute | solution.py:553
  29.8 7.0 %collective-permute-done.5.recv_ref = f32[4,128,128]{2,1,0:T(8,128)S(1)} collective-permute-done((f32[4,128,128]{2,1,0:T(8,128)S(1)}, f32[4,128,128]{2,1,0:T(8,128)S(1)}, u32[]{:S(2)}, u32[]{:S(2)}) %collective-permute-start.5) | collective-permute-done | bytes 262176 | tf_op jit(solution)/shard_map/ppermute | solution.py:553
  36.8 0.1 partial_norms.1
  36.9 0.1 collective-permute-start.6
  37.0 1.2 %collective-permute-done.6 = f32[8,128]{1,0:T(8,128)S(1)} collective-permute-done((f32[8,128]{1,0:T(8,128)S(1)}, f32[8,128]{1,0:T(8,128)S(1)}, u32[]{:S(2)}, u32[]{:S(2)}) %collective-permute-start.6) | collective-permute-done | bytes 4128 | tf_op jit(solution)/shard_map/ppermute | solution.py:621
  38.1 2.4 %collective-permute-start.7 = (f32[8,128]{1,0:T(8,128)S(1)}, f32[8,128]{1,0:T(8,128)S(1)}, u32[]{:S(2)}, u32[]{:S(2)}) collective-permute-start(f32[8,128]{1,0:T(8,128)S(1)} %add.15), channel_id=1, source_target_pairs={{0,3},{1,2},{2,1},{3,0},{4,7},{5,6},{6,5},{7,4},{8,11},{9,10},{10,... | collective-permute-start | bytes 12296 | tf_op jit(solution)/shard_map/ppermute | solution.py:621
  40.5 1.3 %collective-permute-done.7 = f32[8,128]{1,0:T(8,128)S(1)} collective-permute-done((f32[8,128]{1,0:T(8,128)S(1)}, f32[8,128]{1,0:T(8,128)S(1)}, u32[]{:S(2)}, u32[]{:S(2)}) %collective-permute-start.7) | collective-permute-done | bytes 4128 | tf_op jit(solution)/shard_map/ppermute | solution.py:621
  41.8 1.7 %collective-permute-start.8 = (f32[8,128]{1,0:T(8,128)S(1)}, f32[8,128]{1,0:T(8,128)S(1)}, u32[]{:S(2)}, u32[]{:S(2)}) collective-permute-start(f32[8,128]{1,0:T(8,128)S(1)} %add.16.norm_ref), channel_id=1, source_target_pairs={{0,5},{1,4},{2,7},{3,6},{4,1},{5,0},{6,3},{7,2},{8,13},{9,12},{10,... | collective-permute-start | bytes 12296 | tf_op jit(solution)/shard_map/ppermute | solution.py:621
  43.5 2.2 %collective-permute-done.8.other_ref = f32[8,128]{1,0:T(8,128)S(1)} collective-permute-done((f32[8,128]{1,0:T(8,128)S(1)}, f32[8,128]{1,0:T(8,128)S(1)}, u32[]{:S(2)}, u32[]{:S(2)}) %collective-permute-start.8) | collective-permute-done | bytes 4128 | tf_op jit(solution)/shard_map/ppermute | solution.py:621
  45.7 0.8 %rescaled.1 = f32[4,128,128]{2,1,0:T(8,128)} custom-call(f32[4,128,128]{2,1,0:T(8,128)S(1)} %get-tuple-element.41.upd_ref, f32[8,128]{1,0:T(8,128)S(1)} %add.16.norm_ref, f32[8,128]{1,0:T(8,128)S(1)} %collective-permute-done.8.other_ref), custom_call_target="tpu_custom_call" | custom-call | tf_op jit(solution)/shard_map/rescaled/pallas_call | solution.py:541
  (19 shorter events, 0.0 us)
Async XLA Ops:
  0.6 3.1 %copy-start.6 = (f32[128,128]{1,0:T(8,128)S(1)}, f32[128,128]{1,0:T(8,128)}, u32[]{:S(2)}) copy-start(f32[128,128]{1,0:T(8,128)} %m_ref.5) | copy-start | bytes 196612
  0.6 11.1 %collective-permute-start.2 = (f32[4,128,128]{2,1,0:T(8,128)}, f32[4,128,128]{2,1,0:T(8,128)S(1)}, u32[]{:S(2)}, u32[]{:S(2)}) collective-permute-start(f32[4,128,128]{2,1,0:T(8,128)} %o_ref.7), channel_id=1, source_target_pairs={{0,8},{8,16},{16,24},{24,0},{1,9},{9,17},{17,25},{25,1},{2,10},{10... | collective-permute-start | bytes 786440 | tf_op jit(solution)/shard_map/ppermute | solution.py:553
  3.7 1.2 %copy-start = (f32[16,128,128]{2,1,0:T(8,128)S(1)}, f32[16,128,128]{2,1,0:T(8,128)}, u32[]{:S(2)}) copy-start(f32[16,128,128]{2,1,0:T(8,128)} %v_ref.5) | copy-start | bytes 3145732
  4.9 0.9 %copy-start.2 = (f32[4,128,128]{2,1,0:T(8,128)S(1)}, f32[4,128,128]{2,1,0:T(8,128)}, u32[]{:S(2)}) copy-start(f32[4,128,128]{2,1,0:T(8,128)} %o_ref.7) | copy-start | bytes 786436
  5.9 1.0 %copy-start.4 = (f32[5,128,128]{2,1,0:T(8,128)S(1)}, f32[5,128,128]{2,1,0:T(8,128)}, u32[]{:S(2)}) copy-start(f32[5,128,128]{2,1,0:T(8,128)} %c_ref.5) | copy-start | bytes 983044
  7.6 8.1 %collective-permute-start = (f32[26,8,128]{2,1,0:T(8,128)S(1)}, f32[26,8,128]{2,1,0:T(8,128)S(1)}, u32[]{:S(2)}, u32[]{:S(2)}) collective-permute-start(f32[26,8,128]{2,1,0:T(8,128)S(1)} %get-tuple-element.23), channel_id=1, source_target_pairs={{0,2},{1,3},{2,0},{3,1},{4,6},{5,7},{6,4},{7,5},{8,10},{9,11},{10,... | collective-permute-start | bytes 319496 | tf_op jit(solution)/shard_map/ppermute | solution.py:599
  10.8 0.7 %copy-start.7 = (s32[16]{0:T(128)S(1)}, s32[16]{0:T(128)}, u32[]{:S(2)}) copy-start(s32[16]{0:T(128)} %n_ref.7) | copy-start | bytes 196
  10.8 4.8 %collective-permute-start.1 = (f32[26,8,128]{2,1,0:T(8,128)S(1)}, f32[26,8,128]{2,1,0:T(8,128)S(1)}, u32[]{:S(2)}, u32[]{:S(2)}) collective-permute-start(f32[26,8,128]{2,1,0:T(8,128)S(1)} %get-tuple-element.29), channel_id=1, source_target_pairs={{0,1},{1,0},{2,4},{3,5},{4,2},{5,3},{6,7},{7,6},{8,9},{9,8},{10,12... | collective-permute-start | bytes 319496 | tf_op jit(solution)/shard_map/ppermute | solution.py:602
  15.7 4.9 %collective-permute-start.3 = (f32[8,8,128]{2,1,0:T(8,128)S(1)}, f32[8,8,128]{2,1,0:T(8,128)S(1)}, u32[]{:S(2)}, u32[]{:S(2)}) collective-permute-start(f32[8,8,128]{2,1,0:T(8,128)S(1)} %pad_maximum_fusion), channel_id=1, source_target_pairs={{0,8},{8,16},{16,24},{24,0},{1,9},{9,17},{17,25},{25,1},{2,10},{10... | collective-permute-start | bytes 98312 | tf_op jit(solution)/shard_map/ppermute | solution.py:553
  17.2 4.1 %copy-start.5 = (f32[5,128,128]{2,1,0:T(8,128)S(1)}, f32[5,128,128]{2,1,0:T(8,128)}, u32[]{:S(2)}) copy-start(f32[5,128,128]{2,1,0:T(8,128)} %c_ref.5) | copy-start | bytes 983044
  20.0 1.4 %copy-start.1 = (f32[16,128,128]{2,1,0:T(8,128)S(1)}, f32[16,128,128]{2,1,0:T(8,128)}, u32[]{:S(2)}) copy-start(f32[16,128,128]{2,1,0:T(8,128)} %v_ref.5) | copy-start | bytes 3145732
  20.0 1.4 %copy-start.3 = (f32[4,128,128]{2,1,0:T(8,128)S(1)}, f32[4,128,128]{2,1,0:T(8,128)}, u32[]{:S(2)}) copy-start(f32[4,128,128]{2,1,0:T(8,128)} %o_ref.7) | copy-start | bytes 786436
  21.3 2.7 %collective-permute-start.4 = (f32[8,144,128]{2,1,0:T(8,128)S(1)}, f32[8,144,128]{2,1,0:T(8,128)S(1)}, u32[]{:S(2)}, u32[]{:S(2)}) collective-permute-start(f32[8,144,128]{2,1,0:T(8,128)S(1)} %tall_edges.1.e_ref), channel_id=1, source_target_pairs={{0,1},{1,0},{2,3},{3,2},{4,5},{5,4},{6,7},{7,6},{8,9},{9,8},{10,11... | collective-permute-start | bytes 1769480 | tf_op jit(solution)/shard_map/ppermute | solution.py:610
  28.1 8.7 %collective-permute-start.5 = (f32[4,128,128]{2,1,0:T(8,128)S(1)}, f32[4,128,128]{2,1,0:T(8,128)S(1)}, u32[]{:S(2)}, u32[]{:S(2)}) collective-permute-start(f32[4,128,128]{2,1,0:T(8,128)S(1)} %get-tuple-element.40), channel_id=1, source_target_pairs={{0,24},{8,0},{16,8},{24,16},{1,25},{9,1},{17,9},{25,17},{2,26},{10... | collective-permute-start | bytes 786440 | tf_op jit(solution)/shard_map/ppermute | solution.py:553
  36.9 1.2 %collective-permute-start.6 = (f32[8,128]{1,0:T(8,128)S(1)}, f32[8,128]{1,0:T(8,128)S(1)}, u32[]{:S(2)}, u32[]{:S(2)}) collective-permute-start(f32[8,128]{1,0:T(8,128)S(1)} %get-tuple-element.42), channel_id=1, source_target_pairs={{0,1},{1,0},{2,3},{3,2},{4,5},{5,4},{6,7},{7,6},{8,9},{9,8},{10,11... | collective-permute-start | bytes 12296 | tf_op jit(solution)/shard_map/ppermute | solution.py:621
  38.1 3.7 %collective-permute-start.7 = (f32[8,128]{1,0:T(8,128)S(1)}, f32[8,128]{1,0:T(8,128)S(1)}, u32[]{:S(2)}, u32[]{:S(2)}) collective-permute-start(f32[8,128]{1,0:T(8,128)S(1)} %add.15), channel_id=1, source_target_pairs={{0,3},{1,2},{2,1},{3,0},{4,7},{5,6},{6,5},{7,4},{8,11},{9,10},{10,... | collective-permute-start | bytes 12296 | tf_op jit(solution)/shard_map/ppermute | solution.py:621
  41.8 3.9 %collective-permute-start.8 = (f32[8,128]{1,0:T(8,128)S(1)}, f32[8,128]{1,0:T(8,128)S(1)}, u32[]{:S(2)}, u32[]{:S(2)}) collective-permute-start(f32[8,128]{1,0:T(8,128)S(1)} %add.16.norm_ref), channel_id=1, source_target_pairs={{0,5},{1,4},{2,7},{3,6},{4,1},{5,0},{6,3},{7,2},{8,13},{9,12},{10,... | collective-permute-start | bytes 12296 | tf_op jit(solution)/shard_map/ppermute | solution.py:621

commit v4 on v3

--- a/solution.py
+++ b/solution.py
@@ -17,6 +17,7 @@
 SUB = 8
 HALO = 8
 STRIP = 32
+BLOCKS = LANES // STRIP
 LEAST = 4
 GROUP = 4
 BANDS = 8
@@ -146,12 +147,21 @@
     return west, east, dead
 
 
-def prepare_kernel(odd_ref, v_ref, o_ref, m_ref, c_ref, vs_ref, om_ref, cf_ref, e_ref):
+def prepare_kernel(odd_ref, v_hbm, o_hbm, m_hbm, c_hbm, *refs):
+    vs_ref, os_ref, om_ref, cf_ref, e_ref, v_ref, o_ref, m_ref, c_ref, sems = refs
     own, rows, _ = o_ref.shape
     count = rows // SUB
-    e_ref[0] = packed([o_ref[k] for k in range(own)])
+    copies = [
+        pltpu.make_async_copy(source, target, sems.at[at])
+        for at, (source, target) in enumerate(((m_hbm, m_ref), (c_hbm, c_ref), (o_hbm, o_ref)))
+    ]
     for first in range(own):
-        e_ref[1 + first] = packed([v_ref[first * own + k] for k in range(own)])
+        part = pl.ds(first * own, own)
+        copies.append(pltpu.make_async_copy(v_hbm.at[part], v_ref.at[part], sems.at[3 + first]))
+    for copy in copies:
+        copy.start()
+    copies[0].wait()
+    copies[1].wait()
     e_ref[1 + own] = packed([m_ref[...], c_ref[0], c_ref[1], c_ref[2]])
     e_ref[2 + own] = packed([c_ref[3], c_ref[4]])
     dead = lane_masks(odd_ref[1])[2]
@@ -163,34 +173,40 @@
         weights.append(scale * metric[t])
         for n in range(5):
             cf_ref[n, t] = scale * raw[n][t]
+    copies[2].wait()
+    e_ref[0] = packed([o_ref[k] for k in range(own)])
     for k in range(own):
         for t, value in enumerate(spread(o_ref, count, k)):
+            os_ref[k, t] = value
             om_ref[k, t] = weights[t] * value
-
-    def one(p, carry):
-        for t, value in enumerate(spread(v_ref, count, p)):
-            vs_ref[p, t] = value
-        return carry
-
-    lax.fori_loop(0, v_ref.shape[0], one, 0)
+    for first in range(own):
+        copies[3 + first].wait()
+        e_ref[1 + first] = packed([v_ref[first * own + k] for k in range(own)])
+        for k in range(own):
+            for t, value in enumerate(spread(v_ref, count, first * own + k)):
+                vs_ref[first * own + k, t] = value
 
 
 def prepare(odd, potentials, orbitals, metric, coefficients):
     own, rows, lanes = orbitals.shape
     count = rows // SUB
+    arrays = (potentials, orbitals, metric, coefficients)
     return pl.pallas_call(
         prepare_kernel,
         out_shape=(
             f32(potentials.shape[0], count, SUB, lanes),
             f32(own, count, SUB, lanes),
+            f32(own, count, SUB, lanes),
             f32(5, count, SUB, lanes),
             f32(own + 3, rows, lanes),
         ),
-        in_specs=[SMEM] + [VMEM] * 4,
-        out_specs=(VMEM,) * 4,
+        in_specs=[SMEM] + [HBM] * 4,
+        out_specs=(VMEM,) * 5,
+        scratch_shapes=[pltpu.VMEM(a.shape, jnp.float32) for a in arrays]
+        + [pltpu.SemaphoreType.DMA((3 + own,))],
         compiler_params=params(),
         name="prepare",
-    )(odd, potentials, orbitals, metric, coefficients)
+    )(odd, *arrays)
 
 
 def rows_kernel(par_ref, o_ref, v_ref, m_ref, c_ref, pay_a, pay_b, sems):
@@ -226,18 +242,22 @@
     )(odd, orbitals, potentials, metric[None], coefficients)
 
 
-def interior_kernel(groups, before, odd_ref, n_ref, by_ref, vs_ref, om_ref, cf_ref, p_ref, *refs):
-    out_ref, qs, sr, va, vb = refs[-5:]
+def interior_kernel(groups, before, last, odd_ref, n_ref, by_ref, *refs):
+    vs_ref, os_ref, om_ref, cf_ref, p_ref = refs[:5]
+    out_ref, back_ref, back, qs, sr, va, vb = refs[-7:]
     own, count = om_ref.shape[:2]
     masks = lane_masks(odd_ref[1])
     if before:
-        earlier = refs[0]
+        earlier, back_before = refs[5:7]
 
         def keep(k, carry):
             out_ref[by_ref[k]] = earlier[by_ref[k]]
             return carry
 
         lax.fori_loop(0, before * GROUP, keep, 0)
+        back[...] = back_before[...]
+    else:
+        back[...] = jnp.zeros_like(back)
     for k in range(own):
         for t, value in enumerate(spread(p_ref, count, k)):
             qs[k, t] = value
@@ -251,26 +271,35 @@
                 va[k, t] = vs_ref[p, t]
         relax([n_ref[p] for p in pairs], count, va, vb, sr, cf_ref, masks)
         for k, p in enumerate(pairs):
+            first, second = p // own, p % own
             spread_store(out_ref, [va[k, t] for t in range(count)], p)
+            for t in range(count):
+                back[second, t] = back[second, t] + va[k, t] * os_ref[first, t]
         return carry
 
     lax.fori_loop(before, before + groups, group, 0)
-
-
-def interior(groups, before, odd, counts, order, ready, partner, *earlier):
-    spread_v, weighted, coefs, _ = ready
-    pairs, count, _, lanes = spread_v.shape
+    for k in range(own):
+        if last:
+            spread_store(back_ref, [back[k, t] for t in range(count)], k)
+        else:
+            back_ref[k] = back[k]
+
+
+def interior(groups, before, last, odd, counts, order, ready, partner, *earlier):
+    pairs, count, _, lanes = ready[0].shape
     own, rows, _ = partner.shape
     four = pltpu.VMEM((GROUP, count, SUB, lanes), jnp.float32)
-    return pl.pallas_call(
-        functools.partial(interior_kernel, groups, before),
-        out_shape=f32(pairs, rows, lanes),
-        in_specs=[SMEM] * 3 + [VMEM] * (4 + len(earlier)),
-        out_specs=VMEM,
-        scratch_shapes=[pltpu.VMEM((own, count, SUB, lanes), jnp.float32), four, four, four],
+    each = pltpu.VMEM((own, count, SUB, lanes), jnp.float32)
+    back = f32(own, rows, lanes) if last else f32(own, count, SUB, lanes)
+    return pl.pallas_call(
+        functools.partial(interior_kernel, groups, before, last),
+        out_shape=(f32(pairs, rows, lanes), back),
+        in_specs=[SMEM] * 3 + [VMEM] * (5 + len(earlier)),
+        out_specs=(VMEM, VMEM),
+        scratch_shapes=[each, each, four, four, four],
         compiler_params=params(),
         name=f"interior{before}",
-    )(odd, counts, order, spread_v, weighted, coefs, partner, *earlier)
+    )(odd, counts, order, *ready[:4], partner, *earlier)
 
 
 def beyond(odd_ref, a, b):
@@ -310,7 +339,7 @@
 
 def bands_kernel(
     odd_ref, n_ref, by_ref, v_ref, o_ref, p_ref, m_ref, c_ref, ra_ref, rb_ref, p2_ref,
-    out_ref, band, cf, ms, sr, va, vb,
+    out_ref, back_ref, band, cf, ms, sr, va, vb,
 ):
     own, rows, _ = o_ref.shape
     pairs = v_ref.shape[0]
@@ -365,6 +394,11 @@
         return carry
 
     lax.fori_loop(0, pairs // BANDS, group, 0)
+    for end, start in enumerate((0, rows - SUB)):
+        o = [o_ref[k, start : start + SUB] for k in range(own)]
+        for second in range(own):
+            terms = [out_ref[first * own + second, end] * o[first] for first in range(own)]
+            back_ref[end * own + second] = sum(terms[1:], terms[0])
 
 
 def bands(odd, counts, order, potentials, orbitals, partner, metric, coefficients, *received):
@@ -374,9 +408,9 @@
     some = pltpu.VMEM((BANDS, count, SUB, lanes), jnp.float32)
     return pl.pallas_call(
         bands_kernel,
-        out_shape=f32(pairs, 2, SUB, lanes),
+        out_shape=(f32(pairs, 2, SUB, lanes), f32(2 * own, SUB, lanes)),
         in_specs=[SMEM] * 3 + [VMEM] * 8,
-        out_specs=VMEM,
+        out_specs=(VMEM, VMEM),
         scratch_shapes=[
             pltpu.VMEM((pairs + 2 * own + 6, count * SUB, lanes), jnp.float32),
             pltpu.VMEM((5, count, SUB, lanes), jnp.float32),
@@ -390,18 +424,28 @@
     )(odd, counts, order, potentials, orbitals, partner, metric, coefficients, *received)
 
 
-def finish_kernel(sides, odd_ref, n_ref, inner_ref, ends_ref, o_ref, p_ref, e_ref, *refs):
+def strip_place(odd_ref, side):
+    left_own = odd_ref[1] == side
+    in_strip = jnp.where(left_own, HALO, STRIP // 2)
+    in_block = jnp.where(left_own, LANES - HALO, 0)
+    return left_own, in_strip, in_block
+
+
+def strips_kernel(sides, odd_ref, n_ref, rows_ref, e_ref, *refs):
     recv = refs[:sides]
-    v_ref, home_ref, back_ref = refs[sides : sides + 3]
-    st, cf, ms, sr, va, vb, sv, full, sems = refs[sides + 3 :]
-    own, rows, _ = o_ref.shape
+    pay_ref, sv_ref, st, cf, ms, orep, sr, va, vb, flat = refs[sides:]
+    own = n_ref.shape[0] // BLOCKS
     groups, tall, _ = e_ref.shape
+    rows = tall - 2 * SUB
     count = tall // SUB
     lane = lane_of()
     block = lane // STRIP
+    lead = rows_ref.shape[0]
+    fold = rows // SUB // BLOCKS
+    pay_ref[0:lead] = rows_ref[...]
 
     for side in range(sides):
-        left_own = odd_ref[1] == side
+        left_own, in_strip, _ = strip_place(odd_ref, side)
         within = lane_of(tall) % STRIP
         from_own = jnp.where(left_own, within, STRIP - 1 - within) < STRIP // 2
         for g in range(groups):
@@ -418,7 +462,9 @@
         for t in range(count):
             weighted = ms[t] * q[t]
             for g in range(own):
-                sr[g, t] = replicated(o[t], g) * weighted
+                alone = replicated(o[t], g)
+                orep[g, t] = alone
+                sr[g, t] = alone * weighted
         steps = []
         for g in range(own):
             for t, value in enumerate(spread(st, count, 1 + g)):
@@ -435,16 +481,70 @@
             return carry
 
         lax.fori_loop(0, SWEEPS // 2, body, 0)
+        back = []
+        for t in range(count):
+            terms = [va[g, t] * orep[g, t] for g in range(own)]
+            back.append(sum(terms[1:], terms[0]))
+        spread_store(flat, back)
         for g in range(own):
-            spread_store(sv, [va[g, t] for t in range(count)], side * own + g)
+            spread_store(sv_ref, [va[g, t] for t in range(count)], side * own + g)
+        for v in range(fold):
+            out = jnp.zeros((SUB, LANES), jnp.float32)
+            for g in range(BLOCKS):
+                at = SUB + (g * fold + v) * SUB
+                shift = (HALO * g - in_strip) % LANES
+                turned = pltpu.roll(flat[at : at + SUB], shift, 1)
+                out = jnp.where(lane % STRIP // HALO == g, turned, out)
+            pay_ref[lead + side * fold + v] = out
+
+
+def strips(odd, counts, band_back, edges, received):
+    sides = len(received)
+    groups, tall, lanes = edges.shape
+    own = counts.shape[0] // BLOCKS
+    count = tall // SUB
+    fold = (tall - 2 * SUB) // SUB // BLOCKS
+    each = pltpu.VMEM((own, count, SUB, lanes), jnp.float32)
+    return pl.pallas_call(
+        functools.partial(strips_kernel, sides),
+        out_shape=(
+            f32(band_back.shape[0] + sides * fold, SUB, lanes),
+            f32(sides * own, tall, lanes),
+        ),
+        in_specs=[SMEM] * 2 + [VMEM] * (2 + sides),
+        out_specs=(VMEM, VMEM),
+        scratch_shapes=[
+            pltpu.VMEM((groups, tall, lanes), jnp.float32),
+            pltpu.VMEM((5, count, SUB, lanes), jnp.float32),
+            pltpu.VMEM((count, SUB, lanes), jnp.float32),
+            each,
+            each,
+            each,
+            each,
+            pltpu.VMEM((tall, lanes), jnp.float32),
+        ],
+        compiler_params=params(),
+        name="strips",
+    )(odd, counts, band_back, edges, *received)
+
+
+def merge_kernel(sides, odd_ref, inner_ref, ends_ref, sv_ref, o_ref, p_ref, *refs):
+    v_ref, home_ref, full, sems = refs
+    own, rows, _ = o_ref.shape
+    lane = lane_of()
+
+    def copy_out(r):
+        at = pl.multiple_of(r * SUB, SUB)
+        return pltpu.make_async_copy(
+            full.at[:, pl.ds(at, SUB), :], v_ref.at[:, pl.ds(at, SUB), :], sems.at[r]
+        )
 
     def merge(r, carry):
         at = pl.multiple_of(r * SUB, SUB)
-        o = [o_ref[k, pl.ds(at, SUB)] for k in range(own)]
         q = [p_ref[k, pl.ds(at, SUB)] for k in range(own)]
-        home, back = [0.0] * own, [0.0] * own
+        home = [0.0] * own
         for first in range(own):
-            strips = [sv[side * own + first, pl.ds(at + SUB, SUB)] for side in range(sides)]
+            strips = [sv_ref[side * own + first, pl.ds(at + SUB, SUB)] for side in range(sides)]
             for second in range(own):
                 p = first * own + second
                 value = inner_ref[p, pl.ds(at, SUB)]
@@ -459,18 +559,10 @@
                     value = jnp.where(edge, turned, value)
                 full[p, pl.ds(at, SUB)] = value
                 home[first] = home[first] + value * q[second]
-                back[second] = back[second] + value * o[first]
         for k in range(own):
-            home_ref[k, pl.ds(at, SUB)] = o[k] - step_size * home[k]
-            back_ref[k, pl.ds(at, SUB)] = back[k]
+            home_ref[k, pl.ds(at, SUB)] = o_ref[k, pl.ds(at, SUB)] - step_size * home[k]
         copy_out(r).start()
         return carry
-
-    def copy_out(r):
-        at = pl.multiple_of(r * SUB, SUB)
-        return pltpu.make_async_copy(
-            full.at[:, pl.ds(at, SUB), :], v_ref.at[:, pl.ds(at, SUB), :], sems.at[r]
-        )
 
     lax.fori_loop(0, rows // SUB, merge, 0, unroll=4)
 
@@ -481,53 +573,62 @@
     lax.fori_loop(0, rows // SUB, finished, 0)
 
 
-def finish(odd, counts, inner, ends, orbitals, partner, edges, received):
-    own, rows, lanes = orbitals.shape
-    sides = len(received)
-    groups, tall, _ = edges.shape
-    count = tall // SUB
-    strips = pltpu.VMEM((own, count, SUB, lanes), jnp.float32)
-    return pl.pallas_call(
-        functools.partial(finish_kernel, sides),
-        out_shape=(f32(*inner.shape), f32(*orbitals.shape), f32(*orbitals.shape)),
-        in_specs=[SMEM] * 2 + [VMEM] * (5 + sides),
-        out_specs=(ANY, VMEM, VMEM),
+def merged(odd, inner, ends, strip_fields, orbitals, partner):
+    own, rows, _ = orbitals.shape
+    sides = strip_fields.shape[0] // own
+    return pl.pallas_call(
+        functools.partial(merge_kernel, sides),
+        out_shape=(f32(*inner.shape), f32(*orbitals.shape)),
+        in_specs=[SMEM] + [VMEM] * 5,
+        out_specs=(ANY, VMEM),
         scratch_shapes=[
-            pltpu.VMEM((groups, tall, lanes), jnp.float32),
-            pltpu.VMEM((5, count, SUB, lanes), jnp.float32),
-            pltpu.VMEM((count, SUB, lanes), jnp.float32),
-            strips,
-            strips,
-            strips,
-            pltpu.VMEM((sides * own, tall, lanes), jnp.float32),
             pltpu.VMEM(inner.shape, jnp.float32),
             pltpu.SemaphoreType.DMA((rows // SUB,)),
         ],
         compiler_params=params(),
-        name="finish",
-    )(odd, counts, inner, ends, orbitals, partner, edges, *received)
-
-
-def norm_kernel(home_ref, recv_ref, m_ref, upd_ref, norm_ref):
-    own = home_ref.shape[0]
+        name="merge",
+    )(odd, inner, ends, strip_fields, orbitals, partner)
+
+
+def norm_kernel(odd_ref, home_ref, recv_ref, edge_ref, m_ref, upd_ref, norm_ref):
+    own, rows, _ = home_ref.shape
+    lane = lane_of()
+    fold = rows // SUB // BLOCKS
+    lead = 2 * own
+    sides = (edge_ref.shape[0] - lead) // fold
     norm_ref[...] = jnp.zeros_like(norm_ref)
     for k in range(own):
-        updated = home_ref[k] - step_size * recv_ref[k]
-        upd_ref[k] = updated
-        weighted = m_ref[...] * updated * updated
-        norm_ref[k : k + 1] = jnp.sum(weighted, axis=0, keepdims=True)
-
-
-def partial_norms(home, received, metric):
+        total = jnp.zeros((SUB, LANES), jnp.float32)
+        for r in range(rows // SUB):
+            at = r * SUB
+            value = recv_ref[k, at : at + SUB]
+            if r == 0:
+                value = edge_ref[k]
+            if r == rows // SUB - 1:
+                value = edge_ref[own + k]
+            g, v = divmod(r, fold)
+            for side in range(sides):
+                left_own, _, in_block = strip_place(odd_ref, side)
+                edge = jnp.where(left_own, LANES - 1 - lane, lane) < HALO
+                shift = (in_block - STRIP * k - HALO * g) % LANES
+                turned = pltpu.roll(edge_ref[lead + side * fold + v], shift, 1)
+                value = jnp.where(edge, turned, value)
+            updated = home_ref[k, at : at + SUB] - step_size * value
+            upd_ref[k, at : at + SUB] = updated
+            total = total + m_ref[at : at + SUB] * updated * updated
+        norm_ref[k : k + 1] = jnp.sum(total, axis=0, keepdims=True)
+
+
+def partial_norms(odd, home, received, edge_terms, metric):
     own, _, lanes = home.shape
     return pl.pallas_call(
         norm_kernel,
         out_shape=(f32(*home.shape), f32(-(-own // SUB) * SUB, lanes)),
-        in_specs=[VMEM] * 3,
+        in_specs=[SMEM] + [VMEM] * 4,
         out_specs=(VMEM, VMEM),
         compiler_params=params(),
         name="partial_norms",
-    )(home, received, metric)
+    )(odd, home, received, edge_terms, metric)
 
 
 def scale_kernel(cells, upd_ref, norm_ref, other_ref, out_ref):
@@ -600,22 +701,23 @@
     ready = prepare(odd, potentials, orbitals, metric, coefficients)
     pay_b, ready = lax.optimization_barrier((pay_b, ready))
     rows_b = lax.ppermute(pay_b, ("gx", "gy"), row_swaps[1])
-    inner = interior(half, 0, odd, sweep_counts, order, ready, partner)
+    inner = interior(half, 0, False, odd, sweep_counts, order, ready, partner)
     rows_a, rows_b, inner = lax.optimization_barrier((rows_a, rows_b, inner))
     beside = jnp.concatenate([rows_a[:own], rows_b[:own]], 0)
     partner_rows = shifted(beside, "orb", 1)
-    inner = interior(half, half, odd, sweep_counts, order, ready, partner, inner)
-    partner_rows, inner = lax.optimization_barrier((partner_rows, inner))
-    edges = tall_edges(odd, ready[3], rows_a, rows_b, partner_rows, partner)
+    inner, back = interior(half, half, True, odd, sweep_counts, order, ready, partner, *inner)
+    partner_rows, inner, back = lax.optimization_barrier((partner_rows, inner, back))
+    early = shifted(back, "orb", -1)
+    edges = tall_edges(odd, ready[4], rows_a, rows_b, partner_rows, partner)
     received = [lax.ppermute(edges, "gy", swap) for swap in col_swaps]
-    ends = bands(
+    ends, band_back = bands(
         odd, sweep_counts, order, potentials, orbitals, partner, metric, coefficients,
         rows_a, rows_b, partner_rows,
     )
-    fields, home, back = finish(
-        odd, sweep_counts, inner, ends, orbitals, partner, edges, received
-    )
-    updated, norms = partial_norms(home, shifted(back, "orb", -1), metric)
+    edge_back, strip_fields = strips(odd, sweep_counts, band_back, edges, received)
+    edge_terms = shifted(edge_back, "orb", -1)
+    fields, home = merged(odd, inner, ends, strip_fields, orbitals, partner)
+    updated, norms = partial_norms(odd, home, early, edge_terms, metric)
     hops = norm_hops(gx, gy)
     for at, hop in enumerate(hops):
         other = lax.ppermute(norms, ("gx", "gy"), hop)

time: 46.8 us -> 43.7 us (0.934)
  waiting for transfers between devices: 12.3 us -> 5.48 us
  Pallas kernels: 17.1 us -> 20.2 us
  starting transfers between devices: 12.2 us -> 13 us
    ppermute x3 -> x4, waiting for transfers between devices: 7.59 us -> 0.78 us  [shifted(): lax.ppermute(value, axis, [(i, (i + by) % size) for i in range(size)])]
    pallas_call x4 -> x5, Pallas kernels: 13.2 us -> 15 us  [the longest x2 7.42 us: interior(): pl.pallas_call(functools.partial(interior_kernel, groups, before, last),...]
    ppermute x3 -> x4, starting transfers between devices: 6.25 us -> 7.03 us  [shifted(): lax.ppermute(value, axis, [(i, (i + by) % size) for i in range(size)])]
    pallas_call x1, Pallas kernels: 0.06 us -> 0.7 us  [partial_norms(): pl.pallas_call(norm_kernel, out_shape=(f32(*home.shape), f32(-(-own // SU...]
    pallas_call x1, Pallas kernels: 1.61 us -> 2.22 us  [prepare(): pl.pallas_call(prepare_kernel, out_shape=(f32(potentials.shape[0], count,...]
  transfers between devices with their start and end apart: 9 -> 10, of which waited for: 5 -> 4; matrix products, arithmetic and copies ran while one was open for 1% -> 1% of each run, Pallas kernels for 25% -> 41%
where the time goes in v4:
time: 43.7 us; the launch traced here: 43.6 us
  Pallas kernels  20.2 us (46%)
  starting transfers between devices  13 us (30%)
  waiting for transfers between devices  5.48 us (13%)
  local copies, waits for them, and re-layouts  3.75 us (9%)
  between operations  0.83 us (2%)
    pallas_call x2, Pallas kernels, interior(): pl.pallas_call(functools.partial(interior_kernel, groups, before, last),...  7.42 us
    ppermute x4, starting transfers between devices, shifted(): lax.ppermute(value, axis, [(i, (i + by) % size) for i in range(size)])  7.03 us
    ppermute x3, waiting for transfers between devices, local(): other = lax.ppermute(norms, ('gx', 'gy'), hop)  4.69 us
    ppermute x3, starting transfers between devices, local(): other = lax.ppermute(norms, ('gx', 'gy'), hop)  4.14 us
    unnamed x16, local copies, waits for them, and re-layouts  3.74 us
    pallas_call x1, Pallas kernels, bands(): pl.pallas_call(bands_kernel, out_shape=(f32(pairs, 2, SUB, lanes), f32(2...  2.85 us
    pallas_call x1, Pallas kernels, strips(): pl.pallas_call(functools.partial(strips_kernel, sides), out_shape=(f32(ba...  2.81 us
    pallas_call x1, Pallas kernels, prepare(): pl.pallas_call(prepare_kernel, out_shape=(f32(potentials.shape[0], count,...  2.22 us
  transfers between devices with their start and end apart: 10, of which 4 were waited for; matrix products, arithmetic and copies ran while one was open for 1% of the time, Pallas kernels for 41%

profile of v4, /device:TPU:0, one launch (start us, length us, event | category | flops | bytes accessed | tf_op | source)
XLA Modules:
  0.0 43.6 jit_solution(14487400690305187741)
XLA Ops:
  0.6 3.0 %collective-permute-start.2 = (f32[4,128,128]{2,1,0:T(8,128)}, f32[4,128,128]{2,1,0:T(8,128)S(1)}, u32[]{:S(2)}, u32[]{:S(2)}) collective-permute-start(f32[4,128,128]{2,1,0:T(8,128)} %o_ref.5), channel_id=1, source_target_pairs={{0,8},{8,16},{16,24},{24,0},{1,9},{9,17},{17,25},{25,1},{2,10},{10... | collective-permute-start | bytes 786440 | tf_op jit(solution)/shard_map/ppermute | solution.py:654
  3.6 0.1 pad_add_fusion.par_ref.odd_ref
  3.7 1.2 %copy-done = f32[16,128,128]{2,1,0:T(8,128)S(1)} copy-done((f32[16,128,128]{2,1,0:T(8,128)S(1)}, f32[16,128,128]{2,1,0:T(8,128)}, u32[]{:S(2)}) %copy-start) | copy-done | bytes 1048600
  4.9 0.9 %copy-done.2 = f32[4,128,128]{2,1,0:T(8,128)S(1)} copy-done((f32[4,128,128]{2,1,0:T(8,128)S(1)}, f32[4,128,128]{2,1,0:T(8,128)}, u32[]{:S(2)}) %copy-start.2) | copy-done | bytes 262168
  5.9 1.0 %copy-done.4 = f32[5,128,128]{2,1,0:T(8,128)S(1)} copy-done((f32[5,128,128]{2,1,0:T(8,128)S(1)}, f32[5,128,128]{2,1,0:T(8,128)}, u32[]{:S(2)}) %copy-start.4) | copy-done | bytes 327704
  6.9 0.7 %row_payloads.1 = (f32[26,8,128]{2,1,0:T(8,128)S(1)}, f32[26,8,128]{2,1,0:T(8,128)S(1)}) custom-call(s32[3]{0:T(128)S(1)} %pad_add_fusion.par_ref.odd_ref, f32[4,128,128]{2,1,0:T(8,128)S(1)} %copy-done.2, f32[16,128,128]{2,1,0:T(8,128)S(1)} %copy-done, f32[1,128,128]{2,1,0:T(8,128)S(1)} %bitcast.4, f32[5,128,128]{2,1,0:T(8,128)S(1)} %copy-done.4), custom_call_target="tpu_custom_call" | custom-call | tf_op jit(solution)/shard_map/row_payloads/pallas_call | solution.py:234
  7.6 1.6 %collective-permute-start = (f32[26,8,128]{2,1,0:T(8,128)S(1)}, f32[26,8,128]{2,1,0:T(8,128)S(1)}, u32[]{:S(2)}, u32[]{:S(2)}) collective-permute-start(f32[26,8,128]{2,1,0:T(8,128)S(1)} %get-tuple-element.34), channel_id=1, source_target_pairs={{0,2},{1,3},{2,0},{3,1},{4,6},{5,7},{6,4},{7,5},{8,10},{9,11},{10,... | collective-permute-start | bytes 319496 | tf_op jit(solution)/shard_map/ppermute | solution.py:700
  9.2 2.2 %prepare.1 = (f32[16,16,8,128]{3,2,1,0:T(8,128)S(1)}, f32[4,16,8,128]{3,2,1,0:T(8,128)S(1)}, f32[4,16,8,128]{3,2,1,0:T(8,128)S(1)}, f32[5,16,8,128]{3,2,1,0:T(8,128)S(1)}, f32[7,128,128]{2,1,0:T(8,128)S(1)}) custom-call(s32[3]{0:T(128)S(1)} %pad_add_fusion.par_ref.odd_ref, f32[16,128,128]{2,1,0:T(8,128)S(1)} %copy-done, f32[4,128,128]{2,1,0:T(8,128)S(1)} %copy-done.2, ...), custom_call_target="tpu_custom_call" | custom-call | tf_op jit(solution)/shard_map/prepare/pallas_call | solution.py:194
  11.4 0.0 copy-start.7
  11.4 0.1 collective-permute-start.1
  11.5 0.6 %copy-done.7 = s32[16]{0:T(128)S(1)} copy-done((s32[16]{0:T(128)S(1)}, s32[16]{0:T(128)}, u32[]{:S(2)}) %copy-start.7) | copy-done | bytes 88
  12.1 0.2 convert_reduce_fusion
  12.3 0.1 select_reduce_fusion.by_ref
  12.4 3.8 %interior0.1 = (f32[16,128,128]{2,1,0:T(8,128)S(1)}, f32[4,16,8,128]{3,2,1,0:T(8,128)S(1)}) custom-call(s32[3]{0:T(128)S(1)} %pad_add_fusion.par_ref.odd_ref, s32[16]{0:T(128)S(1)} %copy-done.7, s32[16]{0:T(128)S(1)} %select_reduce_fusion.by_ref, f32[16,16,8,128]{3,2,1,0:T(8,128)S(1)} %get-tuple-element.42.refs_0_, ...), custom_call_target="tpu_custom_call" | custom-call | tf_op jit(solution)/shard_map/interior0/pallas_call | solution.py:294
  16.3 1.5 %collective-permute-start.3 = (f32[8,8,128]{2,1,0:T(8,128)S(1)}, f32[8,8,128]{2,1,0:T(8,128)S(1)}, u32[]{:S(2)}, u32[]{:S(2)}) collective-permute-start(f32[8,8,128]{2,1,0:T(8,128)S(1)} %pad_maximum_fusion), channel_id=1, source_target_pairs={{0,8},{8,16},{16,24},{24,0},{1,9},{9,17},{17,25},{25,1},{2,10},{10... | collective-permute-start | bytes 98312 | tf_op jit(solution)/shard_map/ppermute | solution.py:654
  17.8 3.6 %interior2.1 = (f32[16,128,128]{2,1,0:T(8,128)S(1)}, f32[4,128,128]{2,1,0:T(8,128)S(1)}) custom-call(s32[3]{0:T(128)S(1)} %pad_add_fusion.par_ref.odd_ref, s32[16]{0:T(128)S(1)} %copy-done.7, s32[16]{0:T(128)S(1)} %select_reduce_fusion.by_ref, f32[16,16,8,128]{3,2,1,0:T(8,128)S(1)} %get-tuple-element.42.refs_0_, ...), custom_call_target="tpu_custom_call" | custom-call | tf_op jit(solution)/shard_map/interior2/pallas_call | solution.py:294
  21.5 0.7 %tall_edges.1.e_ref = f32[8,144,128]{2,1,0:T(8,128)S(1)} custom-call(s32[3]{0:T(128)S(1)} %pad_add_fusion.par_ref.odd_ref, f32[7,128,128]{2,1,0:T(8,128)S(1)} %get-tuple-element.58.e_ref, f32[26,8,128]{2,1,0:T(8,128)S(1)} %collective-permute-done.ra_ref, f32[26,8,128]{2,1,0:T(8,128)S(1)} %collective-permute-done.1.rb_ref, ...), custom_call_target="tpu_custom_call" | custom-call | tf_op jit(solution)/shard_map/tall_edges/pallas_call | solution.py:330
  22.2 0.1 collective-permute-start.4
  22.3 1.1 %collective-permute-start.5 = (f32[4,128,128]{2,1,0:T(8,128)S(1)}, f32[4,128,128]{2,1,0:T(8,128)S(1)}, u32[]{:S(2)}, u32[]{:S(2)}) collective-permute-start(f32[4,128,128]{2,1,0:T(8,128)S(1)} %get-tuple-element.61), channel_id=1, source_target_pairs={{0,24},{8,0},{16,8},{24,16},{1,25},{9,1},{17,9},{25,17},{2,26},{10... | collective-permute-start | bytes 786440 | tf_op jit(solution)/shard_map/ppermute | solution.py:654
  23.4 2.8 %bands.1 = (f32[16,2,8,128]{3,2,1,0:T(8,128)S(1)}, f32[8,8,128]{2,1,0:T(8,128)S(1)}) custom-call(s32[3]{0:T(128)S(1)} %pad_add_fusion.par_ref.odd_ref, s32[16]{0:T(128)S(1)} %copy-done.7, s32[16]{0:T(128)S(1)} %select_reduce_fusion.by_ref, f32[16,128,128]{2,1,0:T(8,128)S(1)} %copy-done.1, f32[4,128,128]{2,1,0:T(8,128)S(1)} %copy-done.3, ...), custom_call_target="tpu_custom_call" | custom-call | tf_op jit(solution)/shard_map/bands/pallas_call | solution.py:409
  26.3 2.8 %strips.1 = (f32[12,8,128]{2,1,0:T(8,128)S(1)}, f32[4,144,128]{2,1,0:T(8,128)S(1)}) custom-call(s32[3]{0:T(128)S(1)} %pad_add_fusion.par_ref.odd_ref, s32[16]{0:T(128)S(1)} %copy-done.7, f32[8,8,128]{2,1,0:T(8,128)S(1)} %get-tuple-element.57.rows_ref, f32[8,144,128]{2,1,0:T(8,128)S(1)} %tall_edges.1.e_ref, f32[8,144,128]{2,1,0:T(8,128)S(1)} %collective-permute-done.4.refs_0_), custom_call_target="tpu_custom_call" | custom-call | tf_op jit(solution)/shard_map/strips/pallas_call | solution.py:508
  29.1 1.4 %collective-permute-start.6 = (f32[12,8,128]{2,1,0:T(8,128)S(1)}, f32[12,8,128]{2,1,0:T(8,128)S(1)}, u32[]{:S(2)}, u32[]{:S(2)}) collective-permute-start(f32[12,8,128]{2,1,0:T(8,128)S(1)} %get-tuple-element.62), channel_id=1, source_target_pairs={{0,24},{8,0},{16,8},{24,16},{1,25},{9,1},{17,9},{25,17},{2,26},{10... | collective-permute-start | bytes 147464 | tf_op jit(solution)/shard_map/ppermute | solution.py:654
  30.5 2.0 %merge.1 = (f32[16,128,128]{2,1,0:T(8,128)}, f32[4,128,128]{2,1,0:T(8,128)S(1)}) custom-call(s32[3]{0:T(128)S(1)} %pad_add_fusion.par_ref.odd_ref, f32[16,128,128]{2,1,0:T(8,128)S(1)} %get-tuple-element.54.inner_ref, f32[16,2,8,128]{3,2,1,0:T(8,128)S(1)} %get-tuple-element.56.ends_ref, f32[4,144,128]{2,1,0:T(8,128)S(1)} %get-tuple-element.59.sv_ref, ...), custom_call_target="tpu_custom_call" | custom-call | tf_op jit(solution)/shard_map/merge/pallas_call | solution.py:579
  32.4 0.8 %collective-permute-done.6.edge_ref = f32[12,8,128]{2,1,0:T(8,128)S(1)} collective-permute-done((f32[12,8,128]{2,1,0:T(8,128)S(1)}, f32[12,8,128]{2,1,0:T(8,128)S(1)}, u32[]{:S(2)}, u32[]{:S(2)}) %collective-permute-start.6) | collective-permute-done | bytes 49184 | tf_op jit(solution)/shard_map/ppermute | solution.py:654
  33.2 0.7 %partial_norms.1 = (f32[4,128,128]{2,1,0:T(8,128)S(1)}, f32[8,128]{1,0:T(8,128)S(1)}) custom-call(s32[3]{0:T(128)S(1)} %pad_add_fusion.par_ref.odd_ref, f32[4,128,128]{2,1,0:T(8,128)S(1)} %get-tuple-element.60.home_ref, f32[4,128,128]{2,1,0:T(8,128)S(1)} %collective-permute-done.5.recv_ref, f32[12,8,128]{2,1,0:T(8,128)S(1)} %collective-permute-done.6.edge_ref, ...), custom_call_target="tpu_custom_call" | custom-call | tf_op jit(solution)/shard_map/partial_norms/pallas_call | solution.py:624
  33.9 0.1 collective-permute-start.7
  34.0 1.2 %collective-permute-done.7 = f32[8,128]{1,0:T(8,128)S(1)} collective-permute-done((f32[8,128]{1,0:T(8,128)S(1)}, f32[8,128]{1,0:T(8,128)S(1)}, u32[]{:S(2)}, u32[]{:S(2)}) %collective-permute-start.7) | collective-permute-done | bytes 4128 | tf_op jit(solution)/shard_map/ppermute | solution.py:723
  35.2 2.4 %collective-permute-start.8 = (f32[8,128]{1,0:T(8,128)S(1)}, f32[8,128]{1,0:T(8,128)S(1)}, u32[]{:S(2)}, u32[]{:S(2)}) collective-permute-start(f32[8,128]{1,0:T(8,128)S(1)} %add.15), channel_id=1, source_target_pairs={{0,3},{1,2},{2,1},{3,0},{4,7},{5,6},{6,5},{7,4},{8,11},{9,10},{10,... | collective-permute-start | bytes 12296 | tf_op jit(solution)/shard_map/ppermute | solution.py:723
  37.5 1.3 %collective-permute-done.8 = f32[8,128]{1,0:T(8,128)S(1)} collective-permute-done((f32[8,128]{1,0:T(8,128)S(1)}, f32[8,128]{1,0:T(8,128)S(1)}, u32[]{:S(2)}, u32[]{:S(2)}) %collective-permute-start.8) | collective-permute-done | bytes 4128 | tf_op jit(solution)/shard_map/ppermute | solution.py:723
  38.8 1.7 %collective-permute-start.9 = (f32[8,128]{1,0:T(8,128)S(1)}, f32[8,128]{1,0:T(8,128)S(1)}, u32[]{:S(2)}, u32[]{:S(2)}) collective-permute-start(f32[8,128]{1,0:T(8,128)S(1)} %add.16.norm_ref), channel_id=1, source_target_pairs={{0,5},{1,4},{2,7},{3,6},{4,1},{5,0},{6,3},{7,2},{8,13},{9,12},{10,... | collective-permute-start | bytes 12296 | tf_op jit(solution)/shard_map/ppermute | solution.py:723
  40.6 2.2 %collective-permute-done.9.other_ref = f32[8,128]{1,0:T(8,128)S(1)} collective-permute-done((f32[8,128]{1,0:T(8,128)S(1)}, f32[8,128]{1,0:T(8,128)S(1)}, u32[]{:S(2)}, u32[]{:S(2)}) %collective-permute-start.9) | collective-permute-done | bytes 4128 | tf_op jit(solution)/shard_map/ppermute | solution.py:723
  42.8 0.8 %rescaled.1 = f32[4,128,128]{2,1,0:T(8,128)} custom-call(f32[4,128,128]{2,1,0:T(8,128)S(1)} %get-tuple-element.63.upd_ref, f32[8,128]{1,0:T(8,128)S(1)} %add.16.norm_ref, f32[8,128]{1,0:T(8,128)S(1)} %collective-permute-done.9.other_ref), custom_call_target="tpu_custom_call" | custom-call | tf_op jit(solution)/shard_map/rescaled/pallas_call | solution.py:642
  (22 shorter events, 0.1 us)
Async XLA Ops:
  0.6 3.1 %copy-start.6 = (f32[128,128]{1,0:T(8,128)S(1)}, f32[128,128]{1,0:T(8,128)}, u32[]{:S(2)}) copy-start(f32[128,128]{1,0:T(8,128)} %m_ref.3) | copy-start | bytes 196612
  0.6 11.7 %collective-permute-start.2 = (f32[4,128,128]{2,1,0:T(8,128)}, f32[4,128,128]{2,1,0:T(8,128)S(1)}, u32[]{:S(2)}, u32[]{:S(2)}) collective-permute-start(f32[4,128,128]{2,1,0:T(8,128)} %o_ref.5), channel_id=1, source_target_pairs={{0,8},{8,16},{16,24},{24,0},{1,9},{9,17},{17,25},{25,1},{2,10},{10... | collective-permute-start | bytes 786440 | tf_op jit(solution)/shard_map/ppermute | solution.py:654
  3.7 1.2 %copy-start = (f32[16,128,128]{2,1,0:T(8,128)S(1)}, f32[16,128,128]{2,1,0:T(8,128)}, u32[]{:S(2)}) copy-start(f32[16,128,128]{2,1,0:T(8,128)} %v_ref.3) | copy-start | bytes 3145732
  4.9 0.9 %copy-start.2 = (f32[4,128,128]{2,1,0:T(8,128)S(1)}, f32[4,128,128]{2,1,0:T(8,128)}, u32[]{:S(2)}) copy-start(f32[4,128,128]{2,1,0:T(8,128)} %o_ref.5) | copy-start | bytes 786436
  5.9 1.0 %copy-start.4 = (f32[5,128,128]{2,1,0:T(8,128)S(1)}, f32[5,128,128]{2,1,0:T(8,128)}, u32[]{:S(2)}) copy-start(f32[5,128,128]{2,1,0:T(8,128)} %c_ref.3) | copy-start | bytes 983044
  7.6 8.7 %collective-permute-start = (f32[26,8,128]{2,1,0:T(8,128)S(1)}, f32[26,8,128]{2,1,0:T(8,128)S(1)}, u32[]{:S(2)}, u32[]{:S(2)}) collective-permute-start(f32[26,8,128]{2,1,0:T(8,128)S(1)} %get-tuple-element.34), channel_id=1, source_target_pairs={{0,2},{1,3},{2,0},{3,1},{4,6},{5,7},{6,4},{7,5},{8,10},{9,11},{10,... | collective-permute-start | bytes 319496 | tf_op jit(solution)/shard_map/ppermute | solution.py:700
  11.4 0.7 %copy-start.7 = (s32[16]{0:T(128)S(1)}, s32[16]{0:T(128)}, u32[]{:S(2)}) copy-start(s32[16]{0:T(128)} %n_ref.7) | copy-start | bytes 196
  11.4 4.8 %collective-permute-start.1 = (f32[26,8,128]{2,1,0:T(8,128)S(1)}, f32[26,8,128]{2,1,0:T(8,128)S(1)}, u32[]{:S(2)}, u32[]{:S(2)}) collective-permute-start(f32[26,8,128]{2,1,0:T(8,128)S(1)} %get-tuple-element.41), channel_id=1, source_target_pairs={{0,1},{1,0},{2,4},{3,5},{4,2},{5,3},{6,7},{7,6},{8,9},{9,8},{10,12... | collective-permute-start | bytes 319496 | tf_op jit(solution)/shard_map/ppermute | solution.py:703
  16.3 5.2 %collective-permute-start.3 = (f32[8,8,128]{2,1,0:T(8,128)S(1)}, f32[8,8,128]{2,1,0:T(8,128)S(1)}, u32[]{:S(2)}, u32[]{:S(2)}) collective-permute-start(f32[8,8,128]{2,1,0:T(8,128)S(1)} %pad_maximum_fusion), channel_id=1, source_target_pairs={{0,8},{8,16},{16,24},{24,0},{1,9},{9,17},{17,25},{25,1},{2,10},{10... | collective-permute-start | bytes 98312 | tf_op jit(solution)/shard_map/ppermute | solution.py:654
  17.8 5.6 %copy-start.5 = (f32[5,128,128]{2,1,0:T(8,128)S(1)}, f32[5,128,128]{2,1,0:T(8,128)}, u32[]{:S(2)}) copy-start(f32[5,128,128]{2,1,0:T(8,128)} %c_ref.3) | copy-start | bytes 983044
  21.4 2.0 %copy-start.1 = (f32[16,128,128]{2,1,0:T(8,128)S(1)}, f32[16,128,128]{2,1,0:T(8,128)}, u32[]{:S(2)}) copy-start(f32[16,128,128]{2,1,0:T(8,128)} %v_ref.3) | copy-start | bytes 3145732
  21.5 1.9 %copy-start.3 = (f32[4,128,128]{2,1,0:T(8,128)S(1)}, f32[4,128,128]{2,1,0:T(8,128)}, u32[]{:S(2)}) copy-start(f32[4,128,128]{2,1,0:T(8,128)} %o_ref.5) | copy-start | bytes 786436
  22.2 4.0 %collective-permute-start.4 = (f32[8,144,128]{2,1,0:T(8,128)S(1)}, f32[8,144,128]{2,1,0:T(8,128)S(1)}, u32[]{:S(2)}, u32[]{:S(2)}) collective-permute-start(f32[8,144,128]{2,1,0:T(8,128)S(1)} %tall_edges.1.e_ref), channel_id=1, source_target_pairs={{0,1},{1,0},{2,3},{3,2},{4,5},{5,4},{6,7},{7,6},{8,9},{9,8},{10,11... | collective-permute-start | bytes 1769480 | tf_op jit(solution)/shard_map/ppermute | solution.py:712
  22.3 10.2 %collective-permute-start.5 = (f32[4,128,128]{2,1,0:T(8,128)S(1)}, f32[4,128,128]{2,1,0:T(8,128)S(1)}, u32[]{:S(2)}, u32[]{:S(2)}) collective-permute-start(f32[4,128,128]{2,1,0:T(8,128)S(1)} %get-tuple-element.61), channel_id=1, source_target_pairs={{0,24},{8,0},{16,8},{24,16},{1,25},{9,1},{17,9},{25,17},{2,26},{10... | collective-permute-start | bytes 786440 | tf_op jit(solution)/shard_map/ppermute | solution.py:654
  29.1 4.1 %collective-permute-start.6 = (f32[12,8,128]{2,1,0:T(8,128)S(1)}, f32[12,8,128]{2,1,0:T(8,128)S(1)}, u32[]{:S(2)}, u32[]{:S(2)}) collective-permute-start(f32[12,8,128]{2,1,0:T(8,128)S(1)} %get-tuple-element.62), channel_id=1, source_target_pairs={{0,24},{8,0},{16,8},{24,16},{1,25},{9,1},{17,9},{25,17},{2,26},{10... | collective-permute-start | bytes 147464 | tf_op jit(solution)/shard_map/ppermute | solution.py:654
  33.9 1.2 %collective-permute-start.7 = (f32[8,128]{1,0:T(8,128)S(1)}, f32[8,128]{1,0:T(8,128)S(1)}, u32[]{:S(2)}, u32[]{:S(2)}) collective-permute-start(f32[8,128]{1,0:T(8,128)S(1)} %get-tuple-element.64), channel_id=1, source_target_pairs={{0,1},{1,0},{2,3},{3,2},{4,5},{5,4},{6,7},{7,6},{8,9},{9,8},{10,11... | collective-permute-start | bytes 12296 | tf_op jit(solution)/shard_map/ppermute | solution.py:723
  35.2 3.7 %collective-permute-start.8 = (f32[8,128]{1,0:T(8,128)S(1)}, f32[8,128]{1,0:T(8,128)S(1)}, u32[]{:S(2)}, u32[]{:S(2)}) collective-permute-start(f32[8,128]{1,0:T(8,128)S(1)} %add.15), channel_id=1, source_target_pairs={{0,3},{1,2},{2,1},{3,0},{4,7},{5,6},{6,5},{7,4},{8,11},{9,10},{10,... | collective-permute-start | bytes 12296 | tf_op jit(solution)/shard_map/ppermute | solution.py:723
  38.8 3.9 %collective-permute-start.9 = (f32[8,128]{1,0:T(8,128)S(1)}, f32[8,128]{1,0:T(8,128)S(1)}, u32[]{:S(2)}, u32[]{:S(2)}) collective-permute-start(f32[8,128]{1,0:T(8,128)S(1)} %add.16.norm_ref), channel_id=1, source_target_pairs={{0,5},{1,4},{2,7},{3,6},{4,1},{5,0},{6,3},{7,2},{8,13},{9,12},{10,... | collective-permute-start | bytes 12296 | tf_op jit(solution)/shard_map/ppermute | solution.py:723

commit v5 on v4

--- a/solution.py
+++ b/solution.py
@@ -34,8 +34,14 @@
     return jax.ShapeDtypeStruct(shape, jnp.float32)
 
 
-def params(limit=VMEM_LIMIT):
-    return pltpu.CompilerParams(vmem_limit_bytes=limit)
+def params():
+    return pltpu.CompilerParams(vmem_limit_bytes=VMEM_LIMIT)
+
+
+def cost(microseconds):
+    return pl.CostEstimate(
+        flops=0, bytes_accessed=int(microseconds * 3.7e6), transcendentals=0
+    )
 
 
 def lane_of(rows=SUB):
@@ -147,25 +153,38 @@
     return west, east, dead
 
 
-def prepare_kernel(odd_ref, v_hbm, o_hbm, m_hbm, c_hbm, *refs):
-    vs_ref, os_ref, om_ref, cf_ref, e_ref, v_ref, o_ref, m_ref, c_ref, sems = refs
+def prepare_kernel(odd_ref, o_hbm, v_hbm, m_hbm, c_hbm, *refs):
+    vs_ref, os_ref, om_ref, cf_ref, e_ref, pay_a, pay_b, o_ref, v_ref, m_ref, c_ref, sems = refs
     own, rows, _ = o_ref.shape
+    pairs = v_ref.shape[0]
     count = rows // SUB
+    sources = [(m_hbm, m_ref), (c_hbm, c_ref), (o_hbm, o_ref)]
+    for first in range(own):
+        part = pl.ds(first * own, own)
+        sources.append((v_hbm.at[part], v_ref.at[part]))
     copies = [
         pltpu.make_async_copy(source, target, sems.at[at])
-        for at, (source, target) in enumerate(((m_hbm, m_ref), (c_hbm, c_ref), (o_hbm, o_ref)))
+        for at, (source, target) in enumerate(sources)
     ]
-    for first in range(own):
-        part = pl.ds(first * own, own)
-        copies.append(pltpu.make_async_copy(v_hbm.at[part], v_ref.at[part], sems.at[3 + first]))
     for copy in copies:
         copy.start()
+
+    starts = [(1 - odd_ref[0]) * (rows - HALO), odd_ref[0] * (rows - HALO)]
+    starts = [pl.multiple_of(start, HALO) for start in starts]
+
+    def send_rows(at, ref, index):
+        for pay, start in zip((pay_a, pay_b), starts):
+            pay[at] = ref[index, pl.ds(start, HALO)]
+
     copies[0].wait()
     copies[1].wait()
-    e_ref[1 + own] = packed([m_ref[...], c_ref[0], c_ref[1], c_ref[2]])
+    send_rows(own + pairs, m_ref, 0)
+    for n in range(5):
+        send_rows(own + pairs + 1 + n, c_ref, n)
+    e_ref[1 + own] = packed([m_ref[0], c_ref[0], c_ref[1], c_ref[2]])
     e_ref[2 + own] = packed([c_ref[3], c_ref[4]])
     dead = lane_masks(odd_ref[1])[2]
-    metric = spread(m_ref, count)
+    metric = spread(m_ref, count, 0)
     raw = [spread(c_ref, count, n) for n in range(5)]
     weights = []
     for t in range(count):
@@ -176,70 +195,43 @@
     copies[2].wait()
     e_ref[0] = packed([o_ref[k] for k in range(own)])
     for k in range(own):
+        send_rows(k, o_ref, k)
         for t, value in enumerate(spread(o_ref, count, k)):
             os_ref[k, t] = value
             om_ref[k, t] = weights[t] * value
     for first in range(own):
         copies[3 + first].wait()
         e_ref[1 + first] = packed([v_ref[first * own + k] for k in range(own)])
-        for k in range(own):
-            for t, value in enumerate(spread(v_ref, count, first * own + k)):
-                vs_ref[first * own + k, t] = value
-
-
-def prepare(odd, potentials, orbitals, metric, coefficients):
+        for p in range(first * own, (first + 1) * own):
+            send_rows(own + p, v_ref, p)
+            for t, value in enumerate(spread(v_ref, count, p)):
+                vs_ref[p, t] = value
+
+
+def prepare(odd, *arrays):
+    orbitals, potentials, _, coefficients = arrays
     own, rows, lanes = orbitals.shape
+    pairs = potentials.shape[0]
     count = rows // SUB
-    arrays = (potentials, orbitals, metric, coefficients)
+    inputs = [pltpu.with_memory_space_constraint(a, pltpu.HBM) for a in arrays]
     return pl.pallas_call(
         prepare_kernel,
         out_shape=(
-            f32(potentials.shape[0], count, SUB, lanes),
+            f32(pairs, count, SUB, lanes),
             f32(own, count, SUB, lanes),
             f32(own, count, SUB, lanes),
             f32(5, count, SUB, lanes),
             f32(own + 3, rows, lanes),
+            *[f32(own + pairs + 1 + coefficients.shape[0], HALO, lanes)] * 2,
         ),
         in_specs=[SMEM] + [HBM] * 4,
-        out_specs=(VMEM,) * 5,
+        out_specs=(VMEM,) * 7,
         scratch_shapes=[pltpu.VMEM(a.shape, jnp.float32) for a in arrays]
         + [pltpu.SemaphoreType.DMA((3 + own,))],
         compiler_params=params(),
+        cost_estimate=cost(2.0),
         name="prepare",
-    )(odd, *arrays)
-
-
-def rows_kernel(par_ref, o_ref, v_ref, m_ref, c_ref, pay_a, pay_b, sems):
-    rows = o_ref.shape[1]
-    odd = par_ref[0]
-    copies = []
-    for pay, start in ((pay_a, (1 - odd) * (rows - HALO)), (pay_b, odd * (rows - HALO))):
-        start = pl.multiple_of(start, HALO)
-        at = 0
-        for ref in (o_ref, v_ref, m_ref, c_ref):
-            count = ref.shape[0]
-            copy = pltpu.make_async_copy(
-                ref.at[:, pl.ds(start, HALO), :], pay.at[pl.ds(at, count)], sems.at[len(copies)]
-            )
-            copy.start()
-            copies.append(copy)
-            at += count
-    for copy in copies:
-        copy.wait()
-
-
-def row_payloads(odd, orbitals, potentials, metric, coefficients):
-    own, _, lanes = orbitals.shape
-    fields = own + potentials.shape[0] + 1 + coefficients.shape[0]
-    return pl.pallas_call(
-        rows_kernel,
-        out_shape=(f32(fields, HALO, lanes),) * 2,
-        in_specs=[SMEM] + [HBM] * 4,
-        out_specs=(ANY, ANY),
-        scratch_shapes=[pltpu.SemaphoreType.DMA((8,))],
-        compiler_params=params(),
-        name="row_payloads",
-    )(odd, orbitals, potentials, metric[None], coefficients)
+    )(odd, *inputs)
 
 
 def interior_kernel(groups, before, last, odd_ref, n_ref, by_ref, *refs):
@@ -298,6 +290,7 @@
         out_specs=(VMEM, VMEM),
         scratch_shapes=[each, each, four, four, four],
         compiler_params=params(),
+        cost_estimate=cost(1.8 * groups),
         name=f"interior{before}",
     )(odd, counts, order, *ready[:4], partner, *earlier)
 
@@ -333,6 +326,7 @@
         in_specs=[SMEM] + [VMEM] * 5,
         out_specs=VMEM,
         compiler_params=params(),
+        cost_estimate=cost(0.7),
         name="tall_edges",
     )(odd, edges, rows_a, rows_b, partner_rows, partner)
 
@@ -420,6 +414,7 @@
             some,
         ],
         compiler_params=params(),
+        cost_estimate=cost(2.5),
         name="bands",
     )(odd, counts, order, potentials, orbitals, partner, metric, coefficients, *received)
 
@@ -524,20 +519,14 @@
             pltpu.VMEM((tall, lanes), jnp.float32),
         ],
         compiler_params=params(),
+        cost_estimate=cost(2.9),
         name="strips",
     )(odd, counts, band_back, edges, *received)
 
 
-def merge_kernel(sides, odd_ref, inner_ref, ends_ref, sv_ref, o_ref, p_ref, *refs):
-    v_ref, home_ref, full, sems = refs
+def merge_kernel(sides, odd_ref, inner_ref, ends_ref, sv_ref, o_ref, p_ref, v_ref, home_ref):
     own, rows, _ = o_ref.shape
     lane = lane_of()
-
-    def copy_out(r):
-        at = pl.multiple_of(r * SUB, SUB)
-        return pltpu.make_async_copy(
-            full.at[:, pl.ds(at, SUB), :], v_ref.at[:, pl.ds(at, SUB), :], sems.at[r]
-        )
 
     def merge(r, carry):
         at = pl.multiple_of(r * SUB, SUB)
@@ -557,20 +546,13 @@
                         strips[side], (-(STRIP * second + STRIP // 2)) % LANES, 1
                     )
                     value = jnp.where(edge, turned, value)
-                full[p, pl.ds(at, SUB)] = value
+                v_ref[p, pl.ds(at, SUB)] = value
                 home[first] = home[first] + value * q[second]
         for k in range(own):
             home_ref[k, pl.ds(at, SUB)] = o_ref[k, pl.ds(at, SUB)] - step_size * home[k]
-        copy_out(r).start()
         return carry
 
     lax.fori_loop(0, rows // SUB, merge, 0, unroll=4)
-
-    def finished(r, carry):
-        copy_out(r).wait()
-        return carry
-
-    lax.fori_loop(0, rows // SUB, finished, 0)
 
 
 def merged(odd, inner, ends, strip_fields, orbitals, partner):
@@ -580,14 +562,37 @@
         functools.partial(merge_kernel, sides),
         out_shape=(f32(*inner.shape), f32(*orbitals.shape)),
         in_specs=[SMEM] + [VMEM] * 5,
-        out_specs=(ANY, VMEM),
-        scratch_shapes=[
-            pltpu.VMEM(inner.shape, jnp.float32),
-            pltpu.SemaphoreType.DMA((rows // SUB,)),
-        ],
-        compiler_params=params(),
+        out_specs=(VMEM, VMEM),
+        compiler_params=params(),
+        cost_estimate=cost(1.2),
         name="merge",
     )(odd, inner, ends, strip_fields, orbitals, partner)
+
+
+def write_kernel(v_ref, out_ref, sems):
+    parts = sems.shape[0]
+    size = v_ref.shape[0] // parts
+    copies = []
+    for k in range(parts):
+        part = pl.ds(k * size, size)
+        copies.append(pltpu.make_async_copy(v_ref.at[part], out_ref.at[part], sems.at[k]))
+    for copy in copies:
+        copy.start()
+    for copy in copies:
+        copy.wait()
+
+
+def written(fields):
+    return pl.pallas_call(
+        write_kernel,
+        out_shape=f32(*fields.shape),
+        in_specs=[ANY],
+        out_specs=ANY,
+        scratch_shapes=[pltpu.SemaphoreType.DMA((4,))],
+        compiler_params=params(),
+        cost_estimate=cost(1.2),
+        name="write",
+    )(fields)
 
 
 def norm_kernel(odd_ref, home_ref, recv_ref, edge_ref, m_ref, upd_ref, norm_ref):
@@ -627,26 +632,30 @@
         in_specs=[SMEM] + [VMEM] * 4,
         out_specs=(VMEM, VMEM),
         compiler_params=params(),
+        cost_estimate=cost(0.7),
         name="partial_norms",
     )(odd, home, received, edge_terms, metric)
 
 
-def scale_kernel(cells, upd_ref, norm_ref, other_ref, out_ref):
+def scale_kernel(cells, upd_ref, *refs):
+    out_ref = refs[-1]
+    sums = functools.reduce(lambda a, b: a + b, [ref[...] for ref in refs[:-1]])
     for k in range(upd_ref.shape[0]):
-        total = norm_ref[k : k + 1] + other_ref[k : k + 1]
+        total = sums[k : k + 1]
         norm = jnp.sum(total, axis=1, keepdims=True)
         out_ref[k] = upd_ref[k] * jnp.sqrt(cells / norm)
 
 
-def rescaled(updated, norms, others, cells):
+def rescaled(updated, norms, cells):
     return pl.pallas_call(
         functools.partial(scale_kernel, float(cells)),
         out_shape=f32(*updated.shape),
-        in_specs=[VMEM] * 3,
+        in_specs=[VMEM] * (1 + len(norms)),
         out_specs=VMEM,
         compiler_params=params(),
+        cost_estimate=cost(0.8),
         name="rescaled",
-    )(updated, norms, others)
+    )(updated, *norms)
 
 
 def shifted(value, axis, by):
@@ -670,10 +679,9 @@
 
 
 def norm_hops(gx, gy):
-    hops = [[(i, i ^ (1 << k)) for i in range(gx * gy)] for k in range(gy.bit_length() - 1)]
-    for k in range(gx.bit_length() - 1):
-        hops.append([(i, i ^ (gy << k) ^ 1) for i in range(gx * gy)])
-    return hops
+    along = [[(i, i ^ (1 << k)) for i in range(gx * gy)] for k in range(gy.bit_length() - 1)]
+    across = [[(i, i ^ (gy * k) ^ 1) for i in range(gx * gy)] for k in range(1, gx)]
+    return along, across
 
 
 def by_count(counts):
@@ -693,22 +701,22 @@
     order = by_count(sweep_counts)
     col_swaps = [p for p in pair_swaps(gy) if p]
     row_swaps = [row_swap(p, gx, gy) for p in pair_swaps(gx)]
-    half = potentials.shape[0] // GROUP // 2
+    groups = potentials.shape[0] // GROUP
 
     partner = shifted(orbitals, "orb", 1)
-    pay_a, pay_b = row_payloads(odd, orbitals, potentials, metric, coefficients)
+    *ready, edges, pay_a, pay_b = prepare(odd, orbitals, potentials, metric[None], coefficients)
     rows_a = lax.ppermute(pay_a, ("gx", "gy"), row_swaps[0])
-    ready = prepare(odd, potentials, orbitals, metric, coefficients)
-    pay_b, ready = lax.optimization_barrier((pay_b, ready))
     rows_b = lax.ppermute(pay_b, ("gx", "gy"), row_swaps[1])
-    inner = interior(half, 0, False, odd, sweep_counts, order, ready, partner)
+    inner = interior(1, 0, False, odd, sweep_counts, order, ready, partner)
     rows_a, rows_b, inner = lax.optimization_barrier((rows_a, rows_b, inner))
     beside = jnp.concatenate([rows_a[:own], rows_b[:own]], 0)
     partner_rows = shifted(beside, "orb", 1)
-    inner, back = interior(half, half, True, odd, sweep_counts, order, ready, partner, *inner)
+    inner, back = interior(
+        groups - 1, 1, True, odd, sweep_counts, order, ready, partner, *inner
+    )
     partner_rows, inner, back = lax.optimization_barrier((partner_rows, inner, back))
     early = shifted(back, "orb", -1)
-    edges = tall_edges(odd, ready[4], rows_a, rows_b, partner_rows, partner)
+    edges = tall_edges(odd, edges, rows_a, rows_b, partner_rows, partner)
     received = [lax.ppermute(edges, "gy", swap) for swap in col_swaps]
     ends, band_back = bands(
         odd, sweep_counts, order, potentials, orbitals, partner, metric, coefficients,
@@ -718,12 +726,12 @@
     edge_terms = shifted(edge_back, "orb", -1)
     fields, home = merged(odd, inner, ends, strip_fields, orbitals, partner)
     updated, norms = partial_norms(odd, home, early, edge_terms, metric)
-    hops = norm_hops(gx, gy)
-    for at, hop in enumerate(hops):
-        other = lax.ppermute(norms, ("gx", "gy"), hop)
-        if at < len(hops) - 1:
-            norms = norms + other
-    return (rescaled(updated, norms, other, rows * lanes * gx * gy), fields)
+    norms, fields = lax.optimization_barrier((norms, fields))
+    along, across = norm_hops(gx, gy)
+    for hop in along:
+        norms = norms + lax.ppermute(norms, ("gx", "gy"), hop)
+    norms = [norms] + [lax.ppermute(norms, ("gx", "gy"), hop) for hop in across]
+    return (rescaled(updated, norms, rows * lanes * gx * gy), written(fields))
 
 
 def solution(mesh):

time: 43.7 us -> 42.3 us (0.968)
  local copies, waits for them, and re-layouts: 3.75 us -> 0.04 us
  waiting for transfers between devices: 5.48 us -> 8.15 us
  Pallas kernels: 20.2 us -> 19.4 us
    ppermute x4, waiting for transfers between devices: 0.78 us -> 4.58 us  [shifted(): lax.ppermute(value, axis, [(i, (i + by) % size) for i in range(size)])]
    unnamed x16 -> x10, local copies, waits for them, and re-layouts: 3.74 us -> 0.03 us
    ppermute x3 -> x4, waiting for transfers between devices: 4.69 us -> 3.56 us  [the longest x3 2.41 us: local(): norms = [norms] + [lax.ppermute(norms, ('gx', 'gy'), hop) for hop in across]]
    pallas_call x2, Pallas kernels: 2.91 us -> 3.98 us  [the longest x1 2.99 us: prepare(): pl.pallas_call(prepare_kernel, out_shape=(f32(pairs, count, SUB, lanes),...]
    pallas_call x1, Pallas kernels: 1.96 us -> 1.09 us  [merged(): pl.pallas_call(functools.partial(merge_kernel, sides), out_shape=(f32(*in...]
    pallas_call x2, Pallas kernels: 7.42 us -> 6.71 us  [interior(): pl.pallas_call(functools.partial(interior_kernel, groups, before, last),...]
    ppermute x3 -> x4, starting transfers between devices: 4.14 us -> 4.15 us  [the longest x3 4.08 us: local(): norms = [norms] + [lax.ppermute(norms, ('gx', 'gy'), hop) for hop in across]]
  transfers between devices with their start and end apart: 10 -> 11, of which waited for: 4 -> 4; matrix products, arithmetic and copies ran while one was open for 1% -> 1% of each run, Pallas kernels for 41% -> 41%
where the time goes in v5:
time: 42.3 us; the launch traced here: 42 us
  Pallas kernels  19.4 us (46%)
  starting transfers between devices  13.2 us (31%)
  waiting for transfers between devices  8.15 us (19%)
  between operations  0.83 us (2%)
    ppermute x4, starting transfers between devices, shifted(): lax.ppermute(value, axis, [(i, (i + by) % size) for i in range(size)])  7.31 us
    pallas_call x2, Pallas kernels, interior(): pl.pallas_call(functools.partial(interior_kernel, groups, before, last),...  6.71 us
    ppermute x4, waiting for transfers between devices, shifted(): lax.ppermute(value, axis, [(i, (i + by) % size) for i in range(size)])  4.58 us
    ppermute x3, starting transfers between devices, local(): norms = [norms] + [lax.ppermute(norms, ('gx', 'gy'), hop) for hop in across]  4.08 us
    pallas_call x1, Pallas kernels, prepare(): pl.pallas_call(prepare_kernel, out_shape=(f32(pairs, count, SUB, lanes),...  2.99 us
    pallas_call x1, Pallas kernels, strips(): pl.pallas_call(functools.partial(strips_kernel, sides), out_shape=(f32(ba...  2.81 us
    pallas_call x1, Pallas kernels, bands(): pl.pallas_call(bands_kernel, out_shape=(f32(pairs, 2, SUB, lanes), f32(2...  2.58 us
    ppermute x3, waiting for transfers between devices, local(): norms = [norms] + [lax.ppermute(norms, ('gx', 'gy'), hop) for hop in across]  2.41 us
  transfers between devices with their start and end apart: 11, of which 4 were waited for; matrix products, arithmetic and copies ran while one was open for 1% of the time, Pallas kernels for 41%

profile of v5, /device:TPU:0, one launch (start us, length us, event | category | flops | bytes accessed | tf_op | source)
XLA Modules:
  0.0 42.0 jit_solution(2391545280777397138)
XLA Ops:
  0.6 3.0 %collective-permute-start.2 = (f32[4,128,128]{2,1,0:T(8,128)}, f32[4,128,128]{2,1,0:T(8,128)S(1)}, u32[]{:S(2)}, u32[]{:S(2)}) collective-permute-start(f32[4,128,128]{2,1,0:T(8,128)} %o_ref.3), channel_id=1, source_target_pairs={{0,8},{8,16},{16,24},{24,0},{1,9},{9,17},{17,25},{25,1},{2,10},{10... | collective-permute-start | bytes 786440 | tf_op jit(solution)/shard_map/ppermute | solution.py:663
  3.6 0.1 pad_add_fusion.odd_ref
  3.7 3.0 %prepare.1 = (f32[16,16,8,128]{3,2,1,0:T(8,128)S(1)}, f32[4,16,8,128]{3,2,1,0:T(8,128)S(1)}, f32[4,16,8,128]{3,2,1,0:T(8,128)S(1)}, f32[5,16,8,128]{3,2,1,0:T(8,...) custom-call(s32[3]{0:T(128)S(1)} %pad_add_fusion.odd_ref, ...), custom_call_target="tpu_custom_call" | custom-call | bytes 7400000 | tf_op jit(solution)/shard_map/prepare/pallas_call | solution.py:217
  6.7 0.0 copy-start.4
  6.7 1.6 %collective-permute-start = (f32[26,8,128]{2,1,0:T(8,128)S(1)}, f32[26,8,128]{2,1,0:T(8,128)S(1)}, u32[]{:S(2)}, u32[]{:S(2)}) collective-permute-start(f32[26,8,128]{2,1,0:T(8,128)S(1)} %get-tuple-element.30), channel_id=1, source_target_pairs={{0,2},{1,3},{2,0},{3,1},{4,6},{5,7},{6,4},{7,5},{8,10},{9,11},{10,... | collective-permute-start | bytes 319496 | tf_op jit(solution)/shard_map/ppermute | solution.py:708
  8.4 0.2 convert_reduce_fusion
  8.5 0.1 select_reduce_fusion.by_ref
  8.7 2.4 %collective-permute-done.2.refs_4_.p_ref = f32[4,128,128]{2,1,0:T(8,128)S(1)} collective-permute-done((f32[4,128,128]{2,1,0:T(8,128)}, f32[4,128,128]{2,1,0:T(8,128)S(1)}, u32[]{:S(2)}, u32[]{:S(2)}) %collective-permute-start.2) | collective-permute-done | bytes 262176 | tf_op jit(solution)/shard_map/ppermute | solution.py:663
  11.1 2.2 %interior0.1 = (f32[16,128,128]{2,1,0:T(8,128)S(1)}, f32[4,16,8,128]{3,2,1,0:T(8,128)S(1)}) custom-call(s32[3]{0:T(128)S(1)} %pad_add_fusion.odd_ref, s32[16]{0:T(128)S(1)} %copy-done.4, s32[16]{0:T(128)S(1)} %select_reduce_fusion.by_ref, f32[16,16,8,128]{3,2,1,0:T(8,128)S(1)} %get-tuple-element.32.refs_0_, f32[4,16,8,128]{3,2,1,0:T(8,128)S(1)} %get-tuple-element.33.refs_1_, ...), custom_call_target="tpu_custom_call" | custom-call | bytes 6660000 | tf_op jit(solution)/shard_map/interior0/pallas_call | solution.py:286
  13.3 0.0 collective-permute-done.1.rb_ref
  13.4 0.8 %collective-permute-start.3 = (f32[8,8,128]{2,1,0:T(8,128)S(1)}, f32[8,8,128]{2,1,0:T(8,128)S(1)}, u32[]{:S(2)}, u32[]{:S(2)}) collective-permute-start(f32[8,8,128]{2,1,0:T(8,128)S(1)} %pad_maximum_fusion), channel_id=1, source_target_pairs={{0,8},{8,16},{16,24},{24,0},{1,9},{9,17},{17,25},{25,1},{2,10},{10... | collective-permute-start | bytes 98312 | tf_op jit(solution)/shard_map/ppermute | solution.py:663
  14.2 4.5 %interior1.1 = (f32[16,128,128]{2,1,0:T(8,128)S(1)}, f32[4,128,128]{2,1,0:T(8,128)S(1)}) custom-call(s32[3]{0:T(128)S(1)} %pad_add_fusion.odd_ref, s32[16]{0:T(128)S(1)} %copy-done.4, s32[16]{0:T(128)S(1)} %select_reduce_fusion.by_ref, f32[16,16,8,128]{3,2,1,0:T(8,128)S(1)} %get-tuple-element.32.refs_0_, f32[4,16,8,128]{3,2,1,0:T(8,128)S(1)} %get-tuple-element.33.refs_1_, ...), custom_call_target="tpu_custom_call" | custom-call | bytes 19980000 | tf_op jit(solution)/shard_map/interior1/pallas_call | solution.py:286
  18.7 0.0 copy-start
  18.7 0.0 copy-start.1
  18.8 0.0 copy-start.3
  18.8 0.7 %tall_edges.1.e_ref = f32[8,144,128]{2,1,0:T(8,128)S(1)} custom-call(s32[3]{0:T(128)S(1)} %pad_add_fusion.odd_ref, f32[7,128,128]{2,1,0:T(8,128)S(1)} %get-tuple-element.48.e_ref, f32[26,8,128]{2,1,0:T(8,128)S(1)} %collective-permute-done.ra_ref, f32[26,8,128]{2,1,0:T(8,128)S(1)} %collective-permute-done.1.rb_ref, ...), custom_call_target="tpu_custom_call" | custom-call | bytes 2590000 | tf_op jit(solution)/shard_map/tall_edges/pallas_call | solution.py:323
  19.5 0.1 collective-permute-start.4
  19.6 2.6 %collective-permute-start.5 = (f32[4,128,128]{2,1,0:T(8,128)S(1)}, f32[4,128,128]{2,1,0:T(8,128)S(1)}, u32[]{:S(2)}, u32[]{:S(2)}) collective-permute-start(f32[4,128,128]{2,1,0:T(8,128)S(1)} %get-tuple-element.51), channel_id=1, source_target_pairs={{0,24},{8,0},{16,8},{24,16},{1,25},{9,1},{17,9},{25,17},{2,26},{10... | collective-permute-start | bytes 786440 | tf_op jit(solution)/shard_map/ppermute | solution.py:663
  22.2 2.6 %bands.1 = (f32[16,2,8,128]{3,2,1,0:T(8,128)S(1)}, f32[8,8,128]{2,1,0:T(8,128)S(1)}) custom-call(s32[3]{0:T(128)S(1)} %pad_add_fusion.odd_ref, s32[16]{0:T(128)S(1)} %copy-done.4, s32[16]{0:T(128)S(1)} %select_reduce_fusion.by_ref, f32[16,128,128]{2,1,0:T(8,128)S(1)} %copy-done, f32[4,128,128]{2,1,0:T(8,128)S(1)} %copy-done.1, ...), custom_call_target="tpu_custom_call" | custom-call | bytes 9250000 | tf_op jit(solution)/shard_map/bands/pallas_call | solution.py:403
  24.8 2.8 %strips.1 = (f32[12,8,128]{2,1,0:T(8,128)S(1)}, f32[4,144,128]{2,1,0:T(8,128)S(1)}) custom-call(s32[3]{0:T(128)S(1)} %pad_add_fusion.odd_ref, s32[16]{0:T(128)S(1)} %copy-done.4, f32[8,8,128]{2,1,0:T(8,128)S(1)} %get-tuple-element.47.rows_ref, f32[8,144,128]{2,1,0:T(8,128)S(1)} %tall_edges.1.e_ref, f32[8,144,128]{2,1,0:T(8,128)S(1)} %collective-permute-done.4.refs_0_), custom_call_target="tpu_custom_call" | custom-call | bytes 10730000 | tf_op jit(solution)/shard_map/strips/pallas_call | solution.py:503
  27.6 0.9 %collective-permute-start.6 = (f32[12,8,128]{2,1,0:T(8,128)S(1)}, f32[12,8,128]{2,1,0:T(8,128)S(1)}, u32[]{:S(2)}, u32[]{:S(2)}) collective-permute-start(f32[12,8,128]{2,1,0:T(8,128)S(1)} %get-tuple-element.52), channel_id=1, source_target_pairs={{0,24},{8,0},{16,8},{24,16},{1,25},{9,1},{17,9},{25,17},{2,26},{10... | collective-permute-start | bytes 147464 | tf_op jit(solution)/shard_map/ppermute | solution.py:663
  28.5 1.1 %merge.1 = (f32[16,128,128]{2,1,0:T(8,128)S(1)}, f32[4,128,128]{2,1,0:T(8,128)S(1)}) custom-call(s32[3]{0:T(128)S(1)} %pad_add_fusion.odd_ref, f32[16,128,128]{2,1,0:T(8,128)S(1)} %get-tuple-element.44.inner_ref, f32[16,2,8,128]{3,2,1,0:T(8,128)S(1)} %get-tuple-element.46.ends_ref, f32[4,144,128]{2,1,0:T(8,128)S(1)} %get-tuple-element.49.sv_ref, ...), custom_call_target="tpu_custom_call" | custom-call | bytes 4440000 | tf_op jit(solution)/shard_map/merge/pallas_call | solution.py:561
  29.6 2.1 %collective-permute-done.6.edge_ref = f32[12,8,128]{2,1,0:T(8,128)S(1)} collective-permute-done((f32[12,8,128]{2,1,0:T(8,128)S(1)}, f32[12,8,128]{2,1,0:T(8,128)S(1)}, u32[]{:S(2)}, u32[]{:S(2)}) %collective-permute-start.6) | collective-permute-done | bytes 49184 | tf_op jit(solution)/shard_map/ppermute | solution.py:663
  31.7 0.7 %partial_norms.1 = (f32[4,128,128]{2,1,0:T(8,128)S(1)}, f32[8,128]{1,0:T(8,128)S(1)}) custom-call(s32[3]{0:T(128)S(1)} %pad_add_fusion.odd_ref, f32[4,128,128]{2,1,0:T(8,128)S(1)} %get-tuple-element.50.home_ref, f32[4,128,128]{2,1,0:T(8,128)S(1)} %collective-permute-done.5.recv_ref, f32[12,8,128]{2,1,0:T(8,128)S(1)} %collective-permute-done.6.edge_ref, ...), custom_call_target="tpu_custom_call" | custom-call | bytes 2590000 | tf_op jit(solution)/shard_map/partial_norms/pallas_call | solution.py:629
  32.5 0.1 collective-permute-start.7
  32.5 1.2 %collective-permute-done.7 = f32[8,128]{1,0:T(8,128)S(1)} collective-permute-done((f32[8,128]{1,0:T(8,128)S(1)}, f32[8,128]{1,0:T(8,128)S(1)}, u32[]{:S(2)}, u32[]{:S(2)}) %collective-permute-start.7) | collective-permute-done | bytes 4128 | tf_op jit(solution)/shard_map/ppermute | solution.py:732
  33.7 3.6 %collective-permute-start.10 = (f32[8,128]{1,0:T(8,128)S(1)}, f32[8,128]{1,0:T(8,128)S(1)}, u32[]{:S(2)}, u32[]{:S(2)}) collective-permute-start(f32[8,128]{1,0:T(8,128)S(1)} %add.12.refs_0_), channel_id=1, source_target_pairs={{0,7},{1,6},{2,5},{3,4},{4,3},{5,2},{6,1},{7,0},{8,15},{9,14},{10,... | collective-permute-start | bytes 12296 | tf_op jit(solution)/shard_map/ppermute | solution.py:733
  37.3 0.5 %collective-permute-start.8 = (f32[8,128]{1,0:T(8,128)S(1)}, f32[8,128]{1,0:T(8,128)S(1)}, u32[]{:S(2)}, u32[]{:S(2)}) collective-permute-start(f32[8,128]{1,0:T(8,128)S(1)} %add.12.refs_0_), channel_id=1, source_target_pairs={{0,3},{1,2},{2,1},{3,0},{4,7},{5,6},{6,5},{7,4},{8,11},{9,10},{10,... | collective-permute-start | bytes 12296 | tf_op jit(solution)/shard_map/ppermute | solution.py:733
  37.8 1.0 %write.1 = f32[16,128,128]{2,1,0:T(8,128)} custom-call(f32[16,128,128]{2,1,0:T(8,128)S(1)} %get-tuple-element.57.v_ref), custom_call_target="tpu_custom_call" | custom-call | bytes 4440000 | tf_op jit(solution)/shard_map/write/pallas_call | solution.py:586
  38.8 0.0 collective-permute-done.10.refs_3_
  38.8 2.4 %collective-permute-done.9.refs_2_ = f32[8,128]{1,0:T(8,128)S(1)} collective-permute-done((f32[8,128]{1,0:T(8,128)S(1)}, f32[8,128]{1,0:T(8,128)S(1)}, u32[]{:S(2)}, u32[]{:S(2)}) %collective-permute-start.9) | collective-permute-done | bytes 4128 | tf_op jit(solution)/shard_map/ppermute | solution.py:733
  41.2 0.8 %rescaled.1 = f32[4,128,128]{2,1,0:T(8,128)} custom-call(f32[4,128,128]{2,1,0:T(8,128)S(1)} %get-tuple-element.53.upd_ref, f32[8,128]{1,0:T(8,128)S(1)} %add.12.refs_0_, f32[8,128]{1,0:T(8,128)S(1)} %collective-permute-done.8.refs_1_, f32[8,128]{1,0:T(8,128)S(1)} %collective-permute-done.9.refs_2_, f32[8,128]{1,0:T(8,128)S(1)} %collective-permute-done.10.refs_3_), custom_call_target="tpu_custom_call" | custom-call | bytes 2960000 | tf_op jit(solution)/shard_map/rescaled/pallas_call | solution.py:650
  (17 shorter events, 0.0 us)
Async XLA Ops:
  0.6 10.5 %collective-permute-start.2 = (f32[4,128,128]{2,1,0:T(8,128)}, f32[4,128,128]{2,1,0:T(8,128)S(1)}, u32[]{:S(2)}, u32[]{:S(2)}) collective-permute-start(f32[4,128,128]{2,1,0:T(8,128)} %o_ref.3), channel_id=1, source_target_pairs={{0,8},{8,16},{16,24},{24,0},{1,9},{9,17},{17,25},{25,1},{2,10},{10... | collective-permute-start | bytes 786440 | tf_op jit(solution)/shard_map/ppermute | solution.py:663
  6.7 1.7 %copy-start.4 = (s32[16]{0:T(128)S(1)}, s32[16]{0:T(128)}, u32[]{:S(2)}) copy-start(s32[16]{0:T(128)} %n_ref.7) | copy-start | bytes 196
  6.7 6.6 %collective-permute-start = (f32[26,8,128]{2,1,0:T(8,128)S(1)}, f32[26,8,128]{2,1,0:T(8,128)S(1)}, u32[]{:S(2)}, u32[]{:S(2)}) collective-permute-start(f32[26,8,128]{2,1,0:T(8,128)S(1)} %get-tuple-element.30), channel_id=1, source_target_pairs={{0,2},{1,3},{2,0},{3,1},{4,6},{5,7},{6,4},{7,5},{8,10},{9,11},{10,... | collective-permute-start | bytes 319496 | tf_op jit(solution)/shard_map/ppermute | solution.py:708
  8.3 5.0 %collective-permute-start.1 = (f32[26,8,128]{2,1,0:T(8,128)S(1)}, f32[26,8,128]{2,1,0:T(8,128)S(1)}, u32[]{:S(2)}, u32[]{:S(2)}) collective-permute-start(f32[26,8,128]{2,1,0:T(8,128)S(1)} %get-tuple-element.31), channel_id=1, source_target_pairs={{0,1},{1,0},{2,4},{3,5},{4,2},{5,3},{6,7},{7,6},{8,9},{9,8},{10,12... | collective-permute-start | bytes 319496 | tf_op jit(solution)/shard_map/ppermute | solution.py:709
  13.4 5.3 %collective-permute-start.3 = (f32[8,8,128]{2,1,0:T(8,128)S(1)}, f32[8,8,128]{2,1,0:T(8,128)S(1)}, u32[]{:S(2)}, u32[]{:S(2)}) collective-permute-start(f32[8,8,128]{2,1,0:T(8,128)S(1)} %pad_maximum_fusion), channel_id=1, source_target_pairs={{0,8},{8,16},{16,24},{24,0},{1,9},{9,17},{17,25},{25,1},{2,10},{10... | collective-permute-start | bytes 98312 | tf_op jit(solution)/shard_map/ppermute | solution.py:663
  14.2 8.0 %copy-start.2 = (f32[5,128,128]{2,1,0:T(8,128)S(1)}, f32[5,128,128]{2,1,0:T(8,128)}, u32[]{:S(2)}) copy-start(f32[5,128,128]{2,1,0:T(8,128)} %c_ref.1) | copy-start | bytes 983044
  18.7 3.5 %copy-start = (f32[16,128,128]{2,1,0:T(8,128)S(1)}, f32[16,128,128]{2,1,0:T(8,128)}, u32[]{:S(2)}) copy-start(f32[16,128,128]{2,1,0:T(8,128)} %v_ref.1) | copy-start | bytes 3145732
  18.7 3.4 %copy-start.1 = (f32[4,128,128]{2,1,0:T(8,128)S(1)}, f32[4,128,128]{2,1,0:T(8,128)}, u32[]{:S(2)}) copy-start(f32[4,128,128]{2,1,0:T(8,128)} %o_ref.3) | copy-start | bytes 786436
  18.8 3.4 %copy-start.3 = (f32[128,128]{1,0:T(8,128)S(1)}, f32[128,128]{1,0:T(8,128)}, u32[]{:S(2)}) copy-start(f32[128,128]{1,0:T(8,128)} %m_ref.3) | copy-start | bytes 196612
  19.5 5.3 %collective-permute-start.4 = (f32[8,144,128]{2,1,0:T(8,128)S(1)}, f32[8,144,128]{2,1,0:T(8,128)S(1)}, u32[]{:S(2)}, u32[]{:S(2)}) collective-permute-start(f32[8,144,128]{2,1,0:T(8,128)S(1)} %tall_edges.1.e_ref), channel_id=1, source_target_pairs={{0,1},{1,0},{2,3},{3,2},{4,5},{5,4},{6,7},{7,6},{8,9},{9,8},{10,11... | collective-permute-start | bytes 1769480 | tf_op jit(solution)/shard_map/ppermute | solution.py:720
  19.6 10.0 %collective-permute-start.5 = (f32[4,128,128]{2,1,0:T(8,128)S(1)}, f32[4,128,128]{2,1,0:T(8,128)S(1)}, u32[]{:S(2)}, u32[]{:S(2)}) collective-permute-start(f32[4,128,128]{2,1,0:T(8,128)S(1)} %get-tuple-element.51), channel_id=1, source_target_pairs={{0,24},{8,0},{16,8},{24,16},{1,25},{9,1},{17,9},{25,17},{2,26},{10... | collective-permute-start | bytes 786440 | tf_op jit(solution)/shard_map/ppermute | solution.py:663
  27.6 4.1 %collective-permute-start.6 = (f32[12,8,128]{2,1,0:T(8,128)S(1)}, f32[12,8,128]{2,1,0:T(8,128)S(1)}, u32[]{:S(2)}, u32[]{:S(2)}) collective-permute-start(f32[12,8,128]{2,1,0:T(8,128)S(1)} %get-tuple-element.52), channel_id=1, source_target_pairs={{0,24},{8,0},{16,8},{24,16},{1,25},{9,1},{17,9},{25,17},{2,26},{10... | collective-permute-start | bytes 147464 | tf_op jit(solution)/shard_map/ppermute | solution.py:663
  32.5 1.2 %collective-permute-start.7 = (f32[8,128]{1,0:T(8,128)S(1)}, f32[8,128]{1,0:T(8,128)S(1)}, u32[]{:S(2)}, u32[]{:S(2)}) collective-permute-start(f32[8,128]{1,0:T(8,128)S(1)} %get-tuple-element.56), channel_id=1, source_target_pairs={{0,1},{1,0},{2,3},{3,2},{4,5},{5,4},{6,7},{7,6},{8,9},{9,8},{10,11... | collective-permute-start | bytes 12296 | tf_op jit(solution)/shard_map/ppermute | solution.py:732
  33.7 5.1 %collective-permute-start.10 = (f32[8,128]{1,0:T(8,128)S(1)}, f32[8,128]{1,0:T(8,128)S(1)}, u32[]{:S(2)}, u32[]{:S(2)}) collective-permute-start(f32[8,128]{1,0:T(8,128)S(1)} %add.12.refs_0_), channel_id=1, source_target_pairs={{0,7},{1,6},{2,5},{3,4},{4,3},{5,2},{6,1},{7,0},{8,15},{9,14},{10,... | collective-permute-start | bytes 12296 | tf_op jit(solution)/shard_map/ppermute | solution.py:733
  37.3 3.9 %collective-permute-start.9 = (f32[8,128]{1,0:T(8,128)S(1)}, f32[8,128]{1,0:T(8,128)S(1)}, u32[]{:S(2)}, u32[]{:S(2)}) collective-permute-start(f32[8,128]{1,0:T(8,128)S(1)} %add.12.refs_0_), channel_id=1, source_target_pairs={{0,5},{1,4},{2,7},{3,6},{4,1},{5,0},{6,3},{7,2},{8,13},{9,12},{10,... | collective-permute-start | bytes 12296 | tf_op jit(solution)/shard_map/ppermute | solution.py:733
  37.3 3.9 %collective-permute-start.8 = (f32[8,128]{1,0:T(8,128)S(1)}, f32[8,128]{1,0:T(8,128)S(1)}, u32[]{:S(2)}, u32[]{:S(2)}) collective-permute-start(f32[8,128]{1,0:T(8,128)S(1)} %add.12.refs_0_), channel_id=1, source_target_pairs={{0,3},{1,2},{2,1},{3,0},{4,7},{5,6},{6,5},{7,4},{8,11},{9,10},{10,... | collective-permute-start | bytes 12296 | tf_op jit(solution)/shard_map/ppermute | solution.py:733

commit v6 on v5

--- a/solution.py
+++ b/solution.py
@@ -22,10 +22,9 @@
 GROUP = 4
 BANDS = 8
 AHEAD = 16
-VMEM_LIMIT = 40 * 1024 * 1024
+VMEM_LIMIT = 16 * 1024 * 1024
 
 VMEM = pl.BlockSpec(memory_space=pltpu.VMEM)
-SMEM = pl.BlockSpec(memory_space=pltpu.SMEM)
 ANY = pl.BlockSpec(memory_space=pl.ANY)
 HBM = pl.BlockSpec(memory_space=pltpu.HBM)
 
@@ -42,6 +41,12 @@
     return pl.CostEstimate(
         flops=0, bytes_accessed=int(microseconds * 3.7e6), transcendentals=0
     )
+
+
+def place():
+    row, col = lax.axis_index("gx"), lax.axis_index("gy")
+    inside = (row > 0) & (row < lax.axis_size("gx") - 1)
+    return row % 2, col % 2, inside
 
 
 def lane_of(rows=SUB):
@@ -153,7 +158,7 @@
     return west, east, dead
 
 
-def prepare_kernel(odd_ref, o_hbm, v_hbm, m_hbm, c_hbm, *refs):
+def prepare_kernel(by_in, steps_in, o_hbm, v_hbm, m_hbm, c_hbm, by_ref, steps_ref, *refs):
     vs_ref, os_ref, om_ref, cf_ref, e_ref, pay_a, pay_b, o_ref, v_ref, m_ref, c_ref, sems = refs
     own, rows, _ = o_ref.shape
     pairs = v_ref.shape[0]
@@ -168,8 +173,10 @@
     ]
     for copy in copies:
         copy.start()
-
-    starts = [(1 - odd_ref[0]) * (rows - HALO), odd_ref[0] * (rows - HALO)]
+    by_ref[...] = by_in[...]
+    steps_ref[...] = steps_in[...]
+
+    starts = [(1 - place()[0]) * (rows - HALO), place()[0] * (rows - HALO)]
     starts = [pl.multiple_of(start, HALO) for start in starts]
 
     def send_rows(at, ref, index):
@@ -183,7 +190,7 @@
         send_rows(own + pairs + 1 + n, c_ref, n)
     e_ref[1 + own] = packed([m_ref[0], c_ref[0], c_ref[1], c_ref[2]])
     e_ref[2 + own] = packed([c_ref[3], c_ref[4]])
-    dead = lane_masks(odd_ref[1])[2]
+    dead = lane_masks(place()[1])[2]
     metric = spread(m_ref, count, 0)
     raw = [spread(c_ref, count, n) for n in range(5)]
     weights = []
@@ -208,7 +215,7 @@
                 vs_ref[p, t] = value
 
 
-def prepare(odd, *arrays):
+def prepare(order, steps, *arrays):
     orbitals, potentials, _, coefficients = arrays
     own, rows, lanes = orbitals.shape
     pairs = potentials.shape[0]
@@ -217,51 +224,58 @@
     return pl.pallas_call(
         prepare_kernel,
         out_shape=(
+            jax.ShapeDtypeStruct(order.shape, order.dtype),
+            jax.ShapeDtypeStruct(steps.shape, steps.dtype),
             f32(pairs, count, SUB, lanes),
             f32(own, count, SUB, lanes),
             f32(own, count, SUB, lanes),
             f32(5, count, SUB, lanes),
             f32(own + 3, rows, lanes),
             *[f32(own + pairs + 1 + coefficients.shape[0], HALO, lanes)] * 2,
+            *[f32(*a.shape) for a in arrays],
         ),
-        in_specs=[SMEM] + [HBM] * 4,
-        out_specs=(VMEM,) * 7,
-        scratch_shapes=[pltpu.VMEM(a.shape, jnp.float32) for a in arrays]
-        + [pltpu.SemaphoreType.DMA((3 + own,))],
+        in_specs=[VMEM] * 2 + [HBM] * 4,
+        out_specs=(VMEM,) * 13,
+        scratch_shapes=[pltpu.SemaphoreType.DMA((3 + own,))],
         compiler_params=params(),
         cost_estimate=cost(2.0),
         name="prepare",
-    )(odd, *inputs)
-
-
-def interior_kernel(groups, before, last, odd_ref, n_ref, by_ref, *refs):
+    )(order, steps, *inputs)
+
+
+def interior_kernel(groups, before, last, by_any, *refs):
     vs_ref, os_ref, om_ref, cf_ref, p_ref = refs[:5]
-    out_ref, back_ref, back, qs, sr, va, vb = refs[-7:]
+    out_ref, back_ref, back, qs, sr, va, vb, by_ref, sem = refs[-9:]
     own, count = om_ref.shape[:2]
-    masks = lane_masks(odd_ref[1])
+    fetch = pltpu.make_async_copy(by_any, by_ref, sem)
+    fetch.start()
+    masks = lane_masks(place()[1])
+    for k in range(own):
+        for t, value in enumerate(spread(p_ref, count, k)):
+            qs[k, t] = value
     if before:
         earlier, back_before = refs[5:7]
-
-        def keep(k, carry):
-            out_ref[by_ref[k]] = earlier[by_ref[k]]
-            return carry
-
-        lax.fori_loop(0, before * GROUP, keep, 0)
         back[...] = back_before[...]
     else:
         back[...] = jnp.zeros_like(back)
-    for k in range(own):
-        for t, value in enumerate(spread(p_ref, count, k)):
-            qs[k, t] = value
+    fetch.wait()
+    if before:
+
+        def keep(k, carry):
+            out_ref[by_ref[1, k]] = earlier[by_ref[1, k]]
+            return carry
+
+        lax.fori_loop(0, before * GROUP, keep, 0)
 
     def group(g, carry):
-        pairs = [by_ref[g * GROUP + k] for k in range(GROUP)]
+        pairs = [by_ref[1, g * GROUP + k] for k in range(GROUP)]
         for k, p in enumerate(pairs):
             first, second = p // own, p % own
             for t in range(count):
                 sr[k, t] = om_ref[first, t] * qs[second, t]
                 va[k, t] = vs_ref[p, t]
-        relax([n_ref[p] for p in pairs], count, va, vb, sr, cf_ref, masks)
+        steps = [by_ref[0, g * GROUP + k] for k in range(GROUP)]
+        relax(steps, count, va, vb, sr, cf_ref, masks)
         for k, p in enumerate(pairs):
             first, second = p // own, p % own
             spread_store(out_ref, [va[k, t] for t in range(count)], p)
@@ -277,7 +291,7 @@
             back_ref[k] = back[k]
 
 
-def interior(groups, before, last, odd, counts, order, ready, partner, *earlier):
+def interior(groups, before, last, order, ready, partner, *earlier):
     pairs, count, _, lanes = ready[0].shape
     own, rows, _ = partner.shape
     four = pltpu.VMEM((GROUP, count, SUB, lanes), jnp.float32)
@@ -286,30 +300,49 @@
     return pl.pallas_call(
         functools.partial(interior_kernel, groups, before, last),
         out_shape=(f32(pairs, rows, lanes), back),
-        in_specs=[SMEM] * 3 + [VMEM] * (5 + len(earlier)),
+        in_specs=[ANY] + [VMEM] * (5 + len(earlier)),
         out_specs=(VMEM, VMEM),
-        scratch_shapes=[each, each, four, four, four],
+        scratch_shapes=[each, each, four, four, four]
+        + [pltpu.SMEM(order.shape, jnp.int32), pltpu.SemaphoreType.DMA],
         compiler_params=params(),
         cost_estimate=cost(1.8 * groups),
         name=f"interior{before}",
-    )(odd, counts, order, *ready[:4], partner, *earlier)
-
-
-def beyond(odd_ref, a, b):
-    low_is_a = odd_ref[0] == 1
-    b = jnp.where(odd_ref[2] == 1, b, 0.0)
+    )(order, *ready[:4], partner, *earlier)
+
+
+def row_pair_kernel(own, a_ref, b_ref, out_ref):
+    out_ref[0:own] = a_ref[0:own]
+    out_ref[own:] = b_ref[0:own]
+
+
+def row_pair(own, rows_a, rows_b):
+    return pl.pallas_call(
+        functools.partial(row_pair_kernel, own),
+        out_shape=f32(2 * own, *rows_a.shape[1:]),
+        in_specs=[VMEM] * 2,
+        out_specs=VMEM,
+        compiler_params=params(),
+        cost_estimate=cost(0.1),
+        name="row_pair",
+    )(rows_a, rows_b)
+
+
+def beyond(at, a, b):
+    low_is_a = at[0] == 1
+    b = jnp.where(at[2], b, 0.0)
     return jnp.where(low_is_a, a, b), jnp.where(low_is_a, b, a)
 
 
-def edges_kernel(odd_ref, e_ref, ra_ref, rb_ref, p2_ref, p_ref, out_ref):
+def edges_kernel(e_ref, ra_ref, rb_ref, p2_ref, p_ref, out_ref):
+    here_at = place()
     own, rows, _ = p_ref.shape
     groups = e_ref.shape[0]
     for g in range(groups):
         out_ref[g, SUB : SUB + rows] = e_ref[g]
     out_ref[groups, SUB : SUB + rows] = packed([p_ref[k] for k in range(own)])
     pairs = own * own
-    ends = [beyond(odd_ref, ra_ref[f], rb_ref[f]) for f in range(own + pairs + 6)]
-    ends += [beyond(odd_ref, p2_ref[k], p2_ref[own + k]) for k in range(own)]
+    ends = [beyond(here_at, ra_ref[f], rb_ref[f]) for f in range(own + pairs + 6)]
+    ends += [beyond(here_at, p2_ref[k], p2_ref[own + k]) for k in range(own)]
     lists = [range(own)] + [range(own * (1 + k), own * (2 + k)) for k in range(own)]
     at = own + pairs
     lists += [range(at, at + 4), range(at + 4, at + 6), range(at + 6, at + 6 + own)]
@@ -318,23 +351,26 @@
         out_ref[g, SUB + rows :] = packed([ends[f][1] for f in fields])
 
 
-def tall_edges(odd, edges, rows_a, rows_b, partner_rows, partner):
+def tall_edges(edges, rows_a, rows_b, partner_rows, partner):
     groups, rows, lanes = edges.shape
     return pl.pallas_call(
         edges_kernel,
         out_shape=f32(groups + 1, rows + 2 * SUB, lanes),
-        in_specs=[SMEM] + [VMEM] * 5,
+        in_specs=[VMEM] * 5,
         out_specs=VMEM,
         compiler_params=params(),
         cost_estimate=cost(0.7),
         name="tall_edges",
-    )(odd, edges, rows_a, rows_b, partner_rows, partner)
+    )(edges, rows_a, rows_b, partner_rows, partner)
 
 
 def bands_kernel(
-    odd_ref, n_ref, by_ref, v_ref, o_ref, p_ref, m_ref, c_ref, ra_ref, rb_ref, p2_ref,
-    out_ref, back_ref, band, cf, ms, sr, va, vb,
+    by_any, v_ref, o_ref, p_ref, m_ref, c_ref, ra_ref, rb_ref, p2_ref,
+    out_ref, back_ref, band, cf, ms, sr, va, vb, by_ref, sem,
 ):
+    fetch = pltpu.make_async_copy(by_any, by_ref, sem)
+    fetch.start()
+    here_at = place()
     own, rows, _ = o_ref.shape
     pairs = v_ref.shape[0]
     tall = 3 * SUB
@@ -347,7 +383,7 @@
         band[at, tall + 2 * SUB : 2 * tall] = ends[1]
 
     def received(f):
-        return beyond(odd_ref, ra_ref[f], rb_ref[f])
+        return beyond(here_at, ra_ref[f], rb_ref[f])
 
     def fill_pair(p, carry):
         fill(p, received(own + p), v_ref, p)
@@ -358,12 +394,12 @@
     m_at = p_at + own
     for k in range(own):
         fill(o_at + k, received(k), o_ref, k)
-        fill(p_at + k, beyond(odd_ref, p2_ref[k], p2_ref[own + k]), p_ref, k)
+        fill(p_at + k, beyond(here_at, p2_ref[k], p2_ref[own + k]), p_ref, k)
     fill(m_at, received(own + pairs), m_ref)
     for n in range(5):
         fill(m_at + 1 + n, received(own + pairs + 1 + n), c_ref, n)
 
-    masks = lane_masks(odd_ref[1])
+    masks = lane_masks(place()[1])
     metric = spread(band, count, m_at)
     raw = [spread(band, count, m_at + 1 + n) for n in range(5)]
     for t in range(count):
@@ -373,20 +409,22 @@
             cf[n, t] = scale * raw[n][t]
 
     def group(g, carry):
-        chosen = [by_ref[g * BANDS + k] for k in range(BANDS)]
+        chosen = [by_ref[1, g * BANDS + k] for k in range(BANDS)]
         for k, p in enumerate(chosen):
             o, q = spread(band, count, o_at + p // own), spread(band, count, p_at + p % own)
             v = spread(band, count, p)
             for t in range(count):
                 sr[k, t] = ms[t] * (o[t] * q[t])
                 va[k, t] = v[t]
-        relax([n_ref[p] for p in chosen], count, va, vb, sr, cf, masks)
+        steps = [by_ref[0, g * BANDS + k] for k in range(BANDS)]
+        relax(steps, count, va, vb, sr, cf, masks)
         for k, p in enumerate(chosen):
             spread_store(band, [va[k, t] for t in range(count)], p)
             out_ref[p, 0] = band[p, SUB : 2 * SUB]
             out_ref[p, 1] = band[p, tall + SUB : tall + 2 * SUB]
         return carry
 
+    fetch.wait()
     lax.fori_loop(0, pairs // BANDS, group, 0)
     for end, start in enumerate((0, rows - SUB)):
         o = [o_ref[k, start : start + SUB] for k in range(own)]
@@ -395,7 +433,7 @@
             back_ref[end * own + second] = sum(terms[1:], terms[0])
 
 
-def bands(odd, counts, order, potentials, orbitals, partner, metric, coefficients, *received):
+def bands(order, potentials, orbitals, partner, metric, coefficients, *received):
     own, rows, lanes = orbitals.shape
     pairs = potentials.shape[0]
     count = 6
@@ -403,7 +441,7 @@
     return pl.pallas_call(
         bands_kernel,
         out_shape=(f32(pairs, 2, SUB, lanes), f32(2 * own, SUB, lanes)),
-        in_specs=[SMEM] * 3 + [VMEM] * 8,
+        in_specs=[ANY] + [VMEM] * 8,
         out_specs=(VMEM, VMEM),
         scratch_shapes=[
             pltpu.VMEM((pairs + 2 * own + 6, count * SUB, lanes), jnp.float32),
@@ -412,35 +450,36 @@
             some,
             some,
             some,
+            pltpu.SMEM(order.shape, jnp.int32),
+            pltpu.SemaphoreType.DMA,
         ],
         compiler_params=params(),
         cost_estimate=cost(2.5),
         name="bands",
-    )(odd, counts, order, potentials, orbitals, partner, metric, coefficients, *received)
-
-
-def strip_place(odd_ref, side):
-    left_own = odd_ref[1] == side
+    )(order, potentials, orbitals, partner, metric, coefficients, *received)
+
+
+def strip_place(side):
+    left_own = place()[1] == side
     in_strip = jnp.where(left_own, HALO, STRIP // 2)
     in_block = jnp.where(left_own, LANES - HALO, 0)
     return left_own, in_strip, in_block
 
 
-def strips_kernel(sides, odd_ref, n_ref, rows_ref, e_ref, *refs):
+def strips_kernel(sides, n_ref, rows_ref, e_ref, *refs):
     recv = refs[:sides]
     pay_ref, sv_ref, st, cf, ms, orep, sr, va, vb, flat = refs[sides:]
-    own = n_ref.shape[0] // BLOCKS
+    own = n_ref.shape[0]
     groups, tall, _ = e_ref.shape
     rows = tall - 2 * SUB
     count = tall // SUB
     lane = lane_of()
-    block = lane // STRIP
     lead = rows_ref.shape[0]
     fold = rows // SUB // BLOCKS
     pay_ref[0:lead] = rows_ref[...]
 
     for side in range(sides):
-        left_own, in_strip, _ = strip_place(odd_ref, side)
+        left_own, in_strip, _ = strip_place(side)
         within = lane_of(tall) % STRIP
         from_own = jnp.where(left_own, within, STRIP - 1 - within) < STRIP // 2
         for g in range(groups):
@@ -464,10 +503,7 @@
         for g in range(own):
             for t, value in enumerate(spread(st, count, 1 + g)):
                 va[g, t] = value
-            n = jnp.zeros((SUB, LANES), jnp.int32)
-            for k in range(own):
-                n = jnp.where(block == k, n_ref[g * own + k], n)
-            steps.append(n)
+            steps.append(n_ref[g])
 
         def body(turn, carry):
             for s in range(2):
@@ -493,10 +529,10 @@
             pay_ref[lead + side * fold + v] = out
 
 
-def strips(odd, counts, band_back, edges, received):
+def strips(steps, band_back, edges, received):
     sides = len(received)
     groups, tall, lanes = edges.shape
-    own = counts.shape[0] // BLOCKS
+    own = steps.shape[0]
     count = tall // SUB
     fold = (tall - 2 * SUB) // SUB // BLOCKS
     each = pltpu.VMEM((own, count, SUB, lanes), jnp.float32)
@@ -506,7 +542,7 @@
             f32(band_back.shape[0] + sides * fold, SUB, lanes),
             f32(sides * own, tall, lanes),
         ),
-        in_specs=[SMEM] * 2 + [VMEM] * (2 + sides),
+        in_specs=[VMEM] * (3 + sides),
         out_specs=(VMEM, VMEM),
         scratch_shapes=[
             pltpu.VMEM((groups, tall, lanes), jnp.float32),
@@ -521,10 +557,10 @@
         compiler_params=params(),
         cost_estimate=cost(2.9),
         name="strips",
-    )(odd, counts, band_back, edges, *received)
-
-
-def merge_kernel(sides, odd_ref, inner_ref, ends_ref, sv_ref, o_ref, p_ref, v_ref, home_ref):
+    )(steps, band_back, edges, *received)
+
+
+def merge_kernel(sides, inner_ref, ends_ref, sv_ref, o_ref, p_ref, v_ref, home_ref):
     own, rows, _ = o_ref.shape
     lane = lane_of()
 
@@ -540,7 +576,7 @@
                 value = jnp.where(r == 0, ends_ref[p, 0], value)
                 value = jnp.where(r == rows // SUB - 1, ends_ref[p, 1], value)
                 for side in range(sides):
-                    right = odd_ref[1] == side
+                    right = place()[1] == side
                     edge = jnp.where(right, LANES - 1 - lane, lane) < HALO
                     turned = pltpu.roll(
                         strips[side], (-(STRIP * second + STRIP // 2)) % LANES, 1
@@ -555,18 +591,18 @@
     lax.fori_loop(0, rows // SUB, merge, 0, unroll=4)
 
 
-def merged(odd, inner, ends, strip_fields, orbitals, partner):
+def merged(inner, ends, strip_fields, orbitals, partner):
     own, rows, _ = orbitals.shape
     sides = strip_fields.shape[0] // own
     return pl.pallas_call(
         functools.partial(merge_kernel, sides),
         out_shape=(f32(*inner.shape), f32(*orbitals.shape)),
-        in_specs=[SMEM] + [VMEM] * 5,
+        in_specs=[VMEM] * 5,
         out_specs=(VMEM, VMEM),
         compiler_params=params(),
         cost_estimate=cost(1.2),
         name="merge",
-    )(odd, inner, ends, strip_fields, orbitals, partner)
+    )(inner, ends, strip_fields, orbitals, partner)
 
 
 def write_kernel(v_ref, out_ref, sems):
@@ -595,7 +631,7 @@
     )(fields)
 
 
-def norm_kernel(odd_ref, home_ref, recv_ref, edge_ref, m_ref, upd_ref, norm_ref):
+def norm_kernel(home_ref, recv_ref, edge_ref, m_ref, upd_ref, norm_ref):
     own, rows, _ = home_ref.shape
     lane = lane_of()
     fold = rows // SUB // BLOCKS
@@ -613,7 +649,7 @@
                 value = edge_ref[own + k]
             g, v = divmod(r, fold)
             for side in range(sides):
-                left_own, _, in_block = strip_place(odd_ref, side)
+                left_own, _, in_block = strip_place(side)
                 edge = jnp.where(left_own, LANES - 1 - lane, lane) < HALO
                 shift = (in_block - STRIP * k - HALO * g) % LANES
                 turned = pltpu.roll(edge_ref[lead + side * fold + v], shift, 1)
@@ -624,17 +660,17 @@
         norm_ref[k : k + 1] = jnp.sum(total, axis=0, keepdims=True)
 
 
-def partial_norms(odd, home, received, edge_terms, metric):
+def partial_norms(home, received, edge_terms, metric):
     own, _, lanes = home.shape
     return pl.pallas_call(
         norm_kernel,
         out_shape=(f32(*home.shape), f32(-(-own // SUB) * SUB, lanes)),
-        in_specs=[SMEM] + [VMEM] * 4,
+        in_specs=[VMEM] * 4,
         out_specs=(VMEM, VMEM),
         compiler_params=params(),
         cost_estimate=cost(0.7),
         name="partial_norms",
-    )(odd, home, received, edge_terms, metric)
+    )(home, received, edge_terms, metric)
 
 
 def scale_kernel(cells, upd_ref, *refs):
@@ -689,43 +725,42 @@
     more = counts[None] > counts[:, None]
     tie = (counts[None] == counts[:, None]) & (at[None] < at[:, None])
     rank = jnp.sum((more | tie).astype(jnp.int32), axis=1)
-    return jnp.sum(jnp.where(rank[None] == at[:, None], at[None], 0), axis=1)
+    chosen = (rank[None] == at[:, None])[None]
+    return jnp.sum(jnp.where(chosen, jnp.stack([counts, at])[:, None], 0), axis=2)
 
 
 def local(orbitals, potentials, coefficients, metric, sweep_counts):
     own, rows, lanes = orbitals.shape
     gx, gy = lax.axis_size("gx"), lax.axis_size("gy")
-    row_at = lax.axis_index("gx")
-    inside = (row_at > 0) & (row_at < gx - 1)
-    odd = jnp.stack([row_at % 2, lax.axis_index("gy") % 2, inside]).astype(jnp.int32)
     order = by_count(sweep_counts)
+    steps = jnp.repeat(sweep_counts.reshape(own, 1, own), STRIP, axis=2)
+    steps = jnp.broadcast_to(steps, (own, SUB, lanes))
     col_swaps = [p for p in pair_swaps(gy) if p]
     row_swaps = [row_swap(p, gx, gy) for p in pair_swaps(gx)]
     groups = potentials.shape[0] // GROUP
 
     partner = shifted(orbitals, "orb", 1)
-    *ready, edges, pay_a, pay_b = prepare(odd, orbitals, potentials, metric[None], coefficients)
+    order, steps, *ready = prepare(order, steps, orbitals, potentials, metric[None], coefficients)
+    *ready, edges, pay_a, pay_b, orbitals, potentials, metric, coefficients = ready
+    metric = metric.reshape(rows, lanes)
     rows_a = lax.ppermute(pay_a, ("gx", "gy"), row_swaps[0])
     rows_b = lax.ppermute(pay_b, ("gx", "gy"), row_swaps[1])
-    inner = interior(1, 0, False, odd, sweep_counts, order, ready, partner)
+    inner = interior(1, 0, False, order, ready, partner)
     rows_a, rows_b, inner = lax.optimization_barrier((rows_a, rows_b, inner))
-    beside = jnp.concatenate([rows_a[:own], rows_b[:own]], 0)
-    partner_rows = shifted(beside, "orb", 1)
-    inner, back = interior(
-        groups - 1, 1, True, odd, sweep_counts, order, ready, partner, *inner
-    )
+    partner_rows = shifted(row_pair(own, rows_a, rows_b), "orb", 1)
+    inner, back = interior(groups - 1, 1, True, order, ready, partner, *inner)
     partner_rows, inner, back = lax.optimization_barrier((partner_rows, inner, back))
     early = shifted(back, "orb", -1)
-    edges = tall_edges(odd, edges, rows_a, rows_b, partner_rows, partner)
+    edges = tall_edges(edges, rows_a, rows_b, partner_rows, partner)
     received = [lax.ppermute(edges, "gy", swap) for swap in col_swaps]
     ends, band_back = bands(
-        odd, sweep_counts, order, potentials, orbitals, partner, metric, coefficients,
+        order, potentials, orbitals, partner, metric, coefficients,
         rows_a, rows_b, partner_rows,
     )
-    edge_back, strip_fields = strips(odd, sweep_counts, band_back, edges, received)
+    edge_back, strip_fields = strips(steps, band_back, edges, received)
     edge_terms = shifted(edge_back, "orb", -1)
-    fields, home = merged(odd, inner, ends, strip_fields, orbitals, partner)
-    updated, norms = partial_norms(odd, home, early, edge_terms, metric)
+    fields, home = merged(inner, ends, strip_fields, orbitals, partner)
+    updated, norms = partial_norms(home, early, edge_terms, metric)
     norms, fields = lax.optimization_barrier((norms, fields))
     along, across = norm_hops(gx, gy)
     for hop in along:

time: 42.3 us -> 39.1 us (0.924)
  Pallas kernels: 19.4 us -> 15.9 us
  waiting for transfers between devices: 8.15 us -> 7.05 us
  local copies, waits for them, and re-layouts: 0.04 us -> 0.89 us
  other arithmetic: 0.38 us -> 1.05 us
    ppermute x4, waiting for transfers between devices: 4.58 us -> 3.47 us  [shifted(): lax.ppermute(value, axis, [(i, (i + by) % size) for i in range(size)])]
    pallas_call x2, Pallas kernels: 6.71 us -> 5.97 us  [interior(): pl.pallas_call(functools.partial(interior_kernel, groups, before, last),...]
    reduce_sum x1, other arithmetic: 0.18 us -> 0.91 us  [by_count(): rank = jnp.sum((more | tie).astype(jnp.int32), axis=1)]
    unnamed x10 -> x2, local copies, waits for them, and re-layouts: 0.03 us -> 0.64 us
    pallas_call x1, Pallas kernels: 0.7 us -> 0.15 us  [partial_norms(): pl.pallas_call(norm_kernel, out_shape=(f32(*home.shape), f32(-(-own // SU...]
    pallas_call x1, Pallas kernels: 2.81 us -> 2.27 us  [strips(): pl.pallas_call(functools.partial(strips_kernel, sides), out_shape=(f32(ba...]
    pallas_call x1, Pallas kernels: 0.74 us -> 0.2 us  [tall_edges(): pl.pallas_call(edges_kernel, out_shape=f32(groups + 1, rows + 2 * SUB, la...]
    pallas_call x1, Pallas kernels: 1.09 us -> 0.57 us  [merged(): pl.pallas_call(functools.partial(merge_kernel, sides), out_shape=(f32(*in...]
  transfers between devices with their start and end apart: 11 -> 11, of which waited for: 4 -> 5; matrix products, arithmetic and copies ran while one was open for 1% -> 3% of each run, Pallas kernels for 41% -> 38%
where the time goes in v6:
time: 39.1 us; the launch traced here: 38.7 us
  Pallas kernels  15.9 us (41%)
  starting transfers between devices  13 us (33%)
  waiting for transfers between devices  7.05 us (18%)
  other arithmetic  1.05 us (3%)
  local copies, waits for them, and re-layouts  0.89 us (2%)
  between operations  0.79 us (2%)
    ppermute x4, starting transfers between devices, shifted(): lax.ppermute(value, axis, [(i, (i + by) % size) for i in range(size)])  7.16 us
    pallas_call x2, Pallas kernels, interior(): pl.pallas_call(functools.partial(interior_kernel, groups, before, last),...  5.97 us
    ppermute x3, starting transfers between devices, local(): norms = [norms] + [lax.ppermute(norms, ('gx', 'gy'), hop) for hop in across]  4.08 us
    ppermute x4, waiting for transfers between devices, shifted(): lax.ppermute(value, axis, [(i, (i + by) % size) for i in range(size)])  3.47 us
    pallas_call x1, Pallas kernels, bands(): pl.pallas_call(bands_kernel, out_shape=(f32(pairs, 2, SUB, lanes), f32(2...  2.49 us
    pallas_call x1, Pallas kernels, prepare(): pl.pallas_call(prepare_kernel, out_shape=(jax.ShapeDtypeStruct(order.shap...  2.47 us
    ppermute x3, waiting for transfers between devices, local(): norms = [norms] + [lax.ppermute(norms, ('gx', 'gy'), hop) for hop in across]  2.42 us
    pallas_call x1, Pallas kernels, strips(): pl.pallas_call(functools.partial(strips_kernel, sides), out_shape=(f32(ba...  2.27 us
  transfers between devices with their start and end apart: 11, of which 5 were waited for; matrix products, arithmetic and copies ran while one was open for 3% of the time, Pallas kernels for 38%

profile of v6, /device:TPU:0, one launch (start us, length us, event | category | flops | bytes accessed | tf_op | source)
XLA Modules:
  0.0 38.7 jit_solution(3689294437517106104)
XLA Ops:
  0.6 3.0 %collective-permute-start.2 = (f32[4,128,128]{2,1,0:T(8,128)}, f32[4,128,128]{2,1,0:T(8,128)S(1)}, u32[]{:S(2)}, u32[]{:S(2)}) collective-permute-start(f32[4,128,128]{2,1,0:T(8,128)} %o_hbm.1), channel_id=1, source_target_pairs={{0,8},{8,16},{16,24},{24,0},{1,9},{9,17},{17,25},{25,1},{2,10},{10... | collective-permute-start | bytes 786440 | tf_op jit(solution)/shard_map/ppermute | solution.py:699
  3.6 0.9 %convert_reduce_fusion = s32[16]{0:T(128)S(1)} fusion(s32[16]{0:T(128)} %param.9), kind=kLoop, calls=%fused_computation.2 | loop fusion | flops 1776 | bytes 128 | tf_op jit(solution)/shard_map/reduce_sum | solution.py:727
  4.6 0.6 %copy-done = s32[16]{0:T(128)S(1)} copy-done((s32[16]{0:T(128)S(1)}, s32[16]{0:T(128)}, u32[]{:S(2)}) %copy-start) | copy-done | bytes 88
  5.2 0.1 reshape.40
  5.3 0.1 broadcast_in_dim.49
  5.4 0.1 broadcast_in_dim.50
  5.5 0.1 select_reduce_fusion.by_in
  5.6 2.5 %prepare.1 = (s32[2,16]{1,0:T(2,128)S(1)}, s32[4,8,128]{2,1,0:T(8,128)S(1)}, f32[16,16,8,128]{3,2,1,0:T(8,128)S(1)}, f32[4,16,8,128]{3,2,1,0:T(8,128)S(1)}, f32[...) custom-call(s32[2,16]{1,0:T(2,128)S(1)} %select_reduce_fusion.by_in,, ...), custom_call_target="tpu_custom_call" | custom-call | bytes 7400000 | tf_op jit(solution)/shard_map/prepare/pallas_call | solution.py:224
  8.1 1.6 %collective-permute-start = (f32[26,8,128]{2,1,0:T(8,128)S(1)}, f32[26,8,128]{2,1,0:T(8,128)S(1)}, u32[]{:S(2)}, u32[]{:S(2)}) collective-permute-start(f32[26,8,128]{2,1,0:T(8,128)S(1)} %get-tuple-element.36), channel_id=1, source_target_pairs={{0,2},{1,3},{2,0},{3,1},{4,6},{5,7},{6,4},{7,5},{8,10},{9,11},{10,... | collective-permute-start | bytes 319496 | tf_op jit(solution)/shard_map/ppermute | solution.py:746
  9.7 0.0 collective-permute-start.1
  9.7 1.4 %collective-permute-done.2.refs_4_.p_ref = f32[4,128,128]{2,1,0:T(8,128)S(1)} collective-permute-done((f32[4,128,128]{2,1,0:T(8,128)}, f32[4,128,128]{2,1,0:T(8,128)S(1)}, u32[]{:S(2)}, u32[]{:S(2)}) %collective-permute-start.2) | collective-permute-done | bytes 262176 | tf_op jit(solution)/shard_map/ppermute | solution.py:699
  11.1 2.0 %interior0.1 = (f32[16,128,128]{2,1,0:T(8,128)S(1)}, f32[4,16,8,128]{3,2,1,0:T(8,128)S(1)}) custom-call(s32[2,16]{1,0:T(2,128)S(1)} %get-tuple-element.38.by_any, f32[16,16,8,128]{3,2,1,0:T(8,128)S(1)} %get-tuple-element.39.refs_0_, f32[4,16,8,128]{3,2,1,0:T(8,128)S(1)} %get-tuple-element.40.refs_1_, f32[4,16,8,128]{3,2,1,0:T(8,128)S(1)} %get-tuple-element.41.refs_2_, ...), custom_call_target="tpu_custom_call" | custom-call | bytes 6660000 | tf_op jit(solution)/shard_map/interior0/pallas_call | solution.py:300
  13.2 1.2 %collective-permute-start.3 = (f32[8,8,128]{2,1,0:T(8,128)S(1)}, f32[8,8,128]{2,1,0:T(8,128)S(1)}, u32[]{:S(2)}, u32[]{:S(2)}) collective-permute-start(f32[8,8,128]{2,1,0:T(8,128)S(1)} %row_pair.1), channel_id=1, source_target_pairs={{0,8},{8,16},{16,24},{24,0},{1,9},{9,17},{17,25},{25,1},{2,10},{10... | collective-permute-start | bytes 98312 | tf_op jit(solution)/shard_map/ppermute | solution.py:699
  14.3 4.0 %interior1.1 = (f32[16,128,128]{2,1,0:T(8,128)S(1)}, f32[4,128,128]{2,1,0:T(8,128)S(1)}) custom-call(s32[2,16]{1,0:T(2,128)S(1)} %get-tuple-element.38.by_any, f32[16,16,8,128]{3,2,1,0:T(8,128)S(1)} %get-tuple-element.39.refs_0_, f32[4,16,8,128]{3,2,1,0:T(8,128)S(1)} %get-tuple-element.40.refs_1_, f32[4,16,8,128]{3,2,1,0:T(8,128)S(1)} %get-tuple-element.41.refs_2_, ...), custom_call_target="tpu_custom_call" | custom-call | bytes 19980000 | tf_op jit(solution)/shard_map/interior1/pallas_call | solution.py:300
  18.3 0.2 tall_edges.1.e_ref
  18.5 0.1 collective-permute-start.4
  18.6 1.5 %collective-permute-start.5 = (f32[4,128,128]{2,1,0:T(8,128)S(1)}, f32[4,128,128]{2,1,0:T(8,128)S(1)}, u32[]{:S(2)}, u32[]{:S(2)}) collective-permute-start(f32[4,128,128]{2,1,0:T(8,128)S(1)} %get-tuple-element.63), channel_id=1, source_target_pairs={{0,24},{8,0},{16,8},{24,16},{1,25},{9,1},{17,9},{25,17},{2,26},{10... | collective-permute-start | bytes 786440 | tf_op jit(solution)/shard_map/ppermute | solution.py:699
  20.1 2.5 %bands.1 = (f32[16,2,8,128]{3,2,1,0:T(8,128)S(1)}, f32[8,8,128]{2,1,0:T(8,128)S(1)}) custom-call(s32[2,16]{1,0:T(2,128)S(1)} %get-tuple-element.38.by_any, f32[16,128,128]{2,1,0:T(8,128)S(1)} %get-tuple-element.52.v_ref, f32[4,128,128]{2,1,0:T(8,128)S(1)} %get-tuple-element.53.o_ref, f32[4,128,128]{2,1,0:T(8,128)S(1)} %collective-permute-done.2.refs_4_.p_ref, ...), custom_call_target="tpu_custom_call" | custom-call | bytes 9250000 | tf_op jit(solution)/shard_map/bands/pallas_call | solution.py:441
  22.6 2.3 %strips.1 = (f32[12,8,128]{2,1,0:T(8,128)S(1)}, f32[4,144,128]{2,1,0:T(8,128)S(1)}) custom-call(s32[4,8,128]{2,1,0:T(8,128)S(1)} %get-tuple-element.58.n_ref, f32[8,8,128]{2,1,0:T(8,128)S(1)} %get-tuple-element.59.rows_ref, f32[8,144,128]{2,1,0:T(8,128)S(1)} %tall_edges.1.e_ref, f32[8,144,128]{2,1,0:T(8,128)S(1)} %collective-permute-done.4.refs_0_), custom_call_target="tpu_custom_call" | custom-call | bytes 10730000 | tf_op jit(solution)/shard_map/strips/pallas_call | solution.py:539
  24.9 1.5 %collective-permute-start.6 = (f32[12,8,128]{2,1,0:T(8,128)S(1)}, f32[12,8,128]{2,1,0:T(8,128)S(1)}, u32[]{:S(2)}, u32[]{:S(2)}) collective-permute-start(f32[12,8,128]{2,1,0:T(8,128)S(1)} %get-tuple-element.64), channel_id=1, source_target_pairs={{0,24},{8,0},{16,8},{24,16},{1,25},{9,1},{17,9},{25,17},{2,26},{10... | collective-permute-start | bytes 147464 | tf_op jit(solution)/shard_map/ppermute | solution.py:699
  26.4 0.6 %merge.1 = (f32[16,128,128]{2,1,0:T(8,128)S(1)}, f32[4,128,128]{2,1,0:T(8,128)S(1)}) custom-call(f32[16,128,128]{2,1,0:T(8,128)S(1)} %get-tuple-element.51.inner_ref, f32[16,2,8,128]{3,2,1,0:T(8,128)S(1)} %get-tuple-element.57.ends_ref, f32[4,144,128]{2,1,0:T(8,128)S(1)} %get-tuple-element.61.sv_ref, f32[4,128,128]{2,1,0:T(8,128)S(1)} %get-tuple-element.53.o_ref, ...), custom_call_target="tpu_custom_call" | custom-call | bytes 4440000 | tf_op jit(solution)/shard_map/merge/pallas_call | solution.py:597
  26.9 1.3 %collective-permute-done.5.recv_ref = f32[4,128,128]{2,1,0:T(8,128)S(1)} collective-permute-done((f32[4,128,128]{2,1,0:T(8,128)S(1)}, f32[4,128,128]{2,1,0:T(8,128)S(1)}, u32[]{:S(2)}, u32[]{:S(2)}) %collective-permute-start.5) | collective-permute-done | bytes 262176 | tf_op jit(solution)/shard_map/ppermute | solution.py:699
  28.2 0.8 %collective-permute-done.6.edge_ref = f32[12,8,128]{2,1,0:T(8,128)S(1)} collective-permute-done((f32[12,8,128]{2,1,0:T(8,128)S(1)}, f32[12,8,128]{2,1,0:T(8,128)S(1)}, u32[]{:S(2)}, u32[]{:S(2)}) %collective-permute-start.6) | collective-permute-done | bytes 49184 | tf_op jit(solution)/shard_map/ppermute | solution.py:699
  29.0 0.1 partial_norms.1
  29.2 0.1 collective-permute-start.7
  29.2 1.2 %collective-permute-done.7 = f32[8,128]{1,0:T(8,128)S(1)} collective-permute-done((f32[8,128]{1,0:T(8,128)S(1)}, f32[8,128]{1,0:T(8,128)S(1)}, u32[]{:S(2)}, u32[]{:S(2)}) %collective-permute-start.7) | collective-permute-done | bytes 4128 | tf_op jit(solution)/shard_map/ppermute | solution.py:767
  30.4 3.6 %collective-permute-start.10 = (f32[8,128]{1,0:T(8,128)S(1)}, f32[8,128]{1,0:T(8,128)S(1)}, u32[]{:S(2)}, u32[]{:S(2)}) collective-permute-start(f32[8,128]{1,0:T(8,128)S(1)} %add.3.refs_0_), channel_id=1, source_target_pairs={{0,7},{1,6},{2,5},{3,4},{4,3},{5,2},{6,1},{7,0},{8,15},{9,14},{10,... | collective-permute-start | bytes 12296 | tf_op jit(solution)/shard_map/ppermute | solution.py:768
  34.0 0.0 collective-permute-start.9
  34.0 0.5 %collective-permute-start.8 = (f32[8,128]{1,0:T(8,128)S(1)}, f32[8,128]{1,0:T(8,128)S(1)}, u32[]{:S(2)}, u32[]{:S(2)}) collective-permute-start(f32[8,128]{1,0:T(8,128)S(1)} %add.3.refs_0_), channel_id=1, source_target_pairs={{0,3},{1,2},{2,1},{3,0},{4,7},{5,6},{6,5},{7,4},{8,11},{9,10},{10,... | collective-permute-start | bytes 12296 | tf_op jit(solution)/shard_map/ppermute | solution.py:768
  34.5 1.0 %write.1 = f32[16,128,128]{2,1,0:T(8,128)} custom-call(f32[16,128,128]{2,1,0:T(8,128)S(1)} %get-tuple-element.69.v_ref), custom_call_target="tpu_custom_call" | custom-call | bytes 4440000 | tf_op jit(solution)/shard_map/write/pallas_call | solution.py:622
  35.5 2.4 %collective-permute-done.9.refs_2_ = f32[8,128]{1,0:T(8,128)S(1)} collective-permute-done((f32[8,128]{1,0:T(8,128)S(1)}, f32[8,128]{1,0:T(8,128)S(1)}, u32[]{:S(2)}, u32[]{:S(2)}) %collective-permute-start.9) | collective-permute-done | bytes 4128 | tf_op jit(solution)/shard_map/ppermute | solution.py:768
  37.9 0.8 %rescaled.1 = f32[4,128,128]{2,1,0:T(8,128)} custom-call(f32[4,128,128]{2,1,0:T(8,128)S(1)} %get-tuple-element.65.upd_ref, f32[8,128]{1,0:T(8,128)S(1)} %add.3.refs_0_, f32[8,128]{1,0:T(8,128)S(1)} %collective-permute-done.8.refs_1_, f32[8,128]{1,0:T(8,128)S(1)} %collective-permute-done.9.refs_2_, f32[8,128]{1,0:T(8,128)S(1)} %collective-permute-done.10.refs_3_), custom_call_target="tpu_custom_call" | custom-call | bytes 2960000 | tf_op jit(solution)/shard_map/rescaled/pallas_call | solution.py:686
  (13 shorter events, 0.0 us)
Async XLA Ops:
  0.6 10.5 %collective-permute-start.2 = (f32[4,128,128]{2,1,0:T(8,128)}, f32[4,128,128]{2,1,0:T(8,128)S(1)}, u32[]{:S(2)}, u32[]{:S(2)}) collective-permute-start(f32[4,128,128]{2,1,0:T(8,128)} %o_hbm.1), channel_id=1, source_target_pairs={{0,8},{8,16},{16,24},{24,0},{1,9},{9,17},{17,25},{25,1},{2,10},{10... | collective-permute-start | bytes 786440 | tf_op jit(solution)/shard_map/ppermute | solution.py:699
  4.5 0.7 %copy-start = (s32[16]{0:T(128)S(1)}, s32[16]{0:T(128)}, u32[]{:S(2)}) copy-start(s32[16]{0:T(128)} %param.9) | copy-start | bytes 196
  8.1 5.1 %collective-permute-start = (f32[26,8,128]{2,1,0:T(8,128)S(1)}, f32[26,8,128]{2,1,0:T(8,128)S(1)}, u32[]{:S(2)}, u32[]{:S(2)}) collective-permute-start(f32[26,8,128]{2,1,0:T(8,128)S(1)} %get-tuple-element.36), channel_id=1, source_target_pairs={{0,2},{1,3},{2,0},{3,1},{4,6},{5,7},{6,4},{7,5},{8,10},{9,11},{10,... | collective-permute-start | bytes 319496 | tf_op jit(solution)/shard_map/ppermute | solution.py:746
  9.7 3.4 %collective-permute-start.1 = (f32[26,8,128]{2,1,0:T(8,128)S(1)}, f32[26,8,128]{2,1,0:T(8,128)S(1)}, u32[]{:S(2)}, u32[]{:S(2)}) collective-permute-start(f32[26,8,128]{2,1,0:T(8,128)S(1)} %get-tuple-element.37), channel_id=1, source_target_pairs={{0,1},{1,0},{2,4},{3,5},{4,2},{5,3},{6,7},{7,6},{8,9},{9,8},{10,12... | collective-permute-start | bytes 319496 | tf_op jit(solution)/shard_map/ppermute | solution.py:747
  13.2 5.1 %collective-permute-start.3 = (f32[8,8,128]{2,1,0:T(8,128)S(1)}, f32[8,8,128]{2,1,0:T(8,128)S(1)}, u32[]{:S(2)}, u32[]{:S(2)}) collective-permute-start(f32[8,8,128]{2,1,0:T(8,128)S(1)} %row_pair.1), channel_id=1, source_target_pairs={{0,8},{8,16},{16,24},{24,0},{1,9},{9,17},{17,25},{25,1},{2,10},{10... | collective-permute-start | bytes 98312 | tf_op jit(solution)/shard_map/ppermute | solution.py:699
  18.5 4.1 %collective-permute-start.4 = (f32[8,144,128]{2,1,0:T(8,128)S(1)}, f32[8,144,128]{2,1,0:T(8,128)S(1)}, u32[]{:S(2)}, u32[]{:S(2)}) collective-permute-start(f32[8,144,128]{2,1,0:T(8,128)S(1)} %tall_edges.1.e_ref), channel_id=1, source_target_pairs={{0,1},{1,0},{2,3},{3,2},{4,5},{5,4},{6,7},{7,6},{8,9},{9,8},{10,11... | collective-permute-start | bytes 1769480 | tf_op jit(solution)/shard_map/ppermute | solution.py:755
  18.6 9.6 %collective-permute-start.5 = (f32[4,128,128]{2,1,0:T(8,128)S(1)}, f32[4,128,128]{2,1,0:T(8,128)S(1)}, u32[]{:S(2)}, u32[]{:S(2)}) collective-permute-start(f32[4,128,128]{2,1,0:T(8,128)S(1)} %get-tuple-element.63), channel_id=1, source_target_pairs={{0,24},{8,0},{16,8},{24,16},{1,25},{9,1},{17,9},{25,17},{2,26},{10... | collective-permute-start | bytes 786440 | tf_op jit(solution)/shard_map/ppermute | solution.py:699
  24.9 4.1 %collective-permute-start.6 = (f32[12,8,128]{2,1,0:T(8,128)S(1)}, f32[12,8,128]{2,1,0:T(8,128)S(1)}, u32[]{:S(2)}, u32[]{:S(2)}) collective-permute-start(f32[12,8,128]{2,1,0:T(8,128)S(1)} %get-tuple-element.64), channel_id=1, source_target_pairs={{0,24},{8,0},{16,8},{24,16},{1,25},{9,1},{17,9},{25,17},{2,26},{10... | collective-permute-start | bytes 147464 | tf_op jit(solution)/shard_map/ppermute | solution.py:699
  29.2 1.2 %collective-permute-start.7 = (f32[8,128]{1,0:T(8,128)S(1)}, f32[8,128]{1,0:T(8,128)S(1)}, u32[]{:S(2)}, u32[]{:S(2)}) collective-permute-start(f32[8,128]{1,0:T(8,128)S(1)} %get-tuple-element.68), channel_id=1, source_target_pairs={{0,1},{1,0},{2,3},{3,2},{4,5},{5,4},{6,7},{7,6},{8,9},{9,8},{10,11... | collective-permute-start | bytes 12296 | tf_op jit(solution)/shard_map/ppermute | solution.py:767
  30.4 5.1 %collective-permute-start.10 = (f32[8,128]{1,0:T(8,128)S(1)}, f32[8,128]{1,0:T(8,128)S(1)}, u32[]{:S(2)}, u32[]{:S(2)}) collective-permute-start(f32[8,128]{1,0:T(8,128)S(1)} %add.3.refs_0_), channel_id=1, source_target_pairs={{0,7},{1,6},{2,5},{3,4},{4,3},{5,2},{6,1},{7,0},{8,15},{9,14},{10,... | collective-permute-start | bytes 12296 | tf_op jit(solution)/shard_map/ppermute | solution.py:768
  34.0 3.9 %collective-permute-start.9 = (f32[8,128]{1,0:T(8,128)S(1)}, f32[8,128]{1,0:T(8,128)S(1)}, u32[]{:S(2)}, u32[]{:S(2)}) collective-permute-start(f32[8,128]{1,0:T(8,128)S(1)} %add.3.refs_0_), channel_id=1, source_target_pairs={{0,5},{1,4},{2,7},{3,6},{4,1},{5,0},{6,3},{7,2},{8,13},{9,12},{10,... | collective-permute-start | bytes 12296 | tf_op jit(solution)/shard_map/ppermute | solution.py:768
  34.0 3.9 %collective-permute-start.8 = (f32[8,128]{1,0:T(8,128)S(1)}, f32[8,128]{1,0:T(8,128)S(1)}, u32[]{:S(2)}, u32[]{:S(2)}) collective-permute-start(f32[8,128]{1,0:T(8,128)S(1)} %add.3.refs_0_), channel_id=1, source_target_pairs={{0,3},{1,2},{2,1},{3,0},{4,7},{5,6},{6,5},{7,4},{8,11},{9,10},{10,... | collective-permute-start | bytes 12296 | tf_op jit(solution)/shard_map/ppermute | solution.py:768

commit v7 on v6

--- a/solution.py
+++ b/solution.py
@@ -19,7 +19,8 @@
 STRIP = 32
 BLOCKS = LANES // STRIP
 LEAST = 4
-GROUP = 4
+FIRST = 8
+GROUP = 8
 BANDS = 8
 AHEAD = 16
 VMEM_LIMIT = 16 * 1024 * 1024
@@ -131,6 +132,14 @@
         new[k, t] = value
 
 
+class Chosen:
+    def __init__(self, ref, picks):
+        self.ref, self.picks = ref, picks
+
+    def __getitem__(self, at):
+        return self.ref[self.picks[at[0]], at[1]]
+
+
 def relax(steps, count, here, there, source, coefs, masks):
     fields = len(steps)
     west, east, dead = masks
@@ -158,12 +167,35 @@
     return west, east, dead
 
 
-def prepare_kernel(by_in, steps_in, o_hbm, v_hbm, m_hbm, c_hbm, by_ref, steps_ref, *refs):
-    vs_ref, os_ref, om_ref, cf_ref, e_ref, pay_a, pay_b, o_ref, v_ref, m_ref, c_ref, sems = refs
+def sorted_counts(counts):
+    pairs = counts.shape[1]
+    at = lax.broadcasted_iota(jnp.int32, (pairs, pairs), 1)
+    down = lax.broadcasted_iota(jnp.int32, (pairs, pairs), 0)
+    row = jnp.broadcast_to(counts, (pairs, pairs)).astype(jnp.float32)
+
+    def turned(value):
+        return jnp.sum(jnp.where(at == down, value, 0.0), axis=1, keepdims=True)
+
+    def rank(key):
+        own_key = turned(key)
+        before = jnp.where(key > own_key, 1.0, 0.0)
+        before = before + jnp.where((key == own_key) & (at < down), 1.0, 0.0)
+        return jnp.sum(before, axis=1, keepdims=True)
+
+    chosen = jnp.broadcast_to(rank(row), row.shape) == at.astype(jnp.float32)
+    column = jnp.broadcast_to(turned(row), row.shape)
+    steps = jnp.sum(jnp.where(chosen, column, 0.0), axis=0, keepdims=True)
+    which = jnp.sum(jnp.where(chosen, down.astype(jnp.float32), 0.0), axis=0, keepdims=True)
+    return jnp.concatenate([steps, which], axis=0).astype(jnp.int32)
+
+
+def prepare_kernel(n_hbm, o_hbm, v_hbm, m_hbm, c_hbm, by_ref, steps_ref, *refs):
+    vs_ref, os_ref, om_ref, cf_ref, e_ref, pay_a, pay_b, o_ref, v_ref, m_ref, c_ref = refs[:11]
+    n_ref, sems = refs[11:]
     own, rows, _ = o_ref.shape
     pairs = v_ref.shape[0]
     count = rows // SUB
-    sources = [(m_hbm, m_ref), (c_hbm, c_ref), (o_hbm, o_ref)]
+    sources = [(n_hbm, n_ref), (m_hbm, m_ref), (c_hbm, c_ref), (o_hbm, o_ref)]
     for first in range(own):
         part = pl.ds(first * own, own)
         sources.append((v_hbm.at[part], v_ref.at[part]))
@@ -173,8 +205,6 @@
     ]
     for copy in copies:
         copy.start()
-    by_ref[...] = by_in[...]
-    steps_ref[...] = steps_in[...]
 
     starts = [(1 - place()[0]) * (rows - HALO), place()[0] * (rows - HALO)]
     starts = [pl.multiple_of(start, HALO) for start in starts]
@@ -184,7 +214,19 @@
             pay[at] = ref[index, pl.ds(start, HALO)]
 
     copies[0].wait()
+    counts = n_ref[...]
+    by_ref[...] = sorted_counts(counts)
+    at = lax.broadcasted_iota(jnp.int32, counts.shape, 1)
+    floats = counts.astype(jnp.float32)
+    block = lane_of() // STRIP
+    for first in range(own):
+        steps = jnp.zeros((SUB, LANES), jnp.float32)
+        for second in range(own):
+            alone = jnp.where(at == first * own + second, floats, 0.0)
+            steps = jnp.where(block == second, jnp.sum(alone, axis=1, keepdims=True), steps)
+        steps_ref[first] = steps.astype(jnp.int32)
     copies[1].wait()
+    copies[2].wait()
     send_rows(own + pairs, m_ref, 0)
     for n in range(5):
         send_rows(own + pairs + 1 + n, c_ref, n)
@@ -199,7 +241,7 @@
         weights.append(scale * metric[t])
         for n in range(5):
             cf_ref[n, t] = scale * raw[n][t]
-    copies[2].wait()
+    copies[3].wait()
     e_ref[0] = packed([o_ref[k] for k in range(own)])
     for k in range(own):
         send_rows(k, o_ref, k)
@@ -207,7 +249,7 @@
             os_ref[k, t] = value
             om_ref[k, t] = weights[t] * value
     for first in range(own):
-        copies[3 + first].wait()
+        copies[4 + first].wait()
         e_ref[1 + first] = packed([v_ref[first * own + k] for k in range(own)])
         for p in range(first * own, (first + 1) * own):
             send_rows(own + p, v_ref, p)
@@ -215,8 +257,8 @@
                 vs_ref[p, t] = value
 
 
-def prepare(order, steps, *arrays):
-    orbitals, potentials, _, coefficients = arrays
+def prepare(*arrays):
+    counts, orbitals, potentials, _, coefficients = arrays
     own, rows, lanes = orbitals.shape
     pairs = potentials.shape[0]
     count = rows // SUB
@@ -224,35 +266,40 @@
     return pl.pallas_call(
         prepare_kernel,
         out_shape=(
-            jax.ShapeDtypeStruct(order.shape, order.dtype),
-            jax.ShapeDtypeStruct(steps.shape, steps.dtype),
+            jax.ShapeDtypeStruct((2, pairs), jnp.int32),
+            jax.ShapeDtypeStruct((own, SUB, lanes), jnp.int32),
             f32(pairs, count, SUB, lanes),
             f32(own, count, SUB, lanes),
             f32(own, count, SUB, lanes),
             f32(5, count, SUB, lanes),
             f32(own + 3, rows, lanes),
             *[f32(own + pairs + 1 + coefficients.shape[0], HALO, lanes)] * 2,
-            *[f32(*a.shape) for a in arrays],
+            *[f32(*a.shape) for a in arrays[1:]],
         ),
-        in_specs=[VMEM] * 2 + [HBM] * 4,
+        in_specs=[HBM] * 5,
         out_specs=(VMEM,) * 13,
-        scratch_shapes=[pltpu.SemaphoreType.DMA((3 + own,))],
+        scratch_shapes=[
+            pltpu.VMEM(counts.shape, jnp.int32),
+            pltpu.SemaphoreType.DMA((4 + own,)),
+        ],
         compiler_params=params(),
         cost_estimate=cost(2.0),
         name="prepare",
-    )(order, steps, *inputs)
-
-
-def interior_kernel(groups, before, last, by_any, *refs):
+    )(*inputs)
+
+
+def interior_kernel(size, groups, before, by_any, *refs):
     vs_ref, os_ref, om_ref, cf_ref, p_ref = refs[:5]
-    out_ref, back_ref, back, qs, sr, va, vb, by_ref, sem = refs[-9:]
+    out_ref, back_ref, back, flat, sr, va, vb, by_ref, sem = refs[-9:]
     own, count = om_ref.shape[:2]
     fetch = pltpu.make_async_copy(by_any, by_ref, sem)
     fetch.start()
     masks = lane_masks(place()[1])
-    for k in range(own):
-        for t, value in enumerate(spread(p_ref, count, k)):
-            qs[k, t] = value
+    for second in range(own):
+        partner = spread(p_ref, count, second)
+        for first in range(own):
+            for t in range(count):
+                sr[first * own + second, t] = om_ref[first, t] * partner[t]
     if before:
         earlier, back_before = refs[5:7]
         back[...] = back_before[...]
@@ -265,17 +312,15 @@
             out_ref[by_ref[1, k]] = earlier[by_ref[1, k]]
             return carry
 
-        lax.fori_loop(0, before * GROUP, keep, 0)
+        lax.fori_loop(0, before, keep, 0)
 
     def group(g, carry):
-        pairs = [by_ref[1, g * GROUP + k] for k in range(GROUP)]
+        pairs = [by_ref[1, before + g * size + k] for k in range(size)]
         for k, p in enumerate(pairs):
-            first, second = p // own, p % own
             for t in range(count):
-                sr[k, t] = om_ref[first, t] * qs[second, t]
                 va[k, t] = vs_ref[p, t]
-        steps = [by_ref[0, g * GROUP + k] for k in range(GROUP)]
-        relax(steps, count, va, vb, sr, cf_ref, masks)
+        steps = [by_ref[0, before + g * size + k] for k in range(size)]
+        relax(steps, count, va, vb, Chosen(sr, pairs), cf_ref, masks)
         for k, p in enumerate(pairs):
             first, second = p // own, p % own
             spread_store(out_ref, [va[k, t] for t in range(count)], p)
@@ -283,29 +328,32 @@
                 back[second, t] = back[second, t] + va[k, t] * os_ref[first, t]
         return carry
 
-    lax.fori_loop(before, before + groups, group, 0)
+    lax.fori_loop(0, groups, group, 0)
     for k in range(own):
-        if last:
-            spread_store(back_ref, [back[k, t] for t in range(count)], k)
+        if before:
+            spread_store(flat, [back[k, t] for t in range(count)])
+            back_ref[k] = flat[SUB : SUB + back_ref.shape[1]]
         else:
             back_ref[k] = back[k]
 
 
-def interior(groups, before, last, order, ready, partner, *earlier):
+def interior(size, groups, before, order, ready, partner, *earlier):
     pairs, count, _, lanes = ready[0].shape
-    own, rows, _ = partner.shape
-    four = pltpu.VMEM((GROUP, count, SUB, lanes), jnp.float32)
+    own = ready[1].shape[0]
+    rows = count * SUB
+    some = pltpu.VMEM((size, count, SUB, lanes), jnp.float32)
     each = pltpu.VMEM((own, count, SUB, lanes), jnp.float32)
-    back = f32(own, rows, lanes) if last else f32(own, count, SUB, lanes)
-    return pl.pallas_call(
-        functools.partial(interior_kernel, groups, before, last),
+    every = pltpu.VMEM((pairs, count, SUB, lanes), jnp.float32)
+    back = f32(own, rows - 2 * SUB, lanes) if before else f32(own, count, SUB, lanes)
+    return pl.pallas_call(
+        functools.partial(interior_kernel, size, groups, before),
         out_shape=(f32(pairs, rows, lanes), back),
         in_specs=[ANY] + [VMEM] * (5 + len(earlier)),
         out_specs=(VMEM, VMEM),
-        scratch_shapes=[each, each, four, four, four]
+        scratch_shapes=[each, pltpu.VMEM((rows, lanes), jnp.float32), every, some, some]
         + [pltpu.SMEM(order.shape, jnp.int32), pltpu.SemaphoreType.DMA],
         compiler_params=params(),
-        cost_estimate=cost(1.8 * groups),
+        cost_estimate=cost(0.4 * size * groups),
         name=f"interior{before}",
     )(order, *ready[:4], partner, *earlier)
 
@@ -506,12 +554,12 @@
             steps.append(n_ref[g])
 
         def body(turn, carry):
-            for s in range(2):
-                keep = [n > 2 * turn + s for n in steps]
-                sweep(own, count, (va, vb)[s], (vb, va)[s], sr, cf, keep=keep)
+            for s in range(4):
+                keep = [n > 4 * turn + s for n in steps]
+                sweep(own, count, (va, vb)[s % 2], (vb, va)[s % 2], sr, cf, keep=keep)
             return carry
 
-        lax.fori_loop(0, SWEEPS // 2, body, 0)
+        lax.fori_loop(0, SWEEPS // 4, body, 0)
         back = []
         for t in range(count):
             terms = [va[g, t] * orep[g, t] for g in range(own)]
@@ -642,11 +690,12 @@
         total = jnp.zeros((SUB, LANES), jnp.float32)
         for r in range(rows // SUB):
             at = r * SUB
-            value = recv_ref[k, at : at + SUB]
             if r == 0:
                 value = edge_ref[k]
-            if r == rows // SUB - 1:
+            elif r == rows // SUB - 1:
                 value = edge_ref[own + k]
+            else:
+                value = recv_ref[k, at - SUB : at]
             g, v = divmod(r, fold)
             for side in range(sides):
                 left_own, _, in_block = strip_place(side)
@@ -716,39 +765,32 @@
 
 def norm_hops(gx, gy):
     along = [[(i, i ^ (1 << k)) for i in range(gx * gy)] for k in range(gy.bit_length() - 1)]
-    across = [[(i, i ^ (gy * k) ^ 1) for i in range(gx * gy)] for k in range(1, gx)]
+    along += [[(i, i ^ gy ^ 1) for i in range(gx * gy)]]
+    across = [[(i, i ^ (gy * 2) ^ 1) for i in range(gx * gy)]]
     return along, across
-
-
-def by_count(counts):
-    at = jnp.arange(counts.shape[0], dtype=jnp.int32)
-    more = counts[None] > counts[:, None]
-    tie = (counts[None] == counts[:, None]) & (at[None] < at[:, None])
-    rank = jnp.sum((more | tie).astype(jnp.int32), axis=1)
-    chosen = (rank[None] == at[:, None])[None]
-    return jnp.sum(jnp.where(chosen, jnp.stack([counts, at])[:, None], 0), axis=2)
 
 
 def local(orbitals, potentials, coefficients, metric, sweep_counts):
     own, rows, lanes = orbitals.shape
     gx, gy = lax.axis_size("gx"), lax.axis_size("gy")
-    order = by_count(sweep_counts)
-    steps = jnp.repeat(sweep_counts.reshape(own, 1, own), STRIP, axis=2)
-    steps = jnp.broadcast_to(steps, (own, SUB, lanes))
     col_swaps = [p for p in pair_swaps(gy) if p]
     row_swaps = [row_swap(p, gx, gy) for p in pair_swaps(gx)]
-    groups = potentials.shape[0] // GROUP
+    pairs = potentials.shape[0]
 
     partner = shifted(orbitals, "orb", 1)
-    order, steps, *ready = prepare(order, steps, orbitals, potentials, metric[None], coefficients)
+    order, steps, *ready = prepare(
+        sweep_counts[None], orbitals, potentials, metric[None], coefficients
+    )
     *ready, edges, pay_a, pay_b, orbitals, potentials, metric, coefficients = ready
     metric = metric.reshape(rows, lanes)
     rows_a = lax.ppermute(pay_a, ("gx", "gy"), row_swaps[0])
     rows_b = lax.ppermute(pay_b, ("gx", "gy"), row_swaps[1])
-    inner = interior(1, 0, False, order, ready, partner)
+    inner = interior(FIRST, 1, 0, order, ready, partner)
     rows_a, rows_b, inner = lax.optimization_barrier((rows_a, rows_b, inner))
     partner_rows = shifted(row_pair(own, rows_a, rows_b), "orb", 1)
-    inner, back = interior(groups - 1, 1, True, order, ready, partner, *inner)
+    inner, back = interior(
+        GROUP, (pairs - FIRST) // GROUP, FIRST, order, ready, partner, *inner
+    )
     partner_rows, inner, back = lax.optimization_barrier((partner_rows, inner, back))
     early = shifted(back, "orb", -1)
     edges = tall_edges(edges, rows_a, rows_b, partner_rows, partner)

time: 39.1 us -> 39 us (level); the launches traced: 38.7 us -> 39.3 us
  waiting for transfers between devices: 7.05 us -> 8.84 us
  other arithmetic: 1.05 us -> 0.01 us
  Pallas kernels: 15.9 us -> 16.8 us
  local copies, waits for them, and re-layouts: 0.89 us -> 0 us
    ppermute x4, waiting for transfers between devices: 3.47 us -> 5.82 us  [shifted(): lax.ppermute(value, axis, [(i, (i + by) % size) for i in range(size)])]
    ppermute x3 -> x1, waiting for transfers between devices: 2.42 us -> 0.37 us  [local(): norms = [norms] + [lax.ppermute(norms, ('gx', 'gy'), hop) for hop in across]]
    ppermute x1 -> x2, starting transfers between devices: 0.07 us -> 1.61 us  [local(): norms = norms + lax.ppermute(norms, ('gx', 'gy'), hop)]
    ppermute x3 -> x1, starting transfers between devices: 4.08 us -> 2.56 us  [local(): norms = [norms] + [lax.ppermute(norms, ('gx', 'gy'), hop) for hop in across]]
    ppermute x1 -> x2, waiting for transfers between devices: 1.15 us -> 2.64 us  [local(): norms = norms + lax.ppermute(norms, ('gx', 'gy'), hop)]
    reduce_sum x2 -> x0, other arithmetic: 1.03 us -> none  [the longest x1 0.91 us: by_count(): rank = jnp.sum((more | tie).astype(jnp.int32), axis=1)]
    pallas_call x3, Pallas kernels: 8.44 us -> 9.14 us  [the longest x2 6.65 us: interior(): pl.pallas_call(functools.partial(interior_kernel, size, groups, before),...]
    unnamed x2 -> x0, local copies, waits for them, and re-layouts: 0.64 us -> none
  transfers between devices with their start and end apart: 11 -> 10, of which waited for: 5 -> 6; matrix products, arithmetic and copies ran while one was open for 3% -> 0% of each run, Pallas kernels for 38% -> 40%
where the time goes in v7:
time: 39 us; the launch traced here: 39.3 us
  Pallas kernels  16.8 us (43%)
  starting transfers between devices  13 us (33%)
  waiting for transfers between devices  8.84 us (23%)
  between operations  0.76 us (2%)
    ppermute x4, starting transfers between devices, shifted(): lax.ppermute(value, axis, [(i, (i + by) % size) for i in range(size)])  7.1 us
    pallas_call x2, Pallas kernels, interior(): pl.pallas_call(functools.partial(interior_kernel, size, groups, before),...  6.65 us
    ppermute x4, waiting for transfers between devices, shifted(): lax.ppermute(value, axis, [(i, (i + by) % size) for i in range(size)])  5.82 us
    pallas_call x1, Pallas kernels, bands(): pl.pallas_call(bands_kernel, out_shape=(f32(pairs, 2, SUB, lanes), f32(2...  2.77 us
    ppermute x2, waiting for transfers between devices, local(): norms = norms + lax.ppermute(norms, ('gx', 'gy'), hop)  2.64 us
    ppermute x1, starting transfers between devices, local(): norms = [norms] + [lax.ppermute(norms, ('gx', 'gy'), hop) for hop in across]  2.56 us
    pallas_call x1, Pallas kernels, prepare(): pl.pallas_call(prepare_kernel, out_shape=(jax.ShapeDtypeStruct((2, pairs)...  2.49 us
    pallas_call x1, Pallas kernels, strips(): pl.pallas_call(functools.partial(strips_kernel, sides), out_shape=(f32(ba...  2.12 us
  transfers between devices with their start and end apart: 10, of which 6 were waited for; matrix products, arithmetic and copies ran while one was open for 0% of the time, Pallas kernels for 40%

profile of v7, /device:TPU:0, one launch (start us, length us, event | category | flops | bytes accessed | tf_op | source)
XLA Modules:
  0.0 39.3 jit_solution(17950789152359739224)
XLA Ops:
  0.6 3.0 %collective-permute-start.2 = (f32[4,128,128]{2,1,0:T(8,128)}, f32[4,128,128]{2,1,0:T(8,128)S(1)}, u32[]{:S(2)}, u32[]{:S(2)}) collective-permute-start(f32[4,128,128]{2,1,0:T(8,128)} %o_hbm.1), channel_id=1, source_target_pairs={{0,8},{8,16},{16,24},{24,0},{1,9},{9,17},{17,25},{25,1},{2,10},{10... | collective-permute-start | bytes 786440 | tf_op jit(solution)/shard_map/ppermute | solution.py:748
  3.6 2.5 %prepare.1 = (s32[2,16]{1,0:T(2,128)S(1)}, s32[4,8,128]{2,1,0:T(8,128)S(1)}, f32[16,16,8,128]{3,2,1,0:T(8,128)S(1)}, f32[4,16,8,128]{3,2,1,0:T(8,128)S(1)}, f32[...) custom-call(s32[1,16]{1,0:T(1,128)} %bitcast.6, ...), custom_call_target="tpu_custom_call" | custom-call | bytes 7400000 | tf_op jit(solution)/shard_map/prepare/pallas_call | solution.py:266
  6.1 1.6 %collective-permute-start = (f32[26,8,128]{2,1,0:T(8,128)S(1)}, f32[26,8,128]{2,1,0:T(8,128)S(1)}, u32[]{:S(2)}, u32[]{:S(2)}) collective-permute-start(f32[26,8,128]{2,1,0:T(8,128)S(1)} %get-tuple-element.36), channel_id=1, source_target_pairs={{0,2},{1,3},{2,0},{3,1},{4,6},{5,7},{6,4},{7,5},{8,10},{9,11},{10,... | collective-permute-start | bytes 319496 | tf_op jit(solution)/shard_map/ppermute | solution.py:786
  7.8 0.0 collective-permute-start.1
  7.8 3.3 %collective-permute-done.2.refs_4_.p_ref = f32[4,128,128]{2,1,0:T(8,128)S(1)} collective-permute-done((f32[4,128,128]{2,1,0:T(8,128)}, f32[4,128,128]{2,1,0:T(8,128)S(1)}, u32[]{:S(2)}, u32[]{:S(2)}) %collective-permute-start.2) | collective-permute-done | bytes 262176 | tf_op jit(solution)/shard_map/ppermute | solution.py:748
  11.1 3.2 %interior0.1 = (f32[16,128,128]{2,1,0:T(8,128)S(1)}, f32[4,16,8,128]{3,2,1,0:T(8,128)S(1)}) custom-call(s32[2,16]{1,0:T(2,128)S(1)} %get-tuple-element.38.by_any, f32[16,16,8,128]{3,2,1,0:T(8,128)S(1)} %get-tuple-element.39.refs_0_, f32[4,16,8,128]{3,2,1,0:T(8,128)S(1)} %get-tuple-element.40.refs_1_, f32[4,16,8,128]{3,2,1,0:T(8,128)S(1)} %get-tuple-element.41.refs_2_, ...), custom_call_target="tpu_custom_call" | custom-call | bytes 11840000 | tf_op jit(solution)/shard_map/interior0/pallas_call | solution.py:348
  14.3 0.0 collective-permute-done.a_ref.ra_ref
  14.4 0.0 collective-permute-done.1.b_ref.rb_ref
  14.4 0.8 %collective-permute-start.3 = (f32[8,8,128]{2,1,0:T(8,128)S(1)}, f32[8,8,128]{2,1,0:T(8,128)S(1)}, u32[]{:S(2)}, u32[]{:S(2)}) collective-permute-start(f32[8,8,128]{2,1,0:T(8,128)S(1)} %row_pair.1), channel_id=1, source_target_pairs={{0,8},{8,16},{16,24},{24,0},{1,9},{9,17},{17,25},{25,1},{2,10},{10... | collective-permute-start | bytes 98312 | tf_op jit(solution)/shard_map/ppermute | solution.py:748
  15.2 3.4 %interior8.1 = (f32[16,128,128]{2,1,0:T(8,128)S(1)}, f32[4,112,128]{2,1,0:T(8,128)S(1)}) custom-call(s32[2,16]{1,0:T(2,128)S(1)} %get-tuple-element.38.by_any, f32[16,16,8,128]{3,2,1,0:T(8,128)S(1)} %get-tuple-element.39.refs_0_, f32[4,16,8,128]{3,2,1,0:T(8,128)S(1)} %get-tuple-element.40.refs_1_, f32[4,16,8,128]{3,2,1,0:T(8,128)S(1)} %get-tuple-element.41.refs_2_, ...), custom_call_target="tpu_custom_call" | custom-call | bytes 11840000 | tf_op jit(solution)/shard_map/interior8/pallas_call | solution.py:348
  18.6 0.6 %collective-permute-done.3.p2_ref = f32[8,8,128]{2,1,0:T(8,128)S(1)} collective-permute-done((f32[8,8,128]{2,1,0:T(8,128)S(1)}, f32[8,8,128]{2,1,0:T(8,128)S(1)}, u32[]{:S(2)}, u32[]{:S(2)}) %collective-permute-start.3) | collective-permute-done | bytes 32800 | tf_op jit(solution)/shard_map/ppermute | solution.py:748
  19.2 0.2 tall_edges.1.e_ref
  19.4 0.1 collective-permute-start.4
  19.5 1.6 %collective-permute-start.5 = (f32[4,112,128]{2,1,0:T(8,128)S(1)}, f32[4,112,128]{2,1,0:T(8,128)S(1)}, u32[]{:S(2)}, u32[]{:S(2)}) collective-permute-start(f32[4,112,128]{2,1,0:T(8,128)S(1)} %get-tuple-element.63), channel_id=1, source_target_pairs={{0,24},{8,0},{16,8},{24,16},{1,25},{9,1},{17,9},{25,17},{2,26},{10... | collective-permute-start | bytes 688136 | tf_op jit(solution)/shard_map/ppermute | solution.py:748
  21.1 2.8 %bands.1 = (f32[16,2,8,128]{3,2,1,0:T(8,128)S(1)}, f32[8,8,128]{2,1,0:T(8,128)S(1)}) custom-call(s32[2,16]{1,0:T(2,128)S(1)} %get-tuple-element.38.by_any, f32[16,128,128]{2,1,0:T(8,128)S(1)} %get-tuple-element.52.v_ref, f32[4,128,128]{2,1,0:T(8,128)S(1)} %get-tuple-element.53.o_ref, f32[4,128,128]{2,1,0:T(8,128)S(1)} %collective-permute-done.2.refs_4_.p_ref, ...), custom_call_target="tpu_custom_call" | custom-call | bytes 9250000 | tf_op jit(solution)/shard_map/bands/pallas_call | solution.py:489
  23.9 0.0 collective-permute-done.4.refs_0_
  23.9 2.1 %strips.1 = (f32[12,8,128]{2,1,0:T(8,128)S(1)}, f32[4,144,128]{2,1,0:T(8,128)S(1)}) custom-call(s32[4,8,128]{2,1,0:T(8,128)S(1)} %get-tuple-element.58.n_ref, f32[8,8,128]{2,1,0:T(8,128)S(1)} %get-tuple-element.59.rows_ref, f32[8,144,128]{2,1,0:T(8,128)S(1)} %tall_edges.1.e_ref, f32[8,144,128]{2,1,0:T(8,128)S(1)} %collective-permute-done.4.refs_0_), custom_call_target="tpu_custom_call" | custom-call | bytes 10730000 | tf_op jit(solution)/shard_map/strips/pallas_call | solution.py:587
  26.0 1.7 %collective-permute-start.6 = (f32[12,8,128]{2,1,0:T(8,128)S(1)}, f32[12,8,128]{2,1,0:T(8,128)S(1)}, u32[]{:S(2)}, u32[]{:S(2)}) collective-permute-start(f32[12,8,128]{2,1,0:T(8,128)S(1)} %get-tuple-element.64), channel_id=1, source_target_pairs={{0,24},{8,0},{16,8},{24,16},{1,25},{9,1},{17,9},{25,17},{2,26},{10... | collective-permute-start | bytes 147464 | tf_op jit(solution)/shard_map/ppermute | solution.py:748
  27.7 0.6 %merge.1 = (f32[16,128,128]{2,1,0:T(8,128)S(1)}, f32[4,128,128]{2,1,0:T(8,128)S(1)}) custom-call(f32[16,128,128]{2,1,0:T(8,128)S(1)} %get-tuple-element.51.inner_ref, f32[16,2,8,128]{3,2,1,0:T(8,128)S(1)} %get-tuple-element.57.ends_ref, f32[4,144,128]{2,1,0:T(8,128)S(1)} %get-tuple-element.61.sv_ref, f32[4,128,128]{2,1,0:T(8,128)S(1)} %get-tuple-element.53.o_ref, ...), custom_call_target="tpu_custom_call" | custom-call | bytes 4440000 | tf_op jit(solution)/shard_map/merge/pallas_call | solution.py:645
  28.3 0.0 collective-permute-done.5.recv_ref
  28.3 1.9 %collective-permute-done.6.edge_ref = f32[12,8,128]{2,1,0:T(8,128)S(1)} collective-permute-done((f32[12,8,128]{2,1,0:T(8,128)S(1)}, f32[12,8,128]{2,1,0:T(8,128)S(1)}, u32[]{:S(2)}, u32[]{:S(2)}) %collective-permute-start.6) | collective-permute-done | bytes 49184 | tf_op jit(solution)/shard_map/ppermute | solution.py:748
  30.2 0.1 partial_norms.1
  30.3 0.1 collective-permute-start.7
  30.4 1.2 %collective-permute-done.7 = f32[8,128]{1,0:T(8,128)S(1)} collective-permute-done((f32[8,128]{1,0:T(8,128)S(1)}, f32[8,128]{1,0:T(8,128)S(1)}, u32[]{:S(2)}, u32[]{:S(2)}) %collective-permute-start.7) | collective-permute-done | bytes 4128 | tf_op jit(solution)/shard_map/ppermute | solution.py:809
  31.6 1.5 %collective-permute-start.8 = (f32[8,128]{1,0:T(8,128)S(1)}, f32[8,128]{1,0:T(8,128)S(1)}, u32[]{:S(2)}, u32[]{:S(2)}) collective-permute-start(f32[8,128]{1,0:T(8,128)S(1)} %add.6), channel_id=1, source_target_pairs={{0,3},{1,2},{2,1},{3,0},{4,7},{5,6},{6,5},{7,4},{8,11},{9,10},{10,... | collective-permute-start | bytes 12296 | tf_op jit(solution)/shard_map/ppermute | solution.py:809
  33.1 1.5 %collective-permute-done.8 = f32[8,128]{1,0:T(8,128)S(1)} collective-permute-done((f32[8,128]{1,0:T(8,128)S(1)}, f32[8,128]{1,0:T(8,128)S(1)}, u32[]{:S(2)}, u32[]{:S(2)}) %collective-permute-start.8) | collective-permute-done | bytes 4128 | tf_op jit(solution)/shard_map/ppermute | solution.py:809
  34.6 2.6 %collective-permute-start.9 = (f32[8,128]{1,0:T(8,128)S(1)}, f32[8,128]{1,0:T(8,128)S(1)}, u32[]{:S(2)}, u32[]{:S(2)}) collective-permute-start(f32[8,128]{1,0:T(8,128)S(1)} %add.7.refs_0_), channel_id=1, source_target_pairs={{0,5},{1,4},{2,7},{3,6},{4,1},{5,0},{6,3},{7,2},{8,13},{9,12},{10,... | collective-permute-start | bytes 12296 | tf_op jit(solution)/shard_map/ppermute | solution.py:810
  37.2 1.0 %write.1 = f32[16,128,128]{2,1,0:T(8,128)} custom-call(f32[16,128,128]{2,1,0:T(8,128)S(1)} %get-tuple-element.69.v_ref), custom_call_target="tpu_custom_call" | custom-call | bytes 4440000 | tf_op jit(solution)/shard_map/write/pallas_call | solution.py:670
  38.2 0.4 collective-permute-done.9.refs_1_
  38.5 0.8 %rescaled.1 = f32[4,128,128]{2,1,0:T(8,128)} custom-call(f32[4,128,128]{2,1,0:T(8,128)S(1)} %get-tuple-element.65.upd_ref, f32[8,128]{1,0:T(8,128)S(1)} %add.7.refs_0_, f32[8,128]{1,0:T(8,128)S(1)} %collective-permute-done.9.refs_1_), custom_call_target="tpu_custom_call" | custom-call | bytes 2960000 | tf_op jit(solution)/shard_map/rescaled/pallas_call | solution.py:735
  (3 shorter events, 0.0 us)
Async XLA Ops:
  0.6 10.5 %collective-permute-start.2 = (f32[4,128,128]{2,1,0:T(8,128)}, f32[4,128,128]{2,1,0:T(8,128)S(1)}, u32[]{:S(2)}, u32[]{:S(2)}) collective-permute-start(f32[4,128,128]{2,1,0:T(8,128)} %o_hbm.1), channel_id=1, source_target_pairs={{0,8},{8,16},{16,24},{24,0},{1,9},{9,17},{17,25},{25,1},{2,10},{10... | collective-permute-start | bytes 786440 | tf_op jit(solution)/shard_map/ppermute | solution.py:748
  6.1 8.2 %collective-permute-start = (f32[26,8,128]{2,1,0:T(8,128)S(1)}, f32[26,8,128]{2,1,0:T(8,128)S(1)}, u32[]{:S(2)}, u32[]{:S(2)}) collective-permute-start(f32[26,8,128]{2,1,0:T(8,128)S(1)} %get-tuple-element.36), channel_id=1, source_target_pairs={{0,2},{1,3},{2,0},{3,1},{4,6},{5,7},{6,4},{7,5},{8,10},{9,11},{10,... | collective-permute-start | bytes 319496 | tf_op jit(solution)/shard_map/ppermute | solution.py:786
  7.8 6.6 %collective-permute-start.1 = (f32[26,8,128]{2,1,0:T(8,128)S(1)}, f32[26,8,128]{2,1,0:T(8,128)S(1)}, u32[]{:S(2)}, u32[]{:S(2)}) collective-permute-start(f32[26,8,128]{2,1,0:T(8,128)S(1)} %get-tuple-element.37), channel_id=1, source_target_pairs={{0,1},{1,0},{2,4},{3,5},{4,2},{5,3},{6,7},{7,6},{8,9},{9,8},{10,12... | collective-permute-start | bytes 319496 | tf_op jit(solution)/shard_map/ppermute | solution.py:787
  14.4 4.9 %collective-permute-start.3 = (f32[8,8,128]{2,1,0:T(8,128)S(1)}, f32[8,8,128]{2,1,0:T(8,128)S(1)}, u32[]{:S(2)}, u32[]{:S(2)}) collective-permute-start(f32[8,8,128]{2,1,0:T(8,128)S(1)} %row_pair.1), channel_id=1, source_target_pairs={{0,8},{8,16},{16,24},{24,0},{1,9},{9,17},{17,25},{25,1},{2,10},{10... | collective-permute-start | bytes 98312 | tf_op jit(solution)/shard_map/ppermute | solution.py:748
  19.4 4.4 %collective-permute-start.4 = (f32[8,144,128]{2,1,0:T(8,128)S(1)}, f32[8,144,128]{2,1,0:T(8,128)S(1)}, u32[]{:S(2)}, u32[]{:S(2)}) collective-permute-start(f32[8,144,128]{2,1,0:T(8,128)S(1)} %tall_edges.1.e_ref), channel_id=1, source_target_pairs={{0,1},{1,0},{2,3},{3,2},{4,5},{5,4},{6,7},{7,6},{8,9},{9,8},{10,11... | collective-permute-start | bytes 1769480 | tf_op jit(solution)/shard_map/ppermute | solution.py:797
  19.5 8.8 %collective-permute-start.5 = (f32[4,112,128]{2,1,0:T(8,128)S(1)}, f32[4,112,128]{2,1,0:T(8,128)S(1)}, u32[]{:S(2)}, u32[]{:S(2)}) collective-permute-start(f32[4,112,128]{2,1,0:T(8,128)S(1)} %get-tuple-element.63), channel_id=1, source_target_pairs={{0,24},{8,0},{16,8},{24,16},{1,25},{9,1},{17,9},{25,17},{2,26},{10... | collective-permute-start | bytes 688136 | tf_op jit(solution)/shard_map/ppermute | solution.py:748
  26.0 4.1 %collective-permute-start.6 = (f32[12,8,128]{2,1,0:T(8,128)S(1)}, f32[12,8,128]{2,1,0:T(8,128)S(1)}, u32[]{:S(2)}, u32[]{:S(2)}) collective-permute-start(f32[12,8,128]{2,1,0:T(8,128)S(1)} %get-tuple-element.64), channel_id=1, source_target_pairs={{0,24},{8,0},{16,8},{24,16},{1,25},{9,1},{17,9},{25,17},{2,26},{10... | collective-permute-start | bytes 147464 | tf_op jit(solution)/shard_map/ppermute | solution.py:748
  30.3 1.2 %collective-permute-start.7 = (f32[8,128]{1,0:T(8,128)S(1)}, f32[8,128]{1,0:T(8,128)S(1)}, u32[]{:S(2)}, u32[]{:S(2)}) collective-permute-start(f32[8,128]{1,0:T(8,128)S(1)} %get-tuple-element.68), channel_id=1, source_target_pairs={{0,1},{1,0},{2,3},{3,2},{4,5},{5,4},{6,7},{7,6},{8,9},{9,8},{10,11... | collective-permute-start | bytes 12296 | tf_op jit(solution)/shard_map/ppermute | solution.py:809
  31.6 3.0 %collective-permute-start.8 = (f32[8,128]{1,0:T(8,128)S(1)}, f32[8,128]{1,0:T(8,128)S(1)}, u32[]{:S(2)}, u32[]{:S(2)}) collective-permute-start(f32[8,128]{1,0:T(8,128)S(1)} %add.6), channel_id=1, source_target_pairs={{0,3},{1,2},{2,1},{3,0},{4,7},{5,6},{6,5},{7,4},{8,11},{9,10},{10,... | collective-permute-start | bytes 12296 | tf_op jit(solution)/shard_map/ppermute | solution.py:809
  34.6 3.9 %collective-permute-start.9 = (f32[8,128]{1,0:T(8,128)S(1)}, f32[8,128]{1,0:T(8,128)S(1)}, u32[]{:S(2)}, u32[]{:S(2)}) collective-permute-start(f32[8,128]{1,0:T(8,128)S(1)} %add.7.refs_0_), channel_id=1, source_target_pairs={{0,5},{1,4},{2,7},{3,6},{4,1},{5,0},{6,3},{7,2},{8,13},{9,12},{10,... | collective-permute-start | bytes 12296 | tf_op jit(solution)/shard_map/ppermute | solution.py:810

commit v8 on v7

--- a/solution.py
+++ b/solution.py
@@ -19,7 +19,6 @@
 STRIP = 32
 BLOCKS = LANES // STRIP
 LEAST = 4
-FIRST = 8
 GROUP = 8
 BANDS = 8
 AHEAD = 16
@@ -190,10 +189,9 @@
 
 
 def prepare_kernel(n_hbm, o_hbm, v_hbm, m_hbm, c_hbm, by_ref, steps_ref, *refs):
-    vs_ref, os_ref, om_ref, cf_ref, e_ref, pay_a, pay_b, o_ref, v_ref, m_ref, c_ref = refs[:11]
-    n_ref, sems = refs[11:]
+    vs_ref, os_ref, om_ref, cf_ref, e_ref, o_ref, v_ref, m_ref, c_ref = refs[:9]
+    n_ref, sems = refs[9:]
     own, rows, _ = o_ref.shape
-    pairs = v_ref.shape[0]
     count = rows // SUB
     sources = [(n_hbm, n_ref), (m_hbm, m_ref), (c_hbm, c_ref), (o_hbm, o_ref)]
     for first in range(own):
@@ -205,13 +203,6 @@
     ]
     for copy in copies:
         copy.start()
-
-    starts = [(1 - place()[0]) * (rows - HALO), place()[0] * (rows - HALO)]
-    starts = [pl.multiple_of(start, HALO) for start in starts]
-
-    def send_rows(at, ref, index):
-        for pay, start in zip((pay_a, pay_b), starts):
-            pay[at] = ref[index, pl.ds(start, HALO)]
 
     copies[0].wait()
     counts = n_ref[...]
@@ -227,9 +218,6 @@
         steps_ref[first] = steps.astype(jnp.int32)
     copies[1].wait()
     copies[2].wait()
-    send_rows(own + pairs, m_ref, 0)
-    for n in range(5):
-        send_rows(own + pairs + 1 + n, c_ref, n)
     e_ref[1 + own] = packed([m_ref[0], c_ref[0], c_ref[1], c_ref[2]])
     e_ref[2 + own] = packed([c_ref[3], c_ref[4]])
     dead = lane_masks(place()[1])[2]
@@ -244,7 +232,6 @@
     copies[3].wait()
     e_ref[0] = packed([o_ref[k] for k in range(own)])
     for k in range(own):
-        send_rows(k, o_ref, k)
         for t, value in enumerate(spread(o_ref, count, k)):
             os_ref[k, t] = value
             om_ref[k, t] = weights[t] * value
@@ -252,7 +239,6 @@
         copies[4 + first].wait()
         e_ref[1 + first] = packed([v_ref[first * own + k] for k in range(own)])
         for p in range(first * own, (first + 1) * own):
-            send_rows(own + p, v_ref, p)
             for t, value in enumerate(spread(v_ref, count, p)):
                 vs_ref[p, t] = value
 
@@ -262,7 +248,6 @@
     own, rows, lanes = orbitals.shape
     pairs = potentials.shape[0]
     count = rows // SUB
-    inputs = [pltpu.with_memory_space_constraint(a, pltpu.HBM) for a in arrays]
     return pl.pallas_call(
         prepare_kernel,
         out_shape=(
@@ -273,11 +258,10 @@
             f32(own, count, SUB, lanes),
             f32(5, count, SUB, lanes),
             f32(own + 3, rows, lanes),
-            *[f32(own + pairs + 1 + coefficients.shape[0], HALO, lanes)] * 2,
             *[f32(*a.shape) for a in arrays[1:]],
         ),
         in_specs=[HBM] * 5,
-        out_specs=(VMEM,) * 13,
+        out_specs=(VMEM,) * 11,
         scratch_shapes=[
             pltpu.VMEM(counts.shape, jnp.int32),
             pltpu.SemaphoreType.DMA((4 + own,)),
@@ -285,13 +269,47 @@
         compiler_params=params(),
         cost_estimate=cost(2.0),
         name="prepare",
-    )(*inputs)
-
-
-def interior_kernel(size, groups, before, by_any, *refs):
+    )(*arrays)
+
+
+def rows_kernel(o_hbm, v_hbm, m_hbm, c_hbm, pay_a, pay_b, sems):
+    rows = o_hbm.shape[1]
+    odd = place()[0]
+    copies = []
+    for pay, start in ((pay_a, (1 - odd) * (rows - HALO)), (pay_b, odd * (rows - HALO))):
+        start = pl.multiple_of(start, HALO)
+        at = 0
+        for ref in (o_hbm, v_hbm, m_hbm, c_hbm):
+            count = ref.shape[0]
+            copy = pltpu.make_async_copy(
+                ref.at[:, pl.ds(start, HALO), :], pay.at[pl.ds(at, count)], sems.at[len(copies)]
+            )
+            copy.start()
+            copies.append(copy)
+            at += count
+    for copy in copies:
+        copy.wait()
+
+
+def row_payloads(*arrays):
+    fields = sum(a.shape[0] for a in arrays)
+    return pl.pallas_call(
+        rows_kernel,
+        out_shape=(f32(fields, HALO, arrays[0].shape[-1]),) * 2,
+        in_specs=[HBM] * 4,
+        out_specs=(VMEM, VMEM),
+        scratch_shapes=[pltpu.SemaphoreType.DMA((8,))],
+        compiler_params=params(),
+        cost_estimate=cost(1.0),
+        name="row_payloads",
+    )(*arrays)
+
+
+def interior_kernel(by_any, *refs):
     vs_ref, os_ref, om_ref, cf_ref, p_ref = refs[:5]
     out_ref, back_ref, back, flat, sr, va, vb, by_ref, sem = refs[-9:]
     own, count = om_ref.shape[:2]
+    size = va.shape[0]
     fetch = pltpu.make_async_copy(by_any, by_ref, sem)
     fetch.start()
     masks = lane_masks(place()[1])
@@ -300,26 +318,15 @@
         for first in range(own):
             for t in range(count):
                 sr[first * own + second, t] = om_ref[first, t] * partner[t]
-    if before:
-        earlier, back_before = refs[5:7]
-        back[...] = back_before[...]
-    else:
-        back[...] = jnp.zeros_like(back)
+    back[...] = jnp.zeros_like(back)
     fetch.wait()
-    if before:
-
-        def keep(k, carry):
-            out_ref[by_ref[1, k]] = earlier[by_ref[1, k]]
-            return carry
-
-        lax.fori_loop(0, before, keep, 0)
 
     def group(g, carry):
-        pairs = [by_ref[1, before + g * size + k] for k in range(size)]
+        pairs = [by_ref[1, g * size + k] for k in range(size)]
         for k, p in enumerate(pairs):
             for t in range(count):
                 va[k, t] = vs_ref[p, t]
-        steps = [by_ref[0, before + g * size + k] for k in range(size)]
+        steps = [by_ref[0, g * size + k] for k in range(size)]
         relax(steps, count, va, vb, Chosen(sr, pairs), cf_ref, masks)
         for k, p in enumerate(pairs):
             first, second = p // own, p % own
@@ -328,34 +335,30 @@
                 back[second, t] = back[second, t] + va[k, t] * os_ref[first, t]
         return carry
 
-    lax.fori_loop(0, groups, group, 0)
+    lax.fori_loop(0, vs_ref.shape[0] // size, group, 0)
     for k in range(own):
-        if before:
-            spread_store(flat, [back[k, t] for t in range(count)])
-            back_ref[k] = flat[SUB : SUB + back_ref.shape[1]]
-        else:
-            back_ref[k] = back[k]
-
-
-def interior(size, groups, before, order, ready, partner, *earlier):
+        spread_store(flat, [back[k, t] for t in range(count)])
+        back_ref[k] = flat[SUB : SUB + back_ref.shape[1]]
+
+
+def interior(order, ready, partner):
     pairs, count, _, lanes = ready[0].shape
     own = ready[1].shape[0]
     rows = count * SUB
-    some = pltpu.VMEM((size, count, SUB, lanes), jnp.float32)
+    some = pltpu.VMEM((GROUP, count, SUB, lanes), jnp.float32)
     each = pltpu.VMEM((own, count, SUB, lanes), jnp.float32)
     every = pltpu.VMEM((pairs, count, SUB, lanes), jnp.float32)
-    back = f32(own, rows - 2 * SUB, lanes) if before else f32(own, count, SUB, lanes)
-    return pl.pallas_call(
-        functools.partial(interior_kernel, size, groups, before),
-        out_shape=(f32(pairs, rows, lanes), back),
-        in_specs=[ANY] + [VMEM] * (5 + len(earlier)),
+    return pl.pallas_call(
+        interior_kernel,
+        out_shape=(f32(pairs, rows, lanes), f32(own, rows - 2 * SUB, lanes)),
+        in_specs=[ANY] + [VMEM] * 5,
         out_specs=(VMEM, VMEM),
         scratch_shapes=[each, pltpu.VMEM((rows, lanes), jnp.float32), every, some, some]
         + [pltpu.SMEM(order.shape, jnp.int32), pltpu.SemaphoreType.DMA],
         compiler_params=params(),
-        cost_estimate=cost(0.4 * size * groups),
-        name=f"interior{before}",
-    )(order, *ready[:4], partner, *earlier)
+        cost_estimate=cost(5.5),
+        name="interior",
+    )(order, *ready[:4], partner)
 
 
 def row_pair_kernel(own, a_ref, b_ref, out_ref):
@@ -775,22 +778,23 @@
     gx, gy = lax.axis_size("gx"), lax.axis_size("gy")
     col_swaps = [p for p in pair_swaps(gy) if p]
     row_swaps = [row_swap(p, gx, gy) for p in pair_swaps(gx)]
-    pairs = potentials.shape[0]
 
     partner = shifted(orbitals, "orb", 1)
-    order, steps, *ready = prepare(
-        sweep_counts[None], orbitals, potentials, metric[None], coefficients
-    )
-    *ready, edges, pay_a, pay_b, orbitals, potentials, metric, coefficients = ready
-    metric = metric.reshape(rows, lanes)
+    arrays = [
+        pltpu.with_memory_space_constraint(a, pltpu.HBM)
+        for a in (orbitals, potentials, metric[None], coefficients)
+    ]
+    pay_a, pay_b = row_payloads(*arrays)
     rows_a = lax.ppermute(pay_a, ("gx", "gy"), row_swaps[0])
     rows_b = lax.ppermute(pay_b, ("gx", "gy"), row_swaps[1])
-    inner = interior(FIRST, 1, 0, order, ready, partner)
-    rows_a, rows_b, inner = lax.optimization_barrier((rows_a, rows_b, inner))
-    partner_rows = shifted(row_pair(own, rows_a, rows_b), "orb", 1)
-    inner, back = interior(
-        GROUP, (pairs - FIRST) // GROUP, FIRST, order, ready, partner, *inner
-    )
+    counts = pltpu.with_memory_space_constraint(sweep_counts[None], pltpu.HBM)
+    order, steps, *ready = prepare(counts, *arrays)
+    *ready, edges, orbitals, potentials, metric, coefficients = ready
+    metric = metric.reshape(rows, lanes)
+    beside = row_pair(own, rows_a, rows_b)
+    beside, order = lax.optimization_barrier((beside, order))
+    partner_rows = shifted(beside, "orb", 1)
+    inner, back = interior(order, ready, partner)
     partner_rows, inner, back = lax.optimization_barrier((partner_rows, inner, back))
     early = shifted(back, "orb", -1)
     edges = tall_edges(edges, rows_a, rows_b, partner_rows, partner)

time: 39 us -> 38.3 us (0.982); the launches traced: 39.3 us -> 38.3 us
  waiting for transfers between devices: 8.84 us -> 5.28 us
  starting transfers between devices: 13 us -> 14.4 us
  Pallas kernels: 16.8 us -> 17.8 us
    ppermute x4, waiting for transfers between devices: 5.82 us -> 1.79 us  [shifted(): lax.ppermute(value, axis, [(i, (i + by) % size) for i in range(size)])]
    pallas_call x2, Pallas kernels: 6.65 us -> 7.75 us  [the longest x1 6.74 us: interior(): pl.pallas_call(interior_kernel, out_shape=(f32(pairs, rows, lanes), f32(o...]
    ppermute x1, waiting for transfers between devices: 0.01 us -> 0.68 us  [local(): rows_a = lax.ppermute(pay_a, ('gx', 'gy'), row_swaps[0])]
    ppermute x1, starting transfers between devices: 2.56 us -> 3.16 us  [local(): norms = [norms] + [lax.ppermute(norms, ('gx', 'gy'), hop) for hop in across]]
    ppermute x2, starting transfers between devices: 1.61 us -> 2.06 us  [local(): norms = norms + lax.ppermute(norms, ('gx', 'gy'), hop)]
  transfers between devices with their start and end apart: 10 -> 10, of which waited for: 6 -> 6; matrix products, arithmetic and copies ran while one was open for 0% -> 0% of each run, Pallas kernels for 40% -> 43%
where the time goes in v8:
time: 38.3 us
  Pallas kernels  17.8 us (46%)
  starting transfers between devices  14.4 us (38%)
  waiting for transfers between devices  5.28 us (14%)
  between operations  0.74 us (2%)
    ppermute x4, starting transfers between devices, shifted(): lax.ppermute(value, axis, [(i, (i + by) % size) for i in range(size)])  7.48 us
    pallas_call x1, Pallas kernels, interior(): pl.pallas_call(interior_kernel, out_shape=(f32(pairs, rows, lanes), f32(o...  6.74 us
    ppermute x1, starting transfers between devices, local(): norms = [norms] + [lax.ppermute(norms, ('gx', 'gy'), hop) for hop in across]  3.16 us
    pallas_call x1, Pallas kernels, bands(): pl.pallas_call(bands_kernel, out_shape=(f32(pairs, 2, SUB, lanes), f32(2...  2.77 us
    ppermute x2, waiting for transfers between devices, local(): norms = norms + lax.ppermute(norms, ('gx', 'gy'), hop)  2.48 us
    pallas_call x1, Pallas kernels, prepare(): pl.pallas_call(prepare_kernel, out_shape=(jax.ShapeDtypeStruct((2, pairs)...  2.44 us
    pallas_call x1, Pallas kernels, strips(): pl.pallas_call(functools.partial(strips_kernel, sides), out_shape=(f32(ba...  2.12 us
    ppermute x2, starting transfers between devices, local(): norms = norms + lax.ppermute(norms, ('gx', 'gy'), hop)  2.06 us
  transfers between devices with their start and end apart: 10, of which 6 were waited for; matrix products, arithmetic and copies ran while one was open for 0% of the time, Pallas kernels for 43%

profile of v8, /device:TPU:0, one launch (start us, length us, event | category | flops | bytes accessed | tf_op | source)
XLA Modules:
  0.0 38.3 jit_solution(15043657069897129113)
XLA Ops:
  0.6 3.0 %collective-permute-start.3 = (f32[4,128,128]{2,1,0:T(8,128)}, f32[4,128,128]{2,1,0:T(8,128)S(1)}, u32[]{:S(2)}, u32[]{:S(2)}) collective-permute-start(f32[4,128,128]{2,1,0:T(8,128)} %o_hbm.3), channel_id=1, source_target_pairs={{0,8},{8,16},{16,24},{24,0},{1,9},{9,17},{17,25},{25,1},{2,10},{10... | collective-permute-start | bytes 786440 | tf_op jit(solution)/shard_map/ppermute | solution.py:751
  3.6 1.0 %row_payloads.1 = (f32[26,8,128]{2,1,0:T(8,128)S(1)}, f32[26,8,128]{2,1,0:T(8,128)S(1)}) custom-call(f32[4,128,128]{2,1,0:T(8,128)} %o_hbm.3, f32[16,128,128]{2,1,0:T(8,128)} %v_hbm.3, f32[1,128,128]{2,1,0:T(8,128)} %bitcast.5, f32[5,128,128]{2,1,0:T(8,128)} %c_hbm.3), custom_call_target="tpu_custom_call" | custom-call | bytes 3700000 | tf_op jit(solution)/shard_map/row_payloads/pallas_call | solution.py:296
  4.6 1.6 %collective-permute-start = (f32[26,8,128]{2,1,0:T(8,128)S(1)}, f32[26,8,128]{2,1,0:T(8,128)S(1)}, u32[]{:S(2)}, u32[]{:S(2)}) collective-permute-start(f32[26,8,128]{2,1,0:T(8,128)S(1)} %get-tuple-element.32), channel_id=1, source_target_pairs={{0,2},{1,3},{2,0},{3,1},{4,6},{5,7},{6,4},{7,5},{8,10},{9,11},{10,... | collective-permute-start | bytes 319496 | tf_op jit(solution)/shard_map/ppermute | solution.py:788
  6.3 0.0 collective-permute-start.1
  6.3 2.4 %prepare.1 = (s32[2,16]{1,0:T(2,128)S(1)}, s32[4,8,128]{2,1,0:T(8,128)S(1)}, f32[16,16,8,128]{3,2,1,0:T(8,128)S(1)}, f32[4,16,8,128]{3,2,1,0:T(8,128)S(1)}, f32[...) custom-call(s32[1,16]{1,0:T(1,128)} %bitcast.7, ...), custom_call_target="tpu_custom_call" | custom-call | bytes 7400000 | tf_op jit(solution)/shard_map/prepare/pallas_call | solution.py:251
  8.7 0.7 %collective-permute-done.a_ref.ra_ref = f32[26,8,128]{2,1,0:T(8,128)S(1)} collective-permute-done((f32[26,8,128]{2,1,0:T(8,128)S(1)}, f32[26,8,128]{2,1,0:T(8,128)S(1)}, u32[]{:S(2)}, u32[]{:S(2)}) %collective-permute-start) | collective-permute-done | bytes 106528 | tf_op jit(solution)/shard_map/ppermute | solution.py:788
  9.4 0.0 collective-permute-done.1.b_ref.rb_ref
  9.4 1.5 %collective-permute-start.2 = (f32[8,8,128]{2,1,0:T(8,128)S(1)}, f32[8,8,128]{2,1,0:T(8,128)S(1)}, u32[]{:S(2)}, u32[]{:S(2)}) collective-permute-start(f32[8,8,128]{2,1,0:T(8,128)S(1)} %row_pair.1), channel_id=1, source_target_pairs={{0,8},{8,16},{16,24},{24,0},{1,9},{9,17},{17,25},{25,1},{2,10},{10... | collective-permute-start | bytes 98312 | tf_op jit(solution)/shard_map/ppermute | solution.py:751
  10.9 0.2 collective-permute-done.3.refs_4_.p_ref
  11.1 6.7 %interior.1 = (f32[16,128,128]{2,1,0:T(8,128)S(1)}, f32[4,112,128]{2,1,0:T(8,128)S(1)}) custom-call(s32[2,16]{1,0:T(2,128)S(1)} %get-tuple-element.36.by_any, f32[16,16,8,128]{3,2,1,0:T(8,128)S(1)} %get-tuple-element.37.refs_0_, f32[4,16,8,128]{3,2,1,0:T(8,128)S(1)} %get-tuple-element.38.refs_1_, f32[4,16,8,128]{3,2,1,0:T(8,128)S(1)} %get-tuple-element.39.refs_2_, ...), custom_call_target="tpu_custom_call" | custom-call | bytes 20350000 | tf_op jit(solution)/shard_map/interior/pallas_call | solution.py:351
  17.8 0.0 collective-permute-done.2.p2_ref
  17.8 0.2 tall_edges.1.e_ref
  18.0 0.1 collective-permute-start.4
  18.1 1.0 %collective-permute-start.5 = (f32[4,112,128]{2,1,0:T(8,128)S(1)}, f32[4,112,128]{2,1,0:T(8,128)S(1)}, u32[]{:S(2)}, u32[]{:S(2)}) collective-permute-start(f32[4,112,128]{2,1,0:T(8,128)S(1)} %get-tuple-element.55), channel_id=1, source_target_pairs={{0,24},{8,0},{16,8},{24,16},{1,25},{9,1},{17,9},{25,17},{2,26},{10... | collective-permute-start | bytes 688136 | tf_op jit(solution)/shard_map/ppermute | solution.py:751
  19.2 2.8 %bands.1 = (f32[16,2,8,128]{3,2,1,0:T(8,128)S(1)}, f32[8,8,128]{2,1,0:T(8,128)S(1)}) custom-call(s32[2,16]{1,0:T(2,128)S(1)} %get-tuple-element.36.by_any, f32[16,128,128]{2,1,0:T(8,128)S(1)} %get-tuple-element.44.v_ref, f32[4,128,128]{2,1,0:T(8,128)S(1)} %get-tuple-element.45.o_ref, f32[4,128,128]{2,1,0:T(8,128)S(1)} %collective-permute-done.3.refs_4_.p_ref, ...), custom_call_target="tpu_custom_call" | custom-call | bytes 9250000 | tf_op jit(solution)/shard_map/bands/pallas_call | solution.py:492
  22.0 0.0 collective-permute-done.4.refs_0_
  22.0 2.1 %strips.1 = (f32[12,8,128]{2,1,0:T(8,128)S(1)}, f32[4,144,128]{2,1,0:T(8,128)S(1)}) custom-call(s32[4,8,128]{2,1,0:T(8,128)S(1)} %get-tuple-element.50.n_ref, f32[8,8,128]{2,1,0:T(8,128)S(1)} %get-tuple-element.51.rows_ref, f32[8,144,128]{2,1,0:T(8,128)S(1)} %tall_edges.1.e_ref, f32[8,144,128]{2,1,0:T(8,128)S(1)} %collective-permute-done.4.refs_0_), custom_call_target="tpu_custom_call" | custom-call | bytes 10730000 | tf_op jit(solution)/shard_map/strips/pallas_call | solution.py:590
  24.1 1.9 %collective-permute-start.6 = (f32[12,8,128]{2,1,0:T(8,128)S(1)}, f32[12,8,128]{2,1,0:T(8,128)S(1)}, u32[]{:S(2)}, u32[]{:S(2)}) collective-permute-start(f32[12,8,128]{2,1,0:T(8,128)S(1)} %get-tuple-element.56), channel_id=1, source_target_pairs={{0,24},{8,0},{16,8},{24,16},{1,25},{9,1},{17,9},{25,17},{2,26},{10... | collective-permute-start | bytes 147464 | tf_op jit(solution)/shard_map/ppermute | solution.py:751
  26.0 0.6 %merge.1 = (f32[16,128,128]{2,1,0:T(8,128)S(1)}, f32[4,128,128]{2,1,0:T(8,128)S(1)}) custom-call(f32[16,128,128]{2,1,0:T(8,128)S(1)} %get-tuple-element.43.inner_ref, f32[16,2,8,128]{3,2,1,0:T(8,128)S(1)} %get-tuple-element.49.ends_ref, f32[4,144,128]{2,1,0:T(8,128)S(1)} %get-tuple-element.53.sv_ref, f32[4,128,128]{2,1,0:T(8,128)S(1)} %get-tuple-element.45.o_ref, ...), custom_call_target="tpu_custom_call" | custom-call | bytes 4440000 | tf_op jit(solution)/shard_map/merge/pallas_call | solution.py:648
  26.6 0.0 collective-permute-done.5.recv_ref
  26.6 1.6 %collective-permute-done.6.edge_ref = f32[12,8,128]{2,1,0:T(8,128)S(1)} collective-permute-done((f32[12,8,128]{2,1,0:T(8,128)S(1)}, f32[12,8,128]{2,1,0:T(8,128)S(1)}, u32[]{:S(2)}, u32[]{:S(2)}) %collective-permute-start.6) | collective-permute-done | bytes 49184 | tf_op jit(solution)/shard_map/ppermute | solution.py:751
  28.2 0.2 partial_norms.1
  28.4 0.1 collective-permute-start.7
  28.5 1.2 %collective-permute-done.7 = f32[8,128]{1,0:T(8,128)S(1)} collective-permute-done((f32[8,128]{1,0:T(8,128)S(1)}, f32[8,128]{1,0:T(8,128)S(1)}, u32[]{:S(2)}, u32[]{:S(2)}) %collective-permute-start.7) | collective-permute-done | bytes 4128 | tf_op jit(solution)/shard_map/ppermute | solution.py:813
  29.6 2.0 %collective-permute-start.8 = (f32[8,128]{1,0:T(8,128)S(1)}, f32[8,128]{1,0:T(8,128)S(1)}, u32[]{:S(2)}, u32[]{:S(2)}) collective-permute-start(f32[8,128]{1,0:T(8,128)S(1)} %add.6), channel_id=1, source_target_pairs={{0,3},{1,2},{2,1},{3,0},{4,7},{5,6},{6,5},{7,4},{8,11},{9,10},{10,... | collective-permute-start | bytes 12296 | tf_op jit(solution)/shard_map/ppermute | solution.py:813
  31.6 1.3 %collective-permute-done.8 = f32[8,128]{1,0:T(8,128)S(1)} collective-permute-done((f32[8,128]{1,0:T(8,128)S(1)}, f32[8,128]{1,0:T(8,128)S(1)}, u32[]{:S(2)}, u32[]{:S(2)}) %collective-permute-start.8) | collective-permute-done | bytes 4128 | tf_op jit(solution)/shard_map/ppermute | solution.py:813
  32.9 3.2 %collective-permute-start.9 = (f32[8,128]{1,0:T(8,128)S(1)}, f32[8,128]{1,0:T(8,128)S(1)}, u32[]{:S(2)}, u32[]{:S(2)}) collective-permute-start(f32[8,128]{1,0:T(8,128)S(1)} %add.7.refs_0_), channel_id=1, source_target_pairs={{0,5},{1,4},{2,7},{3,6},{4,1},{5,0},{6,3},{7,2},{8,13},{9,12},{10,... | collective-permute-start | bytes 12296 | tf_op jit(solution)/shard_map/ppermute | solution.py:814
  36.1 1.0 %write.1 = f32[16,128,128]{2,1,0:T(8,128)} custom-call(f32[16,128,128]{2,1,0:T(8,128)S(1)} %get-tuple-element.61.v_ref), custom_call_target="tpu_custom_call" | custom-call | bytes 4440000 | tf_op jit(solution)/shard_map/write/pallas_call | solution.py:673
  37.1 0.3 collective-permute-done.9.refs_1_
  37.4 0.8 %rescaled.1 = f32[4,128,128]{2,1,0:T(8,128)} custom-call(f32[4,128,128]{2,1,0:T(8,128)S(1)} %get-tuple-element.57.upd_ref, f32[8,128]{1,0:T(8,128)S(1)} %add.7.refs_0_, f32[8,128]{1,0:T(8,128)S(1)} %collective-permute-done.9.refs_1_), custom_call_target="tpu_custom_call" | custom-call | bytes 2960000 | tf_op jit(solution)/shard_map/rescaled/pallas_call | solution.py:738
  (3 shorter events, 0.0 us)
Async XLA Ops:
  0.6 10.5 %collective-permute-start.3 = (f32[4,128,128]{2,1,0:T(8,128)}, f32[4,128,128]{2,1,0:T(8,128)S(1)}, u32[]{:S(2)}, u32[]{:S(2)}) collective-permute-start(f32[4,128,128]{2,1,0:T(8,128)} %o_hbm.3), channel_id=1, source_target_pairs={{0,8},{8,16},{16,24},{24,0},{1,9},{9,17},{17,25},{25,1},{2,10},{10... | collective-permute-start | bytes 786440 | tf_op jit(solution)/shard_map/ppermute | solution.py:751
  4.6 4.8 %collective-permute-start = (f32[26,8,128]{2,1,0:T(8,128)S(1)}, f32[26,8,128]{2,1,0:T(8,128)S(1)}, u32[]{:S(2)}, u32[]{:S(2)}) collective-permute-start(f32[26,8,128]{2,1,0:T(8,128)S(1)} %get-tuple-element.32), channel_id=1, source_target_pairs={{0,2},{1,3},{2,0},{3,1},{4,6},{5,7},{6,4},{7,5},{8,10},{9,11},{10,... | collective-permute-start | bytes 319496 | tf_op jit(solution)/shard_map/ppermute | solution.py:788
  6.3 3.1 %collective-permute-start.1 = (f32[26,8,128]{2,1,0:T(8,128)S(1)}, f32[26,8,128]{2,1,0:T(8,128)S(1)}, u32[]{:S(2)}, u32[]{:S(2)}) collective-permute-start(f32[26,8,128]{2,1,0:T(8,128)S(1)} %get-tuple-element.33), channel_id=1, source_target_pairs={{0,1},{1,0},{2,4},{3,5},{4,2},{5,3},{6,7},{7,6},{8,9},{9,8},{10,12... | collective-permute-start | bytes 319496 | tf_op jit(solution)/shard_map/ppermute | solution.py:789
  9.4 8.4 %collective-permute-start.2 = (f32[8,8,128]{2,1,0:T(8,128)S(1)}, f32[8,8,128]{2,1,0:T(8,128)S(1)}, u32[]{:S(2)}, u32[]{:S(2)}) collective-permute-start(f32[8,8,128]{2,1,0:T(8,128)S(1)} %row_pair.1), channel_id=1, source_target_pairs={{0,8},{8,16},{16,24},{24,0},{1,9},{9,17},{17,25},{25,1},{2,10},{10... | collective-permute-start | bytes 98312 | tf_op jit(solution)/shard_map/ppermute | solution.py:751
  18.0 3.9 %collective-permute-start.4 = (f32[8,144,128]{2,1,0:T(8,128)S(1)}, f32[8,144,128]{2,1,0:T(8,128)S(1)}, u32[]{:S(2)}, u32[]{:S(2)}) collective-permute-start(f32[8,144,128]{2,1,0:T(8,128)S(1)} %tall_edges.1.e_ref), channel_id=1, source_target_pairs={{0,1},{1,0},{2,3},{3,2},{4,5},{5,4},{6,7},{7,6},{8,9},{9,8},{10,11... | collective-permute-start | bytes 1769480 | tf_op jit(solution)/shard_map/ppermute | solution.py:801
  18.1 8.5 %collective-permute-start.5 = (f32[4,112,128]{2,1,0:T(8,128)S(1)}, f32[4,112,128]{2,1,0:T(8,128)S(1)}, u32[]{:S(2)}, u32[]{:S(2)}) collective-permute-start(f32[4,112,128]{2,1,0:T(8,128)S(1)} %get-tuple-element.55), channel_id=1, source_target_pairs={{0,24},{8,0},{16,8},{24,16},{1,25},{9,1},{17,9},{25,17},{2,26},{10... | collective-permute-start | bytes 688136 | tf_op jit(solution)/shard_map/ppermute | solution.py:751
  24.1 4.1 %collective-permute-start.6 = (f32[12,8,128]{2,1,0:T(8,128)S(1)}, f32[12,8,128]{2,1,0:T(8,128)S(1)}, u32[]{:S(2)}, u32[]{:S(2)}) collective-permute-start(f32[12,8,128]{2,1,0:T(8,128)S(1)} %get-tuple-element.56), channel_id=1, source_target_pairs={{0,24},{8,0},{16,8},{24,16},{1,25},{9,1},{17,9},{25,17},{2,26},{10... | collective-permute-start | bytes 147464 | tf_op jit(solution)/shard_map/ppermute | solution.py:751
  28.4 1.2 %collective-permute-start.7 = (f32[8,128]{1,0:T(8,128)S(1)}, f32[8,128]{1,0:T(8,128)S(1)}, u32[]{:S(2)}, u32[]{:S(2)}) collective-permute-start(f32[8,128]{1,0:T(8,128)S(1)} %get-tuple-element.60), channel_id=1, source_target_pairs={{0,1},{1,0},{2,3},{3,2},{4,5},{5,4},{6,7},{7,6},{8,9},{9,8},{10,11... | collective-permute-start | bytes 12296 | tf_op jit(solution)/shard_map/ppermute | solution.py:813
  29.6 3.3 %collective-permute-start.8 = (f32[8,128]{1,0:T(8,128)S(1)}, f32[8,128]{1,0:T(8,128)S(1)}, u32[]{:S(2)}, u32[]{:S(2)}) collective-permute-start(f32[8,128]{1,0:T(8,128)S(1)} %add.6), channel_id=1, source_target_pairs={{0,3},{1,2},{2,1},{3,0},{4,7},{5,6},{6,5},{7,4},{8,11},{9,10},{10,... | collective-permute-start | bytes 12296 | tf_op jit(solution)/shard_map/ppermute | solution.py:813
  32.9 4.5 %collective-permute-start.9 = (f32[8,128]{1,0:T(8,128)S(1)}, f32[8,128]{1,0:T(8,128)S(1)}, u32[]{:S(2)}, u32[]{:S(2)}) collective-permute-start(f32[8,128]{1,0:T(8,128)S(1)} %add.7.refs_0_), channel_id=1, source_target_pairs={{0,5},{1,4},{2,7},{3,6},{4,1},{5,0},{6,3},{7,2},{8,13},{9,12},{10,... | collective-permute-start | bytes 12296 | tf_op jit(solution)/shard_map/ppermute | solution.py:814

commit v9 on v8

--- a/solution.py
+++ b/solution.py
@@ -155,7 +155,15 @@
             sweep(fields, count, pair[s], pair[1 - s], source, coefs, keep=keep)
         return carry
 
-    lax.fori_loop(0, (top - LEAST + 1) // 2, body, 0)
+    lax.fori_loop(0, (top - LEAST) // 2, body, 0)
+
+    @pl.when((top - LEAST) % 2 == 1)
+    def _():
+        keep = [jnp.full((SUB, LANES), n, jnp.int32) >= top for n in steps]
+        sweep(fields, count, here, there, source, coefs, keep=keep)
+        for k in range(fields):
+            for t in range(count):
+                here[k, t] = there[k, t]
 
 
 def lane_masks(odd):

time: 38.3 us -> 38.1 us (level)
  Pallas kernels: 17.8 us -> 16.8 us
  waiting for transfers between devices: 5.28 us -> 5.74 us
    pallas_call x1, Pallas kernels: 6.74 us -> 6.01 us  [interior(): pl.pallas_call(interior_kernel, out_shape=(f32(pairs, rows, lanes), f32(o...]
    ppermute x4, waiting for transfers between devices: 1.79 us -> 2.25 us  [shifted(): lax.ppermute(value, axis, [(i, (i + by) % size) for i in range(size)])]
  transfers between devices with their start and end apart: 10 -> 10, of which waited for: 6 -> 6; matrix products, arithmetic and copies ran while one was open for 0% -> 0% of each run, Pallas kernels for 43% -> 41%
where the time goes in v9:
time: 38.1 us; the launch traced here: 38 us
  Pallas kernels  16.8 us (44%)
  starting transfers between devices  14.7 us (39%)
  waiting for transfers between devices  5.74 us (15%)
  between operations  0.74 us (2%)
    ppermute x4, starting transfers between devices, shifted(): lax.ppermute(value, axis, [(i, (i + by) % size) for i in range(size)])  7.76 us
    pallas_call x1, Pallas kernels, interior(): pl.pallas_call(interior_kernel, out_shape=(f32(pairs, rows, lanes), f32(o...  6.01 us
    ppermute x1, starting transfers between devices, local(): norms = [norms] + [lax.ppermute(norms, ('gx', 'gy'), hop) for hop in across]  3.16 us
    pallas_call x1, Pallas kernels, bands(): pl.pallas_call(bands_kernel, out_shape=(f32(pairs, 2, SUB, lanes), f32(2...  2.49 us
    ppermute x2, waiting for transfers between devices, local(): norms = norms + lax.ppermute(norms, ('gx', 'gy'), hop)  2.48 us
    pallas_call x1, Pallas kernels, prepare(): pl.pallas_call(prepare_kernel, out_shape=(jax.ShapeDtypeStruct((2, pairs)...  2.44 us
    ppermute x4, waiting for transfers between devices, shifted(): lax.ppermute(value, axis, [(i, (i + by) % size) for i in range(size)])  2.25 us
    pallas_call x1, Pallas kernels, strips(): pl.pallas_call(functools.partial(strips_kernel, sides), out_shape=(f32(ba...  2.12 us
  transfers between devices with their start and end apart: 10, of which 6 were waited for; matrix products, arithmetic and copies ran while one was open for 0% of the time, Pallas kernels for 41%

profile of v9, /device:TPU:0, one launch (start us, length us, event | category | flops | bytes accessed | tf_op | source)
XLA Modules:
  0.0 38.0 jit_solution(15924113335459271502)
XLA Ops:
  0.6 3.0 %collective-permute-start.3 = (f32[4,128,128]{2,1,0:T(8,128)}, f32[4,128,128]{2,1,0:T(8,128)S(1)}, u32[]{:S(2)}, u32[]{:S(2)}) collective-permute-start(f32[4,128,128]{2,1,0:T(8,128)} %o_hbm.3), channel_id=1, source_target_pairs={{0,8},{8,16},{16,24},{24,0},{1,9},{9,17},{17,25},{25,1},{2,10},{10... | collective-permute-start | bytes 786440 | tf_op jit(solution)/shard_map/ppermute | solution.py:759
  3.6 1.0 %row_payloads.1 = (f32[26,8,128]{2,1,0:T(8,128)S(1)}, f32[26,8,128]{2,1,0:T(8,128)S(1)}) custom-call(f32[4,128,128]{2,1,0:T(8,128)} %o_hbm.3, f32[16,128,128]{2,1,0:T(8,128)} %v_hbm.3, f32[1,128,128]{2,1,0:T(8,128)} %bitcast.5, f32[5,128,128]{2,1,0:T(8,128)} %c_hbm.3), custom_call_target="tpu_custom_call" | custom-call | bytes 3700000 | tf_op jit(solution)/shard_map/row_payloads/pallas_call | solution.py:304
  4.6 1.6 %collective-permute-start = (f32[26,8,128]{2,1,0:T(8,128)S(1)}, f32[26,8,128]{2,1,0:T(8,128)S(1)}, u32[]{:S(2)}, u32[]{:S(2)}) collective-permute-start(f32[26,8,128]{2,1,0:T(8,128)S(1)} %get-tuple-element.32), channel_id=1, source_target_pairs={{0,2},{1,3},{2,0},{3,1},{4,6},{5,7},{6,4},{7,5},{8,10},{9,11},{10,... | collective-permute-start | bytes 319496 | tf_op jit(solution)/shard_map/ppermute | solution.py:796
  6.3 0.0 collective-permute-start.1
  6.3 2.4 %prepare.1 = (s32[2,16]{1,0:T(2,128)S(1)}, s32[4,8,128]{2,1,0:T(8,128)S(1)}, f32[16,16,8,128]{3,2,1,0:T(8,128)S(1)}, f32[4,16,8,128]{3,2,1,0:T(8,128)S(1)}, f32[...) custom-call(s32[1,16]{1,0:T(1,128)} %bitcast.7, ...), custom_call_target="tpu_custom_call" | custom-call | bytes 7400000 | tf_op jit(solution)/shard_map/prepare/pallas_call | solution.py:259
  8.7 0.7 %collective-permute-done.a_ref.ra_ref = f32[26,8,128]{2,1,0:T(8,128)S(1)} collective-permute-done((f32[26,8,128]{2,1,0:T(8,128)S(1)}, f32[26,8,128]{2,1,0:T(8,128)S(1)}, u32[]{:S(2)}, u32[]{:S(2)}) %collective-permute-start) | collective-permute-done | bytes 106528 | tf_op jit(solution)/shard_map/ppermute | solution.py:796
  9.4 0.0 collective-permute-done.1.b_ref.rb_ref
  9.4 1.5 %collective-permute-start.2 = (f32[8,8,128]{2,1,0:T(8,128)S(1)}, f32[8,8,128]{2,1,0:T(8,128)S(1)}, u32[]{:S(2)}, u32[]{:S(2)}) collective-permute-start(f32[8,8,128]{2,1,0:T(8,128)S(1)} %row_pair.1), channel_id=1, source_target_pairs={{0,8},{8,16},{16,24},{24,0},{1,9},{9,17},{17,25},{25,1},{2,10},{10... | collective-permute-start | bytes 98312 | tf_op jit(solution)/shard_map/ppermute | solution.py:759
  10.9 0.2 collective-permute-done.3.refs_4_.p_ref
  11.1 6.0 %interior.1 = (f32[16,128,128]{2,1,0:T(8,128)S(1)}, f32[4,112,128]{2,1,0:T(8,128)S(1)}) custom-call(s32[2,16]{1,0:T(2,128)S(1)} %get-tuple-element.36.by_any, f32[16,16,8,128]{3,2,1,0:T(8,128)S(1)} %get-tuple-element.37.refs_0_, f32[4,16,8,128]{3,2,1,0:T(8,128)S(1)} %get-tuple-element.38.refs_1_, f32[4,16,8,128]{3,2,1,0:T(8,128)S(1)} %get-tuple-element.39.refs_2_, ...), custom_call_target="tpu_custom_call" | custom-call | bytes 20350000 | tf_op jit(solution)/shard_map/interior/pallas_call | solution.py:359
  17.1 0.0 collective-permute-done.2.p2_ref
  17.1 0.2 tall_edges.1.e_ref
  17.3 0.1 collective-permute-start.4
  17.4 1.8 %collective-permute-start.5 = (f32[4,112,128]{2,1,0:T(8,128)S(1)}, f32[4,112,128]{2,1,0:T(8,128)S(1)}, u32[]{:S(2)}, u32[]{:S(2)}) collective-permute-start(f32[4,112,128]{2,1,0:T(8,128)S(1)} %get-tuple-element.55), channel_id=1, source_target_pairs={{0,24},{8,0},{16,8},{24,16},{1,25},{9,1},{17,9},{25,17},{2,26},{10... | collective-permute-start | bytes 688136 | tf_op jit(solution)/shard_map/ppermute | solution.py:759
  19.2 2.5 %bands.1 = (f32[16,2,8,128]{3,2,1,0:T(8,128)S(1)}, f32[8,8,128]{2,1,0:T(8,128)S(1)}) custom-call(s32[2,16]{1,0:T(2,128)S(1)} %get-tuple-element.36.by_any, f32[16,128,128]{2,1,0:T(8,128)S(1)} %get-tuple-element.44.v_ref, f32[4,128,128]{2,1,0:T(8,128)S(1)} %get-tuple-element.45.o_ref, f32[4,128,128]{2,1,0:T(8,128)S(1)} %collective-permute-done.3.refs_4_.p_ref, ...), custom_call_target="tpu_custom_call" | custom-call | bytes 9250000 | tf_op jit(solution)/shard_map/bands/pallas_call | solution.py:500
  21.7 0.0 collective-permute-done.4.refs_0_
  21.7 2.1 %strips.1 = (f32[12,8,128]{2,1,0:T(8,128)S(1)}, f32[4,144,128]{2,1,0:T(8,128)S(1)}) custom-call(s32[4,8,128]{2,1,0:T(8,128)S(1)} %get-tuple-element.50.n_ref, f32[8,8,128]{2,1,0:T(8,128)S(1)} %get-tuple-element.51.rows_ref, f32[8,144,128]{2,1,0:T(8,128)S(1)} %tall_edges.1.e_ref, f32[8,144,128]{2,1,0:T(8,128)S(1)} %collective-permute-done.4.refs_0_), custom_call_target="tpu_custom_call" | custom-call | bytes 10730000 | tf_op jit(solution)/shard_map/strips/pallas_call | solution.py:598
  23.8 1.5 %collective-permute-start.6 = (f32[12,8,128]{2,1,0:T(8,128)S(1)}, f32[12,8,128]{2,1,0:T(8,128)S(1)}, u32[]{:S(2)}, u32[]{:S(2)}) collective-permute-start(f32[12,8,128]{2,1,0:T(8,128)S(1)} %get-tuple-element.56), channel_id=1, source_target_pairs={{0,24},{8,0},{16,8},{24,16},{1,25},{9,1},{17,9},{25,17},{2,26},{10... | collective-permute-start | bytes 147464 | tf_op jit(solution)/shard_map/ppermute | solution.py:759
  25.3 0.6 %merge.1 = (f32[16,128,128]{2,1,0:T(8,128)S(1)}, f32[4,128,128]{2,1,0:T(8,128)S(1)}) custom-call(f32[16,128,128]{2,1,0:T(8,128)S(1)} %get-tuple-element.43.inner_ref, f32[16,2,8,128]{3,2,1,0:T(8,128)S(1)} %get-tuple-element.49.ends_ref, f32[4,144,128]{2,1,0:T(8,128)S(1)} %get-tuple-element.53.sv_ref, f32[4,128,128]{2,1,0:T(8,128)S(1)} %get-tuple-element.45.o_ref, ...), custom_call_target="tpu_custom_call" | custom-call | bytes 4440000 | tf_op jit(solution)/shard_map/merge/pallas_call | solution.py:656
  25.9 0.0 collective-permute-done.5.recv_ref
  25.9 2.1 %collective-permute-done.6.edge_ref = f32[12,8,128]{2,1,0:T(8,128)S(1)} collective-permute-done((f32[12,8,128]{2,1,0:T(8,128)S(1)}, f32[12,8,128]{2,1,0:T(8,128)S(1)}, u32[]{:S(2)}, u32[]{:S(2)}) %collective-permute-start.6) | collective-permute-done | bytes 49184 | tf_op jit(solution)/shard_map/ppermute | solution.py:759
  28.0 0.2 partial_norms.1
  28.1 0.1 collective-permute-start.7
  28.2 1.2 %collective-permute-done.7 = f32[8,128]{1,0:T(8,128)S(1)} collective-permute-done((f32[8,128]{1,0:T(8,128)S(1)}, f32[8,128]{1,0:T(8,128)S(1)}, u32[]{:S(2)}, u32[]{:S(2)}) %collective-permute-start.7) | collective-permute-done | bytes 4128 | tf_op jit(solution)/shard_map/ppermute | solution.py:821
  29.4 2.0 %collective-permute-start.8 = (f32[8,128]{1,0:T(8,128)S(1)}, f32[8,128]{1,0:T(8,128)S(1)}, u32[]{:S(2)}, u32[]{:S(2)}) collective-permute-start(f32[8,128]{1,0:T(8,128)S(1)} %add.6), channel_id=1, source_target_pairs={{0,3},{1,2},{2,1},{3,0},{4,7},{5,6},{6,5},{7,4},{8,11},{9,10},{10,... | collective-permute-start | bytes 12296 | tf_op jit(solution)/shard_map/ppermute | solution.py:821
  31.4 1.3 %collective-permute-done.8 = f32[8,128]{1,0:T(8,128)S(1)} collective-permute-done((f32[8,128]{1,0:T(8,128)S(1)}, f32[8,128]{1,0:T(8,128)S(1)}, u32[]{:S(2)}, u32[]{:S(2)}) %collective-permute-start.8) | collective-permute-done | bytes 4128 | tf_op jit(solution)/shard_map/ppermute | solution.py:821
  32.7 3.2 %collective-permute-start.9 = (f32[8,128]{1,0:T(8,128)S(1)}, f32[8,128]{1,0:T(8,128)S(1)}, u32[]{:S(2)}, u32[]{:S(2)}) collective-permute-start(f32[8,128]{1,0:T(8,128)S(1)} %add.7.refs_0_), channel_id=1, source_target_pairs={{0,5},{1,4},{2,7},{3,6},{4,1},{5,0},{6,3},{7,2},{8,13},{9,12},{10,... | collective-permute-start | bytes 12296 | tf_op jit(solution)/shard_map/ppermute | solution.py:822
  35.9 1.0 %write.1 = f32[16,128,128]{2,1,0:T(8,128)} custom-call(f32[16,128,128]{2,1,0:T(8,128)S(1)} %get-tuple-element.61.v_ref), custom_call_target="tpu_custom_call" | custom-call | bytes 4440000 | tf_op jit(solution)/shard_map/write/pallas_call | solution.py:681
  36.9 0.3 collective-permute-done.9.refs_1_
  37.2 0.8 %rescaled.1 = f32[4,128,128]{2,1,0:T(8,128)} custom-call(f32[4,128,128]{2,1,0:T(8,128)S(1)} %get-tuple-element.57.upd_ref, f32[8,128]{1,0:T(8,128)S(1)} %add.7.refs_0_, f32[8,128]{1,0:T(8,128)S(1)} %collective-permute-done.9.refs_1_), custom_call_target="tpu_custom_call" | custom-call | bytes 2960000 | tf_op jit(solution)/shard_map/rescaled/pallas_call | solution.py:746
  (3 shorter events, 0.0 us)
Async XLA Ops:
  0.6 10.5 %collective-permute-start.3 = (f32[4,128,128]{2,1,0:T(8,128)}, f32[4,128,128]{2,1,0:T(8,128)S(1)}, u32[]{:S(2)}, u32[]{:S(2)}) collective-permute-start(f32[4,128,128]{2,1,0:T(8,128)} %o_hbm.3), channel_id=1, source_target_pairs={{0,8},{8,16},{16,24},{24,0},{1,9},{9,17},{17,25},{25,1},{2,10},{10... | collective-permute-start | bytes 786440 | tf_op jit(solution)/shard_map/ppermute | solution.py:759
  4.6 4.8 %collective-permute-start = (f32[26,8,128]{2,1,0:T(8,128)S(1)}, f32[26,8,128]{2,1,0:T(8,128)S(1)}, u32[]{:S(2)}, u32[]{:S(2)}) collective-permute-start(f32[26,8,128]{2,1,0:T(8,128)S(1)} %get-tuple-element.32), channel_id=1, source_target_pairs={{0,2},{1,3},{2,0},{3,1},{4,6},{5,7},{6,4},{7,5},{8,10},{9,11},{10,... | collective-permute-start | bytes 319496 | tf_op jit(solution)/shard_map/ppermute | solution.py:796
  6.3 3.1 %collective-permute-start.1 = (f32[26,8,128]{2,1,0:T(8,128)S(1)}, f32[26,8,128]{2,1,0:T(8,128)S(1)}, u32[]{:S(2)}, u32[]{:S(2)}) collective-permute-start(f32[26,8,128]{2,1,0:T(8,128)S(1)} %get-tuple-element.33), channel_id=1, source_target_pairs={{0,1},{1,0},{2,4},{3,5},{4,2},{5,3},{6,7},{7,6},{8,9},{9,8},{10,12... | collective-permute-start | bytes 319496 | tf_op jit(solution)/shard_map/ppermute | solution.py:797
  9.4 7.7 %collective-permute-start.2 = (f32[8,8,128]{2,1,0:T(8,128)S(1)}, f32[8,8,128]{2,1,0:T(8,128)S(1)}, u32[]{:S(2)}, u32[]{:S(2)}) collective-permute-start(f32[8,8,128]{2,1,0:T(8,128)S(1)} %row_pair.1), channel_id=1, source_target_pairs={{0,8},{8,16},{16,24},{24,0},{1,9},{9,17},{17,25},{25,1},{2,10},{10... | collective-permute-start | bytes 98312 | tf_op jit(solution)/shard_map/ppermute | solution.py:759
  17.3 4.4 %collective-permute-start.4 = (f32[8,144,128]{2,1,0:T(8,128)S(1)}, f32[8,144,128]{2,1,0:T(8,128)S(1)}, u32[]{:S(2)}, u32[]{:S(2)}) collective-permute-start(f32[8,144,128]{2,1,0:T(8,128)S(1)} %tall_edges.1.e_ref), channel_id=1, source_target_pairs={{0,1},{1,0},{2,3},{3,2},{4,5},{5,4},{6,7},{7,6},{8,9},{9,8},{10,11... | collective-permute-start | bytes 1769480 | tf_op jit(solution)/shard_map/ppermute | solution.py:809
  17.4 8.5 %collective-permute-start.5 = (f32[4,112,128]{2,1,0:T(8,128)S(1)}, f32[4,112,128]{2,1,0:T(8,128)S(1)}, u32[]{:S(2)}, u32[]{:S(2)}) collective-permute-start(f32[4,112,128]{2,1,0:T(8,128)S(1)} %get-tuple-element.55), channel_id=1, source_target_pairs={{0,24},{8,0},{16,8},{24,16},{1,25},{9,1},{17,9},{25,17},{2,26},{10... | collective-permute-start | bytes 688136 | tf_op jit(solution)/shard_map/ppermute | solution.py:759
  23.8 4.1 %collective-permute-start.6 = (f32[12,8,128]{2,1,0:T(8,128)S(1)}, f32[12,8,128]{2,1,0:T(8,128)S(1)}, u32[]{:S(2)}, u32[]{:S(2)}) collective-permute-start(f32[12,8,128]{2,1,0:T(8,128)S(1)} %get-tuple-element.56), channel_id=1, source_target_pairs={{0,24},{8,0},{16,8},{24,16},{1,25},{9,1},{17,9},{25,17},{2,26},{10... | collective-permute-start | bytes 147464 | tf_op jit(solution)/shard_map/ppermute | solution.py:759
  28.1 1.2 %collective-permute-start.7 = (f32[8,128]{1,0:T(8,128)S(1)}, f32[8,128]{1,0:T(8,128)S(1)}, u32[]{:S(2)}, u32[]{:S(2)}) collective-permute-start(f32[8,128]{1,0:T(8,128)S(1)} %get-tuple-element.60), channel_id=1, source_target_pairs={{0,1},{1,0},{2,3},{3,2},{4,5},{5,4},{6,7},{7,6},{8,9},{9,8},{10,11... | collective-permute-start | bytes 12296 | tf_op jit(solution)/shard_map/ppermute | solution.py:821
  29.4 3.3 %collective-permute-start.8 = (f32[8,128]{1,0:T(8,128)S(1)}, f32[8,128]{1,0:T(8,128)S(1)}, u32[]{:S(2)}, u32[]{:S(2)}) collective-permute-start(f32[8,128]{1,0:T(8,128)S(1)} %add.6), channel_id=1, source_target_pairs={{0,3},{1,2},{2,1},{3,0},{4,7},{5,6},{6,5},{7,4},{8,11},{9,10},{10,... | collective-permute-start | bytes 12296 | tf_op jit(solution)/shard_map/ppermute | solution.py:821
  32.7 4.5 %collective-permute-start.9 = (f32[8,128]{1,0:T(8,128)S(1)}, f32[8,128]{1,0:T(8,128)S(1)}, u32[]{:S(2)}, u32[]{:S(2)}) collective-permute-start(f32[8,128]{1,0:T(8,128)S(1)} %add.7.refs_0_), channel_id=1, source_target_pairs={{0,5},{1,4},{2,7},{3,6},{4,1},{5,0},{6,3},{7,2},{8,13},{9,12},{10,... | collective-permute-start | bytes 12296 | tf_op jit(solution)/shard_map/ppermute | solution.py:822
